TPU v7x, 32 devices: a whole 2x2x4 slice. The times are simulated.
32 devices in a mesh: parts: 2 (over y), dp: 4 (over z), tensor: 4 (over x, core).
Axes of the slice: x: 2, y: 2, z: 4, core: 2. Of those that a mesh axis runs over, the one named last changes fastest.
Arguments:
- acts: bfloat16 [5632, 8192], P(('parts', 'dp'), 'tensor'), parts along dimension 0, may hold values from -6 to 6
- output_weight: bfloat16 [8192, 8192], P('tensor'), may hold values from -0.09375 to 0.09375
- adapter_down_weight: bfloat16 [384, 16, 8192], P('dp', None, 'tensor'), may hold values from -0.0625 to 0.0625
- adapter_up_weight: bfloat16 [384, 16, 8192], P('dp', None, 'tensor'), may hold values from -1.5 to 1.5
- segment_block_count: int32 [8, 16], P(('parts', 'dp')), parts along dimension 0, may hold values from 1 to 11, 44 in all within a row
- segment_adapter_id: int32 [8, 16], P(('parts', 'dp')), parts along dimension 0, may hold values from 0 to 383, as said below
- adapter_store_row: int32 [768], P('parts'), parts along dimension 0, may hold values from 0 to 383, as said below
Outputs:
- projected: bfloat16 [5632, 8192], P(('parts', 'dp'), 'tensor'), parts along dimension 0
There are 2 independent parts, one for each index of `parts`. A program takes and returns all parts, laid end to end along the dimension named above; an argument that names none is the same for every part. Nothing has to cross between parts.
Inputs may be any that keep to these rules, and one draw needn't show every extreme that they name: `segment_adapter_id`: in each group, at most 5 segments name adapters whose slots lie in one block of 96 consecutive rows, and exactly 5 for some block. `adapter_store_row`: A permutation of 0 to 383.
All inputs are finite; a program needn't handle non-finite values.
Results may differ from a plain program's by a relative error of at most 0.012.
Values may be sent and summed in bfloat16 or wider, within the bound.
No kernel may reach another device: no remote copies, remote signals or barrier semaphores. Data moves between devices by JAX's collectives and lax.ppermute only.
A program may use at most 256 MiB of HBM per device.

v0:
```python
import jax
import jax.numpy as jnp
from jax import lax
from jax.sharding import PartitionSpec as P

ADAPTER_RANK = 16
GROUP_SEGMENTS = 16


adapter_scale = 0.5


def body(
    acts,
    output_weight,
    adapter_down_weight,
    adapter_up_weight,
    segment_block_count,
    segment_adapter_id,
    adapter_store_row,
):
    tok_rows = acts.shape[0]
    feature_width = acts.shape[1]
    stored_adapters = adapter_store_row[segment_adapter_id[0]]
    pieces = (
        lax.all_gather(adapter_down_weight, "dp", axis=0, tiled=True),
        lax.all_gather(adapter_up_weight, "dp", axis=0, tiled=True),
    )
    count = pieces[0].shape[0]
    picker = (stored_adapters[:, None] == jnp.arange(count, dtype=jnp.int32)[None, :]).astype(
        jnp.bfloat16
    )
    down_add = jnp.einsum("sn,nrd->srd", picker, pieces[0], preferred_element_type=jnp.float32)
    up_add = jnp.einsum("sn,nrd->srd", picker, pieces[1], preferred_element_type=jnp.float32)
    down_sel = down_add
    up_sel = up_add
    down_sel = down_sel.astype(jnp.bfloat16)
    up_sel = up_sel.astype(jnp.bfloat16)
    ends = jnp.cumsum(segment_block_count[0]) * 16
    positions = jnp.arange(tok_rows, dtype=jnp.int32)
    segment = jnp.sum((positions[:, None] >= ends[None, :]).astype(jnp.int32), axis=1)
    rank_cols = jnp.arange(GROUP_SEGMENTS * ADAPTER_RANK, dtype=jnp.int32) // ADAPTER_RANK
    within = segment[:, None] == rank_cols[None, :]
    low_part = lax.dot_general(
        acts,
        down_sel.reshape(GROUP_SEGMENTS * ADAPTER_RANK, feature_width),
        (((1,), (1,)), ((), ())),
        preferred_element_type=jnp.float32,
    )
    low_part = jnp.where(within, low_part, jnp.zeros_like(low_part))
    low = lax.psum(low_part.astype(jnp.bfloat16), "tensor")
    partial_sum = jnp.dot(acts, output_weight, preferred_element_type=jnp.float32)
    base_output = lax.psum_scatter(
        partial_sum.astype(jnp.bfloat16), "tensor", scatter_dimension=1, tiled=True
    ).astype(jnp.float32)
    adapter_delta = jnp.dot(
        low,
        up_sel.reshape(GROUP_SEGMENTS * ADAPTER_RANK, feature_width),
        preferred_element_type=jnp.float32,
    )
    return (base_output + adapter_scale * adapter_delta).astype(jnp.bfloat16)


def solution(mesh):
    in_specs = (
        P(("parts", "dp"), "tensor"),
        P("tensor", None),
        P("dp", None, "tensor"),
        P("dp", None, "tensor"),
        P(("parts", "dp"), None),
        P(("parts", "dp"), None),
        P("parts"),
    )
    out_specs = P(("parts", "dp"), "tensor")
    return jax.shard_map(body, mesh=mesh, in_specs=in_specs, out_specs=out_specs, check_vma=False)
```

profile of v0, /device:TPU:0, one launch (start us, length us, event | category | flops | bytes accessed | tf_op | source)
XLA Modules:
  0.0 894.1 jit_solution(12616775448118138298)
XLA Ops:
  7.4 0.0 copy-start
  7.4 0.0 all-gather.3.cloned.1.call-start
  7.4 9.0 %copy.17 = bf16[96,16,2048]{2,0,1:T(8,128)(2,1)} copy(bf16[96,16,2048]{2,1,0:T(8,128)(2,1)} %param.9) | data formatting | bytes 12582912 | tf_op args[2]
  16.4 0.0 all-gather.3.cloned.1.call-update
  16.4 0.0 all-gather.5.cloned.1.call-start
  16.5 8.8 copy.19
  25.3 0.0 all-gather.5.cloned.1.call-update
  25.3 0.0 reduce-scatter.2.cloned.1.call-start
  25.4 0.0 copy-done
  25.4 31.5 %convolution_convert_fusion = bf16[704,8192]{1,0:T(8,128)(2,1)} fusion(bf16[704,2048]{1,0:T(8,128)(2,1)S(1)} %copy-done, bf16[2048,8192]{1,0:T(8,128)(2,1)} %param.8), kind=kOutput, calls=%fused_computation.1 | convolution fusion | flops 23628087296 | bytes 47972352 | tf_op jit(solution)/shard_map/dot_general | solution.py:52
  56.9 0.0 copy-start.2
  56.9 0.0 copy-start.3
  56.9 0.0 copy-start.1
  56.9 0.0 reduce-scatter.2.cloned.1.call-update
  57.0 0.2 all-reduce.2.cloned.1.call-start
  57.2 0.4 copy-done.2
  57.6 0.1 copy.16
  57.7 0.0 copy-done.3
  57.7 0.0 copy-done.1
  57.7 0.7 gather_fusion
  58.4 0.1 multiply_reduce_fusion
  58.5 0.1 convert_reduce_fusion
  58.6 385.6 %all-gather.3.cloned.1.call-done = bf16[384,16,2048]{2,0,1:T(8,128)(2,1)} async-done(((bf16[96,16,2048]{2,0,1:T(8,128)(2,1)}), bf16[384,16,2048]{2,0,1:T(8,128)(2,1)}) %all-gather.3.cloned.1.call-update) | async-done | bytes 25165840 | tf_op jit(solution)/shard_map/all_gather | solution.py:26
  444.2 13.0 %convolution_convert_fusion.2 = bf16[16,16,2048]{2,0,1:T(8,128)(2,1)S(1)} fusion(bf16[384,16,2048]{2,0,1:T(8,128)(2,1)} %all-gather.3.cloned.1.call-done, s32[16]{0:T(128)S(1)} %gather_fusion), kind=kOutput, calls=%fused_computation.4 | convolution fusion | flops 403183616 | bytes 26214464 | tf_op jit(solution)/shard_map/sn,nrd->srd/dot_general | solution.py:33
  457.2 0.6 copy.18
  457.8 1.8 fusion.1
  459.5 0.0 all-reduce.2.cloned.1.call-update
  459.5 409.3 %all-gather.5.cloned.1.call-done = bf16[384,16,2048]{2,0,1:T(8,128)(2,1)} async-done(((bf16[96,16,2048]{2,0,1:T(8,128)(2,1)}), bf16[384,16,2048]{2,0,1:T(8,128)(2,1)}) %all-gather.5.cloned.1.call-update) | async-done | bytes 25165840 | tf_op jit(solution)/shard_map/all_gather | solution.py:27
  868.8 11.6 %convolution_convert_fusion.1 = bf16[16,16,2048]{2,0,1:T(8,128)(2,1)S(1)} fusion(bf16[384,16,2048]{2,0,1:T(8,128)(2,1)} %all-gather.5.cloned.1.call-done, s32[16]{0:T(128)S(1)} %gather_fusion), kind=kOutput, calls=%fused_computation.3 | convolution fusion | flops 403183616 | bytes 26214464 | tf_op jit(solution)/shard_map/sn,nrd->srd/dot_general | solution.py:34
  880.4 1.5 copy.20
  882.0 0.0 reduce-scatter.2.cloned.1.call-done
  882.0 0.0 all-reduce.2.cloned.1.call-done
  882.0 4.7 add_convert_fusion
  (4 shorter events, 0.0 us)
Async XLA Ops:
  7.4 18.0 %copy-start = (bf16[704,2048]{1,0:T(8,128)(2,1)S(1)}, bf16[704,2048]{1,0:T(8,128)(2,1)}, u32[]{:S(2)}) copy-start(bf16[704,2048]{1,0:T(8,128)(2,1)} %param.7) | copy-start | bytes 8650756
  7.4 436.8 %all-gather.3.cloned.1.call-start = ((), (), s32[]{:S(2)}) async-start(), calls=%async_computation.2 | async-start | bytes 31457280 | tf_op jit(solution)/shard_map/all_gather | solution.py:26
  16.4 852.4 %all-gather.5.cloned.1.call-start = ((), (), s32[]{:S(2)}) async-start(), calls=%async_computation.4 | async-start | bytes 31457280 | tf_op jit(solution)/shard_map/all_gather | solution.py:27
  25.3 856.6 %reduce-scatter.2.cloned.1.call-start = ((), (), s32[]{:S(2)}) async-start(), calls=%async_computation.1 | async-start | bytes 14417920 | tf_op jit(solution)/shard_map/reduce_scatter | solution.py:53
  56.9 0.7 copy-start.2
  56.9 0.7 copy-start.3
  56.9 0.8 copy-start.1
  57.0 825.0 %all-reduce.2.cloned.1.call-start = ((), (), s32[]{:S(2)}) async-start(), calls=%async_computation.3 | async-start | bytes 720896 | tf_op jit(solution)/shard_map/psum | solution.py:51
Sparse Core Ops, SparseCore 0:
  16.6 427.5 all-gather.2
  445.7 423.0 all-gather.4
Sparse Core Ops, SparseCore 1:
  57.0 95.5 reduce-scatter.1
  459.6 30.1 all-reduce.1
where the time goes:
time: 894 us
  waiting for transfers between devices  795 us (89%)
  matrix products  62.6 us (7%)
  local copies, waits for them, and re-layouts  21.1 us (2%)
  between operations  14.9 us (2%)
    all_gather x1, waiting for transfers between devices, body(): lax.all_gather(adapter_up_weight, 'dp', axis=0, tiled=True)  409 us
    all_gather x1, waiting for transfers between devices, body(): lax.all_gather(adapter_down_weight, 'dp', axis=0, tiled=True)  386 us
    dot_general x1, matrix products, body(): jnp.dot(acts, output_weight, preferred_element_type=jnp.float32)  31.5 us
    unnamed x10, local copies, waits for them, and re-layouts  18.3 us
  transfers between devices with their start and end apart: 4, of which 2 were waited for; matrix products, arithmetic and copies ran while one was open for 8% of the time, Pallas kernels for 0%

commit v1 on v0

v1 whole, which is shorter than its diff:
```python
import functools

import jax
import jax.numpy as jnp
from jax import lax
from jax.experimental import pallas as pl
from jax.experimental.pallas import tpu as pltpu
from jax.sharding import PartitionSpec as P

RANK = 16
SEGMENTS = 16
BLOCK = 16
CORES = 2
LANES = 128
adapter_scale = 0.5
VMEM_LIMIT = 40 * 1024 * 1024

ANY = pl.BlockSpec(memory_space=pl.ANY)
SMEM = pl.BlockSpec(memory_space=pltpu.SMEM)


def cost(flops, size):
    return pl.CostEstimate(flops=int(flops), bytes_accessed=int(size), transcendentals=0)


def chunks_of(width):
    if width % 1024:
        return [(0, width)]
    unit = width // 8
    return [(0, unit), (unit, 3 * unit), (4 * unit, 4 * unit)]


def product(place, acts, weight, shift, same_core, start, width, chips, add=None, after=()):
    rows, depth = acts.shape
    block = weight.shape[1] // (chips * CORES)
    tile = next(t for t in (256, 128) if start % t == 0 and width % t == 0)
    stride, first = block // tile, start // tile

    def columns(j, place_ref):
        core = place_ref[1] if same_core else 1 - place_ref[1]
        chip = lax.rem(place_ref[0] + shift, chips)
        return (0, (chip * CORES + core) * stride + first + j)

    def kernel(*refs):
        acts_ref, weight_ref = refs[1], refs[2]
        total = jnp.dot(acts_ref[...], weight_ref[...], preferred_element_type=jnp.float32)
        if add is not None:
            total = total + refs[3][...].astype(jnp.float32)
        refs[-1][...] = total.astype(jnp.bfloat16)

    operands = [acts, weight]
    specs = [pl.BlockSpec((rows, depth), lambda j, p: (0, 0)), pl.BlockSpec((depth, tile), columns)]
    if add is not None:
        operands.append(add)
        specs.append(pl.BlockSpec((rows, tile), lambda j, p: (0, j)))
    operands += list(after)
    specs += [ANY] * len(after)
    return pl.pallas_call(
        kernel,
        grid_spec=pltpu.PrefetchScalarGridSpec(
            num_scalar_prefetch=1,
            grid=(width // tile,),
            in_specs=specs,
            out_specs=pl.BlockSpec((rows, tile), lambda j, p: (0, j)),
        ),
        out_shape=jax.ShapeDtypeStruct((rows, width), jnp.bfloat16),
        compiler_params=pltpu.CompilerParams(vmem_limit_bytes=VMEM_LIMIT),
        cost_estimate=cost(2 * rows * depth * width, 2 * (rows * depth + depth * width + 2 * rows * width)),
    )(place, *operands)


def pick(ids, store_row, down, up, ways, cap, after=()):
    per_owner, rank, width = down.shape
    n_after = len(after)

    def kernel(*refs):
        id_refs, row_ref = refs[:ways], refs[ways]
        stores = refs[ways + 1 : ways + 3]
        outs = refs[ways + 3 + n_after : -2]
        slots, sems = refs[-2:]
        me = lax.axis_index("dp")
        for s in range(ways):
            for k in range(cap + 1):
                slots[s * (cap + 1) + k] = 0
            used = jnp.int32(0)
            for j in range(SEGMENTS):
                row = row_ref[id_refs[s][0, j]]
                local = row - me * per_owner
                mine = jnp.logical_and(local >= 0, local < per_owner)
                place = s * (cap + 1) + jnp.where(mine, jnp.minimum(used, cap), cap)
                slots[place] = jnp.where(mine, local, 0)
                used = used + mine.astype(jnp.int32)
        for which in range(2):
            for s in range(ways):
                out = outs[which * ways + s]
                for k in range(cap):
                    pltpu.make_async_copy(
                        stores[which].at[slots[s * (cap + 1) + k]],
                        out.at[pl.ds(k * rank, rank)],
                        sems.at[which * ways + s],
                    ).start()
        for which in range(2):
            for s in range(ways):
                out = outs[which * ways + s]
                pltpu.make_async_copy(out, out, sems.at[which * ways + s]).wait()

    shape = jax.ShapeDtypeStruct((cap * rank, width), jnp.bfloat16)
    outs = pl.pallas_call(
        kernel,
        in_specs=[SMEM] * (ways + 1) + [ANY] * (2 + n_after),
        out_specs=[ANY] * (2 * ways),
        out_shape=[shape] * (2 * ways),
        scratch_shapes=[pltpu.SMEM((ways * (cap + 1),), jnp.int32), pltpu.SemaphoreType.DMA((2 * ways,))],
        cost_estimate=cost(0, 4 * 2 * ways * cap * rank * width),
    )(*ids, store_row, down, up, *after)
    return outs[:ways], outs[ways:]


def token_slots(shape, axis, counts_ref, id_ref, row_ref, ways, cap, per_owner):
    me = lax.axis_index("dp")
    position = lax.broadcasted_iota(jnp.int32, shape, axis)
    owners, slot, start = [], jnp.full(shape, -1, jnp.int32), jnp.int32(0)
    for j in range(SEGMENTS):
        owner = row_ref[id_ref[0, j]] // per_owner
        order = jnp.int32(0)
        for other in owners:
            order = order + (other == owner).astype(jnp.int32)
        owners.append(owner)
        mine = lax.rem(me - owner + ways, ways) * cap + order
        slot = jnp.where(position >= start, mine, slot)
        start = start + counts_ref[0, j] * BLOCK
    return slot


def low_parts(acts, downs, counts, ids, store_row, cap, per_owner):
    rows, depth = acts.shape
    ways = len(downs)
    wide = ways * cap * RANK

    def kernel(counts_ref, id_ref, row_ref, acts_ref, *refs):
        out_ref = refs[-1]
        slot = token_slots((1, rows), 1, counts_ref, id_ref, row_ref, ways, cap, per_owner)
        total = jnp.zeros((RANK, rows), jnp.float32)
        for s in range(ways):
            part = lax.dot_general(
                refs[s][...], acts_ref[...], (((1,), (1,)), ((), ())), preferred_element_type=jnp.float32
            )
            for k in range(cap):
                piece = part[k * RANK : (k + 1) * RANK, :]
                total = total + jnp.where(slot == s * cap + k, piece, 0.0)
        out_ref[...] = total

    whole = pl.BlockSpec(memory_space=pltpu.VMEM)
    return pl.pallas_call(
        kernel,
        in_specs=[SMEM] * 3 + [whole] * (1 + ways),
        out_specs=whole,
        out_shape=jax.ShapeDtypeStruct((RANK, rows), jnp.float32),
        compiler_params=pltpu.CompilerParams(vmem_limit_bytes=VMEM_LIMIT),
        cost_estimate=cost(2 * rows * depth * wide, 2 * (rows * depth + wide * depth)),
    )(counts, ids, store_row, acts, *downs)


def spread(low, counts, ids, store_row, ways, cap, per_owner):
    rows = low.shape[1]
    wide = ways * cap * RANK

    def kernel(counts_ref, id_ref, row_ref, low_ref, out_ref):
        slot = token_slots((1, rows), 1, counts_ref, id_ref, row_ref, ways, cap, per_owner)
        held = low_ref[...]
        for k in range(ways * cap):
            out_ref[k * RANK : (k + 1) * RANK, :] = jnp.where(slot == k, held, 0.0).astype(jnp.bfloat16)

    whole = pl.BlockSpec(memory_space=pltpu.VMEM)
    return pl.pallas_call(
        kernel,
        in_specs=[SMEM] * 3 + [whole],
        out_specs=whole,
        out_shape=jax.ShapeDtypeStruct((wide, rows), jnp.bfloat16),
        cost_estimate=cost(0, 2 * wide * rows),
    )(counts, ids, store_row, low)


def finish(out, bases, base_start, arrived, low, ups, start, width, full):
    wide, rows = low.shape
    tile = next(t for t in (256, 128) if start % t == 0 and width % t == 0)
    first = start // tile
    ways = len(ups)
    depth = ups[0].shape[0]

    def kernel(*refs):
        out_ref = refs[-1]
        low_ref, up_refs = refs[0], refs[1 : 1 + ways]
        total = refs[1 + ways][...].astype(jnp.float32)
        for ref in refs[2 + ways : 2 + ways + len(arrived)]:
            total = total + ref[...].astype(jnp.float32)
        delta = jnp.zeros((rows, tile), jnp.float32)
        for s in range(ways):
            delta = delta + lax.dot_general(
                low_ref[s * depth : (s + 1) * depth, :],
                up_refs[s][...],
                (((0,), (0,)), ((), ())),
                preferred_element_type=jnp.float32,
            )
        out_ref[...] = (total + adapter_scale * delta).astype(jnp.bfloat16)

    here = pl.BlockSpec((rows, tile), lambda j: (0, j))
    there = pl.BlockSpec((rows, tile), lambda j: (0, first + j))
    base_first = (start - base_start) // tile
    specs = [pl.BlockSpec((wide, rows), lambda j: (0, 0))]
    specs += [pl.BlockSpec((depth, tile), lambda j: (0, first + j))] * ways
    specs += [pl.BlockSpec((rows, tile), lambda j: (0, base_first + j))] + [here] * len(arrived)
    operands = [low, *ups, bases, *arrived]
    aliases = {}
    if out is not None:
        aliases = {len(operands): 0}
        operands.append(out)
        specs.append(ANY)
    return pl.pallas_call(
        kernel,
        grid=(width // tile,),
        in_specs=specs,
        out_specs=there,
        out_shape=jax.ShapeDtypeStruct((rows, full), jnp.bfloat16),
        input_output_aliases=aliases,
        compiler_params=pltpu.CompilerParams(vmem_limit_bytes=VMEM_LIMIT),
        cost_estimate=cost(2 * rows * wide * width, 2 * rows * width * (2 + len(arrived)) + 2 * wide * width),
    )(*operands)


def body(ways, chips, acts, weight, down, up, counts, ids, store_row):
    per_owner = down.shape[0]
    rows, depth = acts.shape
    block = weight.shape[1] // (chips * CORES)
    cap = SEGMENTS // ways + 1
    tensor = lax.axis_index("tensor")
    place = jnp.stack([tensor // CORES, lax.rem(tensor, CORES)]).astype(jnp.int32)

    def along_dp(array, shift):
        return lax.ppermute(array, "dp", [(i, (i + shift) % ways) for i in range(ways)])

    def to_core(array):
        return lax.ppermute(array, "tensor", [(i, i ^ 1) for i in range(chips * CORES)])

    def to_chip(array, shift):
        size = chips * CORES
        return lax.ppermute(array, "tensor", [(i, (i + CORES * shift) % size) for i in range(size)])

    mul = functools.partial(product, place, acts, weight, chips=chips)
    chunks = chunks_of(block)
    first = [(shift, start, width) for (start, width) in chunks for shift in range(1, chips)]

    all_ids = [ids] + [along_dp(ids, -s) for s in range(1, ways)]
    sent = mul(*[first[0][0], False, *first[0][1:]])
    crossed = to_core(sent)
    downs, ups = pick(all_ids, store_row, down, up, ways, cap, after=(sent,))
    far_downs = [downs[0]] + [along_dp(downs[s], s) for s in range(1, ways)]

    arrived = {}
    for n, (shift, start, width) in enumerate(first):
        after = (downs[0],) if n == 0 else ()
        summed = mul(shift, True, start, width, add=crossed, after=after)
        arrived[shift, start] = to_chip(summed, shift)
        if n + 1 < len(first):
            shift, start, width = first[n + 1]
            crossed = to_core(mul(shift, False, start, width, after=(summed,)))
    crossed = to_core(mul(0, False, 0, block, after=(summed,)))
    base = mul(0, True, 0, block, add=crossed)

    low = lax.psum(low_parts(acts, far_downs, counts, ids, store_row, cap, per_owner), "tensor")
    low = spread(low, counts, ids, store_row, ways, cap, per_owner)
    far_ups = [ups[0]]
    for s in range(1, ways):
        held, _ = lax.optimization_barrier((ups[s], far_downs[s]))
        far_ups.append(along_dp(held, s))

    out = None
    for start, width in chunks:
        terms = [arrived[shift, start] for shift in range(1, chips)]
        out = finish(out, base, 0, terms, low, far_ups, start, width, block)
    return out


def solution(mesh):
    in_specs = (
        P(("parts", "dp"), "tensor"),
        P("tensor", None),
        P("dp", None, "tensor"),
        P("dp", None, "tensor"),
        P(("parts", "dp"), None),
        P(("parts", "dp"), None),
        P("parts"),
    )
    out_specs = P(("parts", "dp"), "tensor")
    ways, chips = mesh.shape["dp"], mesh.shape["tensor"] // CORES
    return jax.shard_map(
        functools.partial(body, ways, chips), mesh=mesh, in_specs=in_specs, out_specs=out_specs, check_vma=False
    )
```

time: 894 us -> 234 us (0.26)
  waiting for transfers between devices: 795 us -> 28.6 us
  Pallas kernels: 0 us -> 149 us
  matrix products: 62.6 us -> 0 us
  starting transfers between devices: 0.31 us -> 26 us
  blocking collectives: 0 us -> 25 us
  local copies, waits for them, and re-layouts: 21.1 us -> 4.03 us
  between operations: 14.9 us -> 0.23 us
    all_gather x2 -> x0, waiting for transfers between devices: 795 us -> none  [the longest x1 409 us: body(): lax.all_gather(adapter_up_weight, 'dp', axis=0, tiled=True)]
    pallas_call x0 -> x14, Pallas kernels: none -> 149 us  [the longest x1 81.6 us: pick(): pl.pallas_call(kernel, in_specs=[SMEM] * (ways + 1) + [ANY] * (2 + n_afte...]
    dot_general x5 -> x0, matrix products: 62.6 us -> none  [the longest x1 31.5 us: body(): jnp.dot(acts, output_weight, preferred_element_type=jnp.float32)]
    ppermute x0 -> x16, waiting for transfers between devices: none -> 28.6 us  [the longest x9 22.8 us: along_dp(): lax.ppermute(array, 'dp', [(i, (i + shift) % ways) for i in range(ways)])]
    ppermute x0 -> x16, starting transfers between devices: none -> 26 us  [the longest x9 22.4 us: along_dp(): lax.ppermute(array, 'dp', [(i, (i + shift) % ways) for i in range(ways)])]
    psum x0 -> x1, blocking collectives: none -> 25 us  [body(): lax.psum(low_parts(acts, far_downs, counts, ids, store_row, cap, per_owne...]
    unnamed x10 -> x38, local copies, waits for them, and re-layouts: 18.3 us -> 4.03 us
  transfers between devices with their start and end apart: 4 -> 16, of which waited for: 2 -> 6; matrix products, arithmetic and copies ran while one was open for 8% -> 0% of each run, Pallas kernels for 0% -> 45%
where the time goes in v1:
time: 234 us; the launch traced here: 233 us
  Pallas kernels  149 us (64%)
  waiting for transfers between devices  28.6 us (12%)
  starting transfers between devices  26 us (11%)
  blocking collectives  25 us (11%)
  local copies, waits for them, and re-layouts  4.03 us (2%)
    pallas_call x1, Pallas kernels, pick(): pl.pallas_call(kernel, in_specs=[SMEM] * (ways + 1) + [ANY] * (2 + n_afte...  81.6 us
    pallas_call x8, Pallas kernels, product(): pl.pallas_call(kernel, grid_spec=pltpu.PrefetchScalarGridSpec(num_scalar_...  51.2 us
    psum x1, blocking collectives, body(): lax.psum(low_parts(acts, far_downs, counts, ids, store_row, cap, per_owne...  25 us
    ppermute x9, waiting for transfers between devices, along_dp(): lax.ppermute(array, 'dp', [(i, (i + shift) % ways) for i in range(ways)])  22.8 us
    ppermute x9, starting transfers between devices, along_dp(): lax.ppermute(array, 'dp', [(i, (i + shift) % ways) for i in range(ways)])  22.4 us
    pallas_call x3, Pallas kernels, finish(): pl.pallas_call(kernel, grid=(width // tile,), in_specs=specs, out_specs=t...  10.2 us
    ppermute x4, waiting for transfers between devices, to_core(): lax.ppermute(array, 'tensor', [(i, i ^ 1) for i in range(chips * CORES)])  5.78 us
  transfers between devices with their start and end apart: 16, of which 6 were waited for; matrix products, arithmetic and copies ran while one was open for 0% of the time, Pallas kernels for 45%

profile of v1, /device:TPU:0, one launch (start us, length us, event | category | flops | bytes accessed | tf_op | source)
XLA Modules:
  0.0 233.1 jit_solution(17656110102321063564)
XLA Ops:
  0.0 0.1 pad_add_fusion.refs_0_
  0.1 1.8 copy-done
  1.9 2.7 %shard_map.73.refs_7_ = bf16[704,256]{1,0:T(8,128)(2,1)S(1)} custom-call(s32[2]{0:T(128)S(1)} %pad_add_fusion.refs_0_, bf16[704,2048]{1,0:T(8,128)(2,1)S(1)} %copy-done, bf16[2048,8192]{1,0:T(8,128)(2,1)} %refs_2_.15), custom_call_target="tpu_custom_call" | custom-call | flops 738197504 | bytes 4653056 | tf_op jit(solution)/shard_map/pallas_call | solution.py:58
  4.6 0.0 copy-start.5
  4.6 0.0 copy-start.1
  4.6 0.5 collective-permute-start.9
  5.1 2.6 %collective-permute-start.2 = (s32[1,16]{1,0:T(1,128)S(1)}, s32[1,16]{1,0:T(1,128)S(1)}, u32[]{:S(2)}, u32[]{:S(2)}) collective-permute-start(s32[1,16]{1,0:T(1,128)S(1)} %copy-done.10), channel_id=1, source_target_pairs={{0,4},{4,8},{8,12},{12,0},{1,5},{5,9},{9,13},{13,1},{2,6},{6,10},{... | collective-permute-start | bytes 200 | tf_op jit(solution)/shard_map/ppermute | solution.py:240
  7.8 2.6 %collective-permute-start.1 = (s32[1,16]{1,0:T(1,128)S(1)}, s32[1,16]{1,0:T(1,128)S(1)}, u32[]{:S(2)}, u32[]{:S(2)}) collective-permute-start(s32[1,16]{1,0:T(1,128)S(1)} %copy-done.10), channel_id=1, source_target_pairs={{0,8},{4,12},{8,0},{12,4},{1,9},{5,13},{9,1},{13,5},{2,10},{6,14},... | collective-permute-start | bytes 200 | tf_op jit(solution)/shard_map/ppermute | solution.py:240
  10.4 1.3 collective-permute-start
  11.7 0.0 collective-permute-done.2.refs_3_
  11.7 0.5 collective-permute-done.1.refs_2_
  12.2 1.7 collective-permute-done.refs_1_
  13.9 0.6 copy-done.15
  14.5 81.6 %shard_map.74 = (bf16[80,2048]{1,0:T(8,128)(2,1)}, bf16[80,2048]{1,0:T(8,128)(2,1)}, bf16[80,2048]{1,0:T(8,128)(2,1)}, bf16[80,2048]{1,0:T(8,128)(2,1)}, bf16[80...) custom-call(s32[1,16]{1,0:T(1,128)} %id_ref.3, ...), custom_call_target="tpu_custom_call" | custom-call | bytes 5242880 | tf_op jit(solution)/shard_map/pallas_call | solution.py:108
  96.1 1.0 copy-done.6
  97.1 2.8 %shard_map.77.refs_3_ = bf16[704,256]{1,0:T(8,128)(2,1)S(1)} custom-call(s32[2]{0:T(128)S(1)} %pad_add_fusion.refs_0_, bf16[704,2048]{1,0:T(8,128)(2,1)S(1)} %copy-done.1, bf16[2048,8192]{1,0:T(8,128)(2,1)} %refs_2_.15, bf16[704,256]{1,0:T(8,128)(2,1)} %collective-permute-done.9.refs_3_, bf16[80,2048]{1,0:T(8,128)(2,1)S(1)} %copy-done.6), custom_call_target="tpu_custom_call" | custom-call | flops 738197504 | bytes 4653056 | tf_op jit(solution)/shard_map/pallas_call | solution.py:58
  99.9 4.9 %shard_map.78 = bf16[704,768]{1,0:T(8,128)(2,1)S(1)} custom-call(s32[2]{0:T(128)S(1)} %pad_add_fusion.refs_0_, bf16[704,2048]{1,0:T(8,128)(2,1)S(1)} %copy-done.1, bf16[2048,8192]{1,0:T(8,128)(2,1)} %refs_2_.15, bf16[704,256]{1,0:T(8,128)(2,1)S(1)} %shard_map.77.refs_3_), custom_call_target="tpu_custom_call" | custom-call | flops 2214592512 | bytes 8192000 | tf_op jit(solution)/shard_map/pallas_call | solution.py:58
  104.8 0.1 collective-permute-start.10
  104.9 2.7 %collective-permute-done.10.refs_3_ = bf16[704,768]{1,0:T(8,128)(2,1)S(1)} collective-permute-done((bf16[704,768]{1,0:T(8,128)(2,1)S(1)}, bf16[704,768]{1,0:T(8,128)(2,1)S(1)}, u32[]{:S(2)}, u32[]{:S(2)}) %collective-permute-start.10) | collective-permute-done | bytes 1081376 | tf_op jit(solution)/shard_map/ppermute | solution.py:243
  107.6 5.8 %shard_map.79.refs_3_ = bf16[704,768]{1,0:T(8,128)(2,1)} custom-call(s32[2]{0:T(128)S(1)} %pad_add_fusion.refs_0_, bf16[704,2048]{1,0:T(8,128)(2,1)S(1)} %copy-done.1, bf16[2048,8192]{1,0:T(8,128)(2,1)} %refs_2_.15, bf16[704,768]{1,0:T(8,128)(2,1)S(1)} %collective-permute-done.10.refs_3_), custom_call_target="tpu_custom_call" | custom-call | flops 2214592512 | bytes 8192000 | tf_op jit(solution)/shard_map/pallas_call | solution.py:58
  113.4 5.9 %shard_map.80 = bf16[704,1024]{1,0:T(8,128)(2,1)S(1)} custom-call(s32[2]{0:T(128)S(1)} %pad_add_fusion.refs_0_, bf16[704,2048]{1,0:T(8,128)(2,1)S(1)} %copy-done.1, bf16[2048,8192]{1,0:T(8,128)(2,1)} %refs_2_.15, bf16[704,768]{1,0:T(8,128)(2,1)} %shard_map.79.refs_3_), custom_call_target="tpu_custom_call" | custom-call | flops 2952790016 | bytes 9961472 | tf_op jit(solution)/shard_map/pallas_call | solution.py:58
  119.3 0.2 collective-permute-start.11
  119.5 3.1 %collective-permute-done.11.refs_3_ = bf16[704,1024]{1,0:T(8,128)(2,1)S(1)} collective-permute-done((bf16[704,1024]{1,0:T(8,128)(2,1)S(1)}, bf16[704,1024]{1,0:T(8,128)(2,1)S(1)}, u32[]{:S(2)}, u32[]{:S(2)}) %collective-permute-start.11) | collective-permute-done | bytes 1441824 | tf_op jit(solution)/shard_map/ppermute | solution.py:243
  122.6 6.9 %shard_map.81.refs_3_ = bf16[704,1024]{1,0:T(8,128)(2,1)} custom-call(s32[2]{0:T(128)S(1)} %pad_add_fusion.refs_0_, bf16[704,2048]{1,0:T(8,128)(2,1)S(1)} %copy-done.1, bf16[2048,8192]{1,0:T(8,128)(2,1)} %refs_2_.15, bf16[704,1024]{1,0:T(8,128)(2,1)S(1)} %collective-permute-done.11.refs_3_), custom_call_target="tpu_custom_call" | custom-call | flops 2952790016 | bytes 9961472 | tf_op jit(solution)/shard_map/pallas_call | solution.py:58
  129.5 0.0 copy-start.9
  129.5 0.0 copy-start.11
  129.5 0.0 copy-start.12
  129.5 11.5 %shard_map.82 = bf16[704,2048]{1,0:T(8,128)(2,1)} custom-call(s32[2]{0:T(128)S(1)} %pad_add_fusion.refs_0_, bf16[704,2048]{1,0:T(8,128)(2,1)S(1)} %copy-done.1, bf16[2048,8192]{1,0:T(8,128)(2,1)} %refs_2_.15, bf16[704,1024]{1,0:T(8,128)(2,1)} %shard_map.81.refs_3_), custom_call_target="tpu_custom_call" | custom-call | flops 5905580032 | bytes 17039360 | tf_op jit(solution)/shard_map/pallas_call | solution.py:58
  141.0 0.1 collective-permute-start.12
  141.1 1.5 collective-permute-start.13
  142.6 0.5 collective-permute-start.3
  143.1 3.3 %collective-permute-start.4 = (bf16[80,2048]{1,0:T(8,128)(2,1)S(1)}, bf16[80,2048]{1,0:T(8,128)(2,1)S(1)}, u32[]{:S(2)}, u32[]{:S(2)}) collective-permute-start(bf16[80,2048]{1,0:T(8,128)(2,1)S(1)} %copy-done.17), channel_id=1, source_target_pairs={{0,8},{4,12},{8,0},{12,4},{1,9},{5,13},{9,1},{13,5},{2,10},{6,14},... | collective-permute-start | bytes 983048 | tf_op jit(solution)/shard_map/ppermute | solution.py:240
  146.3 0.5 collective-permute-start.14
  146.9 8.2 %collective-permute-done.3.refs_1_ = bf16[80,2048]{1,0:T(8,128)(2,1)S(1)} collective-permute-done((bf16[80,2048]{1,0:T(8,128)(2,1)S(1)}, bf16[80,2048]{1,0:T(8,128)(2,1)S(1)}, u32[]{:S(2)}, u32[]{:S(2)}) %collective-permute-start.3) | collective-permute-done | bytes 327712 | tf_op jit(solution)/shard_map/ppermute | solution.py:240
  155.1 0.8 collective-permute-start.5
  155.9 12.4 %collective-permute-done.4.refs_2_ = bf16[80,2048]{1,0:T(8,128)(2,1)S(1)} collective-permute-done((bf16[80,2048]{1,0:T(8,128)(2,1)S(1)}, bf16[80,2048]{1,0:T(8,128)(2,1)S(1)}, u32[]{:S(2)}, u32[]{:S(2)}) %collective-permute-start.4) | collective-permute-done | bytes 327712 | tf_op jit(solution)/shard_map/ppermute | solution.py:240
  168.2 4.8 %collective-permute-start.6 = (bf16[80,2048]{1,0:T(8,128)(2,1)}, bf16[80,2048]{1,0:T(8,128)(2,1)S(1)}, u32[]{:S(2)}, u32[]{:S(2)}) collective-permute-start(bf16[80,2048]{1,0:T(8,128)(2,1)} %get-tuple-element.22), channel_id=1, source_target_pairs={{0,4},{4,8},{8,12},{12,0},{1,5},{5,9},{9,13},{13,1},{2,6},{6,10},{... | collective-permute-start | bytes 983048 | tf_op jit(solution)/shard_map/ppermute | solution.py:240
  173.0 3.4 %collective-permute-start.7 = (bf16[80,2048]{1,0:T(8,128)(2,1)}, bf16[80,2048]{1,0:T(8,128)(2,1)S(1)}, u32[]{:S(2)}, u32[]{:S(2)}) collective-permute-start(bf16[80,2048]{1,0:T(8,128)(2,1)} %get-tuple-element.24), channel_id=1, source_target_pairs={{0,8},{4,12},{8,0},{12,4},{1,9},{5,13},{9,1},{13,5},{2,10},{6,14},... | collective-permute-start | bytes 983048 | tf_op jit(solution)/shard_map/ppermute | solution.py:240
  176.4 4.2 %shard_map.75 = f32[16,704]{1,0:T(8,128)S(1)} custom-call(s32[1,16]{1,0:T(1,128)S(1)} %copy-done.12, s32[1,16]{1,0:T(1,128)S(1)} %copy-done.11, s32[384]{0:T(512)S(1)} %copy-done.9, bf16[704,2048]{1,0:T(8,128)(2,1)S(1)} %copy-done.1, bf16[80,2048]{1,0:T(8,128)(2,1)S(1)} %copy-done.7, bf16[80,2048]{1,0:T(8,128)(2,1)S(1)} %collective-permute-done.3.refs_1_, ...), custom_call_target="tpu_custom_call" | custom-call | flops 922746880 | bytes 4194304 | tf_op jit(solution)/shard_map/pallas_call | solution.py:154
  180.6 0.6 copy-done.8
  181.2 25.0 %psum.7.low_ref = f32[16,704]{1,0:T(8,128)} all-reduce(f32[16,704]{1,0:T(8,128)} %copy-done.8), channel_id=1, replica_groups=mesh['parts'=2,'dp'=4,'tensor'=4] {'tensor'}, use_global_device_ids=true, to_apply=%region_0.1 | all-reduce | flops 11264 | bytes 90112 | tf_op jit(solution)/shard_map/psum | solution.py:270
  206.2 2.0 shard_map.76.refs_0_
  208.2 3.2 %collective-permute-start.8 = (bf16[80,2048]{1,0:T(8,128)(2,1)}, bf16[80,2048]{1,0:T(8,128)(2,1)S(1)}, u32[]{:S(2)}, u32[]{:S(2)}) collective-permute-start(bf16[80,2048]{1,0:T(8,128)(2,1)} %get-tuple-element.26), channel_id=1, source_target_pairs={{0,12},{4,0},{8,4},{12,8},{1,13},{5,1},{9,5},{13,9},{2,14},{6,2},{... | collective-permute-start | bytes 983048 | tf_op jit(solution)/shard_map/ppermute | solution.py:240
  211.4 0.6 collective-permute-start.15
  212.0 10.8 %shard_map.83.refs_5_ = bf16[704,2048]{1,0:T(8,128)(2,1)S(1)} custom-call(s32[2]{0:T(128)S(1)} %pad_add_fusion.refs_0_, bf16[704,2048]{1,0:T(8,128)(2,1)S(1)} %copy-done.1, bf16[2048,8192]{1,0:T(8,128)(2,1)} %refs_2_.15, bf16[704,2048]{1,0:T(8,128)(2,1)} %collective-permute-done.12.refs_3_), custom_call_target="tpu_custom_call" | custom-call | flops 5905580032 | bytes 17039360 | tf_op jit(solution)/shard_map/pallas_call | solution.py:58
  222.9 1.3 shard_map.84.refs_7_
  224.2 4.1 %shard_map.85.refs_7_ = bf16[704,2048]{1,0:T(8,128)(2,1)} custom-call(bf16[320,704]{1,0:T(8,128)(2,1)S(1)} %copy-done.2, bf16[80,2048]{1,0:T(8,128)(2,1)S(1)} %copy-done.3, bf16[80,2048]{1,0:T(8,128)(2,1)S(1)} %collective-permute-done.6.refs_2_, bf16[80,2048]{1,0:T(8,128)(2,1)S(1)} %collective-permute-done.7.refs_3_, ...), custom_call_target="tpu_custom_call", output_to_operand_aliasing={{}: (7, {})} | custom-call | flops 346030080 | bytes 3735552 | tf_op jit(solution)/shard_map/pallas_call | solution.py:219
  228.3 4.8 %shard_map.86 = bf16[704,2048]{1,0:T(8,128)(2,1)} custom-call(bf16[320,704]{1,0:T(8,128)(2,1)S(1)} %copy-done.2, bf16[80,2048]{1,0:T(8,128)(2,1)S(1)} %copy-done.3, bf16[80,2048]{1,0:T(8,128)(2,1)S(1)} %collective-permute-done.6.refs_2_, bf16[80,2048]{1,0:T(8,128)(2,1)S(1)} %collective-permute-done.7.refs_3_, ...), custom_call_target="tpu_custom_call", output_to_operand_aliasing={{}: (7, {})} | custom-call | flops 461373440 | bytes 4980736 | tf_op jit(solution)/shard_map/pallas_call | solution.py:219
  (38 shorter events, 0.1 us)
Async XLA Ops:
  0.1 1.8 copy-start
  1.9 3.2 %copy-start.10 = (s32[1,16]{1,0:T(1,128)S(1)}, s32[1,16]{1,0:T(1,128)}, u32[]{:S(2)}) copy-start(s32[1,16]{1,0:T(1,128)} %id_ref.3) | copy-start | bytes 196
  4.6 9.3 %copy-start.5 = (bf16[704,256]{1,0:T(8,128)(2,1)}, bf16[704,256]{1,0:T(8,128)(2,1)S(1)}, u32[]{:S(2)}) copy-start(bf16[704,256]{1,0:T(8,128)(2,1)S(1)} %shard_map.73.refs_7_) | copy-start | bytes 1081348
  4.6 91.5 %copy-start.1 = (bf16[704,2048]{1,0:T(8,128)(2,1)S(1)}, bf16[704,2048]{1,0:T(8,128)(2,1)}, u32[]{:S(2)}) copy-start(bf16[704,2048]{1,0:T(8,128)(2,1)} %refs_1_.15) | copy-start | bytes 8650756
  4.6 91.5 %collective-permute-start.9 = (bf16[704,256]{1,0:T(8,128)(2,1)S(1)}, bf16[704,256]{1,0:T(8,128)(2,1)}, u32[]{:S(2)}, u32[]{:S(2)}) collective-permute-start(bf16[704,256]{1,0:T(8,128)(2,1)S(1)} %shard_map.73.refs_7_), channel_id=1, source_target_pairs={{0,1},{1,0},{2,3},{3,2},{4,5},{5,4},{6,7},{7,6},{8,9},{9,8},{10,11... | collective-permute-start | bytes 1081352 | tf_op jit(solution)/shard_map/ppermute | solution.py:243
  5.1 6.6 %collective-permute-start.2 = (s32[1,16]{1,0:T(1,128)S(1)}, s32[1,16]{1,0:T(1,128)S(1)}, u32[]{:S(2)}, u32[]{:S(2)}) collective-permute-start(s32[1,16]{1,0:T(1,128)S(1)} %copy-done.10), channel_id=1, source_target_pairs={{0,4},{4,8},{8,12},{12,0},{1,5},{5,9},{9,13},{13,1},{2,6},{6,10},{... | collective-permute-start | bytes 200 | tf_op jit(solution)/shard_map/ppermute | solution.py:240
  7.8 4.4 %collective-permute-start.1 = (s32[1,16]{1,0:T(1,128)S(1)}, s32[1,16]{1,0:T(1,128)S(1)}, u32[]{:S(2)}, u32[]{:S(2)}) collective-permute-start(s32[1,16]{1,0:T(1,128)S(1)} %copy-done.10), channel_id=1, source_target_pairs={{0,8},{4,12},{8,0},{12,4},{1,9},{5,13},{9,1},{13,5},{2,10},{6,14},... | collective-permute-start | bytes 200 | tf_op jit(solution)/shard_map/ppermute | solution.py:240
  10.4 3.5 %collective-permute-start = (s32[1,16]{1,0:T(1,128)S(1)}, s32[1,16]{1,0:T(1,128)S(1)}, u32[]{:S(2)}, u32[]{:S(2)}) collective-permute-start(s32[1,16]{1,0:T(1,128)S(1)} %copy-done.10), channel_id=1, source_target_pairs={{0,12},{4,0},{8,4},{12,8},{1,13},{5,1},{9,5},{13,9},{2,14},{6,2},{... | collective-permute-start | bytes 200 | tf_op jit(solution)/shard_map/ppermute | solution.py:240
  11.7 2.2 copy-start.13
  12.2 1.7 copy-start.14
  13.9 0.6 copy-start.15
  96.1 1.0 copy-start.6
  99.9 4.9 %copy-start.4 = (bf16[704,256]{1,0:T(8,128)(2,1)}, bf16[704,256]{1,0:T(8,128)(2,1)S(1)}, u32[]{:S(2)}) copy-start(bf16[704,256]{1,0:T(8,128)(2,1)S(1)} %shard_map.77.refs_3_) | copy-start | bytes 1081348
  104.8 2.8 %collective-permute-start.10 = (bf16[704,768]{1,0:T(8,128)(2,1)S(1)}, bf16[704,768]{1,0:T(8,128)(2,1)S(1)}, u32[]{:S(2)}, u32[]{:S(2)}) collective-permute-start(bf16[704,768]{1,0:T(8,128)(2,1)S(1)} %shard_map.78), channel_id=1, source_target_pairs={{0,1},{1,0},{2,3},{3,2},{4,5},{5,4},{6,7},{7,6},{8,9},{9,8},{10,11... | collective-permute-start | bytes 3244040 | tf_op jit(solution)/shard_map/ppermute | solution.py:243
  119.3 3.3 %collective-permute-start.11 = (bf16[704,1024]{1,0:T(8,128)(2,1)S(1)}, bf16[704,1024]{1,0:T(8,128)(2,1)S(1)}, u32[]{:S(2)}, u32[]{:S(2)}) collective-permute-start(bf16[704,1024]{1,0:T(8,128)(2,1)S(1)} %shard_map.80), channel_id=1, source_target_pairs={{0,1},{1,0},{2,3},{3,2},{4,5},{5,4},{6,7},{7,6},{8,9},{9,8},{10,11... | collective-permute-start | bytes 4325384 | tf_op jit(solution)/shard_map/ppermute | solution.py:243
  129.5 13.2 %copy-start.18 = (bf16[80,2048]{1,0:T(8,128)(2,1)S(1)}, bf16[80,2048]{1,0:T(8,128)(2,1)}, u32[]{:S(2)}) copy-start(bf16[80,2048]{1,0:T(8,128)(2,1)} %get-tuple-element.17) | copy-start | bytes 983044
  129.5 13.6 %copy-start.17 = (bf16[80,2048]{1,0:T(8,128)(2,1)S(1)}, bf16[80,2048]{1,0:T(8,128)(2,1)}, u32[]{:S(2)}) copy-start(bf16[80,2048]{1,0:T(8,128)(2,1)} %get-tuple-element.18) | copy-start | bytes 983044
  129.5 25.6 %copy-start.16 = (bf16[80,2048]{1,0:T(8,128)(2,1)S(1)}, bf16[80,2048]{1,0:T(8,128)(2,1)}, u32[]{:S(2)}) copy-start(bf16[80,2048]{1,0:T(8,128)(2,1)} %get-tuple-element.19) | copy-start | bytes 983044
  129.5 46.9 %copy-start.7 = (bf16[80,2048]{1,0:T(8,128)(2,1)S(1)}, bf16[80,2048]{1,0:T(8,128)(2,1)}, u32[]{:S(2)}) copy-start(bf16[80,2048]{1,0:T(8,128)(2,1)} %get-tuple-element.16.refs_0_.refs_4_) | copy-start | bytes 983044
  129.5 46.9 %copy-start.9 = (s32[384]{0:T(512)S(1)}, s32[384]{0:T(512)}, u32[]{:S(2)}) copy-start(s32[384]{0:T(512)} %row_ref.3) | copy-start | bytes 4612
  129.5 46.9 %copy-start.11 = (s32[1,16]{1,0:T(1,128)S(1)}, s32[1,16]{1,0:T(1,128)}, u32[]{:S(2)}) copy-start(s32[1,16]{1,0:T(1,128)} %id_ref.3) | copy-start | bytes 196
  129.5 46.9 %copy-start.12 = (s32[1,16]{1,0:T(1,128)S(1)}, s32[1,16]{1,0:T(1,128)}, u32[]{:S(2)}) copy-start(s32[1,16]{1,0:T(1,128)} %counts_ref.3) | copy-start | bytes 196
  141.0 70.4 %collective-permute-start.12 = (bf16[704,2048]{1,0:T(8,128)(2,1)}, bf16[704,2048]{1,0:T(8,128)(2,1)}, u32[]{:S(2)}, u32[]{:S(2)}) collective-permute-start(bf16[704,2048]{1,0:T(8,128)(2,1)} %shard_map.82), channel_id=1, source_target_pairs={{0,1},{1,0},{2,3},{3,2},{4,5},{5,4},{6,7},{7,6},{8,9},{9,8},{10,11... | collective-permute-start | bytes 8650760 | tf_op jit(solution)/shard_map/ppermute | solution.py:243
  141.1 87.2 %collective-permute-start.13 = (bf16[704,1024]{1,0:T(8,128)(2,1)}, bf16[704,1024]{1,0:T(8,128)(2,1)}, u32[]{:S(2)}, u32[]{:S(2)}) collective-permute-start(bf16[704,1024]{1,0:T(8,128)(2,1)} %shard_map.81.refs_3_), channel_id=1, source_target_pairs={{0,2},{1,3},{2,0},{3,1},{4,6},{5,7},{6,4},{7,5},{8,10},{9,11},{10,... | collective-permute-start | bytes 4325384 | tf_op jit(solution)/shard_map/ppermute | solution.py:247
  142.6 12.5 %collective-permute-start.3 = (bf16[80,2048]{1,0:T(8,128)(2,1)S(1)}, bf16[80,2048]{1,0:T(8,128)(2,1)S(1)}, u32[]{:S(2)}, u32[]{:S(2)}) collective-permute-start(bf16[80,2048]{1,0:T(8,128)(2,1)S(1)} %copy-done.18), channel_id=1, source_target_pairs={{0,4},{4,8},{8,12},{12,0},{1,5},{5,9},{9,13},{13,1},{2,6},{6,10},{... | collective-permute-start | bytes 983048 | tf_op jit(solution)/shard_map/ppermute | solution.py:240
  143.1 25.2 %collective-permute-start.4 = (bf16[80,2048]{1,0:T(8,128)(2,1)S(1)}, bf16[80,2048]{1,0:T(8,128)(2,1)S(1)}, u32[]{:S(2)}, u32[]{:S(2)}) collective-permute-start(bf16[80,2048]{1,0:T(8,128)(2,1)S(1)} %copy-done.17), channel_id=1, source_target_pairs={{0,8},{4,12},{8,0},{12,4},{1,9},{5,13},{9,1},{13,5},{2,10},{6,14},... | collective-permute-start | bytes 983048 | tf_op jit(solution)/shard_map/ppermute | solution.py:240
  146.3 77.9 %collective-permute-start.14 = (bf16[704,768]{1,0:T(8,128)(2,1)}, bf16[704,768]{1,0:T(8,128)(2,1)}, u32[]{:S(2)}, u32[]{:S(2)}) collective-permute-start(bf16[704,768]{1,0:T(8,128)(2,1)} %shard_map.79.refs_3_), channel_id=1, source_target_pairs={{0,2},{1,3},{2,0},{3,1},{4,6},{5,7},{6,4},{7,5},{8,10},{9,11},{10,... | collective-permute-start | bytes 3244040 | tf_op jit(solution)/shard_map/ppermute | solution.py:247
  155.1 17.9 %collective-permute-start.5 = (bf16[80,2048]{1,0:T(8,128)(2,1)S(1)}, bf16[80,2048]{1,0:T(8,128)(2,1)S(1)}, u32[]{:S(2)}, u32[]{:S(2)}) collective-permute-start(bf16[80,2048]{1,0:T(8,128)(2,1)S(1)} %copy-done.16), channel_id=1, source_target_pairs={{0,12},{4,0},{8,4},{12,8},{1,13},{5,1},{9,5},{13,9},{2,14},{6,2},{... | collective-permute-start | bytes 983048 | tf_op jit(solution)/shard_map/ppermute | solution.py:240
  168.2 40.0 %collective-permute-start.6 = (bf16[80,2048]{1,0:T(8,128)(2,1)}, bf16[80,2048]{1,0:T(8,128)(2,1)S(1)}, u32[]{:S(2)}, u32[]{:S(2)}) collective-permute-start(bf16[80,2048]{1,0:T(8,128)(2,1)} %get-tuple-element.22), channel_id=1, source_target_pairs={{0,4},{4,8},{8,12},{12,0},{1,5},{5,9},{9,13},{13,1},{2,6},{6,10},{... | collective-permute-start | bytes 983048 | tf_op jit(solution)/shard_map/ppermute | solution.py:240
  173.0 49.8 %collective-permute-start.7 = (bf16[80,2048]{1,0:T(8,128)(2,1)}, bf16[80,2048]{1,0:T(8,128)(2,1)S(1)}, u32[]{:S(2)}, u32[]{:S(2)}) collective-permute-start(bf16[80,2048]{1,0:T(8,128)(2,1)} %get-tuple-element.24), channel_id=1, source_target_pairs={{0,8},{4,12},{8,0},{12,4},{1,9},{5,13},{9,1},{13,5},{2,10},{6,14},... | collective-permute-start | bytes 983048 | tf_op jit(solution)/shard_map/ppermute | solution.py:240
  180.6 0.6 copy-start.8
  208.2 14.6 %copy-start.2 = (bf16[320,704]{1,0:T(8,128)(2,1)S(1)}, bf16[320,704]{1,0:T(8,128)(2,1)}, u32[]{:S(2)}) copy-start(bf16[320,704]{1,0:T(8,128)(2,1)} %shard_map.76.refs_0_) | copy-start | bytes 1351684
  208.2 14.6 %copy-start.3 = (bf16[80,2048]{1,0:T(8,128)(2,1)S(1)}, bf16[80,2048]{1,0:T(8,128)(2,1)}, u32[]{:S(2)}) copy-start(bf16[80,2048]{1,0:T(8,128)(2,1)} %get-tuple-element.20.refs_1_) | copy-start | bytes 983044
  208.2 14.6 %collective-permute-start.8 = (bf16[80,2048]{1,0:T(8,128)(2,1)}, bf16[80,2048]{1,0:T(8,128)(2,1)S(1)}, u32[]{:S(2)}, u32[]{:S(2)}) collective-permute-start(bf16[80,2048]{1,0:T(8,128)(2,1)} %get-tuple-element.26), channel_id=1, source_target_pairs={{0,12},{4,0},{8,4},{12,8},{1,13},{5,1},{9,5},{13,9},{2,14},{6,2},{... | collective-permute-start | bytes 983048 | tf_op jit(solution)/shard_map/ppermute | solution.py:240
  211.4 11.4 %collective-permute-start.15 = (bf16[704,256]{1,0:T(8,128)(2,1)}, bf16[704,256]{1,0:T(8,128)(2,1)S(1)}, u32[]{:S(2)}, u32[]{:S(2)}) collective-permute-start(bf16[704,256]{1,0:T(8,128)(2,1)} %copy-done.4), channel_id=1, source_target_pairs={{0,2},{1,3},{2,0},{3,1},{4,6},{5,7},{6,4},{7,5},{8,10},{9,11},{10,... | collective-permute-start | bytes 1081352 | tf_op jit(solution)/shard_map/ppermute | solution.py:247

commit v2 on v1

v2 whole, which is shorter than its diff:
```python
import functools
import math

import jax
import jax.numpy as jnp
from jax import lax
from jax.experimental import pallas as pl
from jax.experimental.pallas import tpu as pltpu
from jax.sharding import PartitionSpec as P

RANK = 16
SEGMENTS = 16
BLOCK = 16
CORES = 2
LANES = 128
adapter_scale = 0.5
VMEM_LIMIT = 20 * 1024 * 1024

ANY = pl.BlockSpec(memory_space=pl.ANY)
SMEM = pl.BlockSpec(memory_space=pltpu.SMEM)
WHOLE = pl.BlockSpec(memory_space=pltpu.VMEM)
CHEAP = pl.CostEstimate(flops=1000, bytes_accessed=1000, transcendentals=0)
PARAMS = pltpu.CompilerParams(vmem_limit_bytes=VMEM_LIMIT)


def chunks_of(width):
    if width % 2048:
        return [(0, width)]
    unit = width // 8
    return [(0, 2 * unit), (2 * unit, 3 * unit), (5 * unit, 3 * unit)]


def tile_of(start, width):
    return next(t for t in (512, 384, 256, 128) if start % t == 0 and width % t == 0)


def product(place, acts, weight, shift, same_core, start, width, chips, add=None, after=(), into=None, total=None, at=0):
    rows, depth = acts.shape
    block = weight.shape[1] // (chips * CORES)
    tile = tile_of(math.gcd(start, at), width)
    stride, first = block // tile, start // tile

    def columns(j, place_ref):
        core = place_ref[1] if same_core else 1 - place_ref[1]
        chip = lax.rem(place_ref[0] + shift, chips)
        return (0, (chip * CORES + core) * stride + first + j)

    def kernel(*refs):
        acts_ref, weight_ref = refs[1], refs[2]
        value = jnp.dot(acts_ref[...], weight_ref[...], preferred_element_type=jnp.float32)
        if add is not None:
            value = value + refs[3][...].astype(jnp.float32)
        refs[-1][...] = value.astype(jnp.bfloat16)

    operands = [acts, weight]
    specs = [WHOLE, pl.BlockSpec((depth, tile), columns)]
    if add is not None:
        operands.append(add)
        specs.append(pl.BlockSpec((rows, tile), lambda j, p: (0, j)))
    aliases = {}
    if into is not None:
        aliases = {len(operands) + 1: 0}
        operands.append(into)
        specs.append(ANY)
    operands += list(after)
    specs += [ANY] * len(after)
    place_at = at // tile
    return pl.pallas_call(
        kernel,
        grid_spec=pltpu.PrefetchScalarGridSpec(
            num_scalar_prefetch=1,
            grid=(width // tile,),
            in_specs=specs,
            out_specs=pl.BlockSpec((rows, tile), lambda j, p: (0, place_at + j)),
        ),
        out_shape=jax.ShapeDtypeStruct((rows, total or width), jnp.bfloat16),
        input_output_aliases=aliases,
        compiler_params=PARAMS,
        cost_estimate=CHEAP,
    )(place, *operands)


def pick(ids, store_row, down, up, ways, cap, after=()):
    per_owner, rank, width = down.shape
    n_after = len(after)

    def kernel(*refs):
        id_refs, row_ref = refs[:ways], refs[ways]
        stores = refs[ways + 1 : ways + 3]
        outs = refs[ways + 3 + n_after : -2]
        slots, sems = refs[-2:]
        me = lax.axis_index("dp")
        for s in range(ways):
            for k in range(cap + 1):
                slots[s * (cap + 1) + k] = 0
            used = jnp.int32(0)
            for j in range(SEGMENTS):
                row = row_ref[id_refs[s][0, j]]
                local = row - me * per_owner
                mine = jnp.logical_and(local >= 0, local < per_owner)
                place = s * (cap + 1) + jnp.where(mine, jnp.minimum(used, cap), cap)
                slots[place] = jnp.where(mine, local, 0)
                used = used + mine.astype(jnp.int32)
        for which in range(2):
            for s in range(ways):
                out = outs[which * ways + s]
                for k in range(cap):
                    pltpu.make_async_copy(
                        stores[which].at[slots[s * (cap + 1) + k]],
                        out.at[pl.ds(k * rank, rank)],
                        sems.at[which * ways + s],
                    ).start()
        for which in range(2):
            for s in range(ways):
                out = outs[which * ways + s]
                pltpu.make_async_copy(out, out, sems.at[which * ways + s]).wait()

    shape = jax.ShapeDtypeStruct((cap * rank, width), jnp.bfloat16)
    outs = pl.pallas_call(
        kernel,
        in_specs=[SMEM] * (ways + 1) + [ANY] * (2 + n_after),
        out_specs=[WHOLE] * (2 * ways),
        out_shape=[shape] * (2 * ways),
        scratch_shapes=[pltpu.SMEM((ways * (cap + 1),), jnp.int32), pltpu.SemaphoreType.DMA((2 * ways,))],
        compiler_params=PARAMS,
        cost_estimate=CHEAP,
    )(*ids, store_row, down, up, *after)
    return outs[:ways], outs[ways:]


def slot_mask(shape, counts_ref, id_ref, row_ref, ways, cap, per_owner):
    me = lax.axis_index("dp")
    column = lax.broadcasted_iota(jnp.int32, (1, shape[1]), 1) // RANK
    first = jnp.zeros((1, shape[1]), jnp.int32)
    last, start, owners = first, jnp.int32(0), []
    for j in range(SEGMENTS):
        owner = row_ref[id_ref[0, j]] // per_owner
        order = jnp.int32(0)
        for other in owners:
            order = order + (other == owner).astype(jnp.int32)
        owners.append(owner)
        here = column == lax.rem(me - owner + ways, ways) * cap + order
        first = jnp.where(here, start, first)
        start = start + counts_ref[0, j] * BLOCK
        last = jnp.where(here, start, last)
    position = lax.broadcasted_iota(jnp.int32, shape, 0)
    return jnp.logical_and(position >= first, position < last)


def rank_of(wide):
    row = lax.broadcasted_iota(jnp.int32, (RANK, wide), 0)
    column = lax.broadcasted_iota(jnp.int32, (RANK, wide), 1)
    return (lax.rem(column, RANK) == row).astype(jnp.bfloat16)


def low_parts(acts, downs, counts, ids, store_row, cap, per_owner, after=()):
    rows = acts.shape[0]
    ways = len(downs)
    wide = ways * cap * RANK

    def kernel(counts_ref, id_ref, row_ref, acts_ref, *refs):
        mask = slot_mask((rows, wide), counts_ref, id_ref, row_ref, ways, cap, per_owner)
        blocks = jnp.concatenate([ref[...] for ref in refs[:ways]], axis=0)
        part = lax.dot_general(
            acts_ref[...], blocks, (((1,), (1,)), ((), ())), preferred_element_type=jnp.float32
        )
        part = jnp.where(mask, part, 0.0).astype(jnp.bfloat16)
        refs[-1][...] = lax.dot_general(
            rank_of(wide), part, (((1,), (1,)), ((), ())), preferred_element_type=jnp.float32
        )

    return pl.pallas_call(
        kernel,
        in_specs=[SMEM] * 3 + [WHOLE] * (1 + ways) + [ANY] * len(after),
        out_specs=WHOLE,
        out_shape=jax.ShapeDtypeStruct((RANK, rows), jnp.float32),
        compiler_params=PARAMS,
        cost_estimate=CHEAP,
    )(counts, ids, store_row, acts, *downs, *after)


def spread(parts, counts, ids, store_row, ways, cap, per_owner):
    rows = parts[0].shape[1]
    wide = ways * cap * RANK

    def kernel(counts_ref, id_ref, row_ref, *refs):
        mask = slot_mask((rows, wide), counts_ref, id_ref, row_ref, ways, cap, per_owner)
        low = refs[0][...]
        for ref in refs[1:-1]:
            low = low + ref[...]
        low = lax.dot_general(
            low.astype(jnp.bfloat16), rank_of(wide), (((0,), (0,)), ((), ())), preferred_element_type=jnp.float32
        )
        refs[-1][...] = jnp.where(mask, low, 0.0).astype(jnp.bfloat16)

    return pl.pallas_call(
        kernel,
        in_specs=[SMEM] * 3 + [WHOLE] * len(parts),
        out_specs=WHOLE,
        out_shape=jax.ShapeDtypeStruct((rows, wide), jnp.bfloat16),
        compiler_params=PARAMS,
        cost_estimate=CHEAP,
    )(counts, ids, store_row, *parts)


def finish(out, bases, base_start, arrived, low, ups, start, width, full):
    rows, wide = low.shape
    tile = tile_of(start, width)
    first = start // tile
    ways = len(ups)
    depth = ups[0].shape[0]

    def kernel(*refs):
        out_ref = refs[-1]
        low_ref, up_refs = refs[0], refs[1 : 1 + ways]
        total = refs[1 + ways][...].astype(jnp.float32)
        for ref in refs[2 + ways : 2 + ways + len(arrived)]:
            total = total + ref[...].astype(jnp.float32)
        blocks = jnp.concatenate([ref[...] for ref in up_refs], axis=0)
        delta = jnp.dot(low_ref[...], blocks, preferred_element_type=jnp.float32)
        out_ref[...] = (total + adapter_scale * delta).astype(jnp.bfloat16)

    here = pl.BlockSpec((rows, tile), lambda j: (0, j))
    there = pl.BlockSpec((rows, tile), lambda j: (0, first + j))
    base_first = (start - base_start) // tile
    specs = [WHOLE]
    specs += [pl.BlockSpec((depth, tile), lambda j: (0, first + j))] * ways
    specs += [pl.BlockSpec((rows, tile), lambda j: (0, base_first + j))] + [here] * len(arrived)
    operands = [low, *ups, bases, *arrived]
    aliases = {}
    if out is not None:
        aliases = {len(operands): 0}
        operands.append(out)
        specs.append(ANY)
    return pl.pallas_call(
        kernel,
        grid=(width // tile,),
        in_specs=specs,
        out_specs=there,
        out_shape=jax.ShapeDtypeStruct((rows, full), jnp.bfloat16),
        input_output_aliases=aliases,
        compiler_params=PARAMS,
        cost_estimate=CHEAP,
    )(*operands)


def body(ways, chips, acts, weight, down, up, counts, ids, store_row):
    per_owner = down.shape[0]
    rows, depth = acts.shape
    block = weight.shape[1] // (chips * CORES)
    cap = SEGMENTS // ways + 1
    tensor = lax.axis_index("tensor")
    place = jnp.stack([tensor // CORES, lax.rem(tensor, CORES)]).astype(jnp.int32)

    def along_dp(array, shift):
        return lax.ppermute(array, "dp", [(i, (i + shift) % ways) for i in range(ways)])

    def to_core(array):
        return lax.ppermute(array, "tensor", [(i, i ^ 1) for i in range(chips * CORES)])

    def to_chip(array, shift):
        size = chips * CORES
        return lax.ppermute(array, "tensor", [(i, (i + CORES * shift) % size) for i in range(size)])

    mul = functools.partial(product, place, acts, weight, chips=chips)
    head, *tail = chunks_of(block)
    rest = block - head[1]

    all_ids = [ids] + [along_dp(ids, -s) for s in range(1, ways)]
    sent = mul(1, False, *head)
    crossed = to_core(sent)
    downs, ups = pick(all_ids, store_row, down, up, ways, cap, after=(sent,))
    far_downs = [downs[0]] + [along_dp(downs[s], s) for s in range(1, ways)]

    heads, tails, last = [], [], downs[0]
    for shift in range(1, chips):
        if shift > 1:
            crossed = to_core(mul(shift, False, *head, after=(last,)))
        last = mul(shift, True, *head, add=crossed, after=(last,))
        heads.append(to_chip(last, shift))
    for shift in range(1, chips) if tail else ():
        crossed, into = [], None
        for start, width in tail:
            last = mul(shift, False, start, width, after=(last,))
            crossed.append(to_core(last))
        for (start, width), add in zip(tail, crossed):
            into = mul(shift, True, start, width, add=add, after=(last,), into=into, total=rest, at=start - head[1])
            last = into
        tails.append(to_chip(into, shift))

    last = mul(0, False, 0, block, after=(last, *heads))
    crossed = to_core(last)
    low = low_parts(acts, far_downs, counts, ids, store_row, cap, per_owner, after=(last,))
    far_ups = [ups[0]]
    for s in range(1, ways):
        held, _ = lax.optimization_barrier((ups[s], far_downs[s]))
        far_ups.append(along_dp(held, s))
    chip_low = low + to_core(low)
    lows = [chip_low] + [to_chip(chip_low, shift) for shift in range(1, chips)]
    base = mul(0, True, 0, block, add=crossed, after=(chip_low,))
    low = spread(lows, counts, ids, store_row, ways, cap, per_owner)

    out = finish(None, base, 0, heads, low, far_ups, *head, block)
    if tail:
        out = finish(out, base, 0, tails, low, far_ups, head[1], rest, block)
    return out


def solution(mesh):
    in_specs = (
        P(("parts", "dp"), "tensor"),
        P("tensor", None),
        P("dp", None, "tensor"),
        P("dp", None, "tensor"),
        P(("parts", "dp"), None),
        P(("parts", "dp"), None),
        P("parts"),
    )
    out_specs = P(("parts", "dp"), "tensor")
    ways, chips = mesh.shape["dp"], mesh.shape["tensor"] // CORES
    return jax.shard_map(
        functools.partial(body, ways, chips), mesh=mesh, in_specs=in_specs, out_specs=out_specs, check_vma=False
    )
```

time: 234 us -> 133 us (0.57)
  Pallas kernels: 149 us -> 58.6 us
  blocking collectives: 25 us -> 0 us
  waiting for transfers between devices: 28.6 us -> 46 us
    pallas_call x1, Pallas kernels: 81.6 us -> 4.71 us  [pick(): pl.pallas_call(kernel, in_specs=[SMEM] * (ways + 1) + [ANY] * (2 + n_afte...]
    psum x1 -> x0, blocking collectives: 25 us -> none  [body(): lax.psum(low_parts(acts, far_downs, counts, ids, store_row, cap, per_owne...]
    ppermute x3, waiting for transfers between devices: 0.01 us -> 17.9 us  [to_chip(): lax.ppermute(array, 'tensor', [(i, (i + CORES * shift) % size) for i in r...]
    pallas_call x3 -> x2, Pallas kernels: 10.2 us -> 4.55 us  [finish(): pl.pallas_call(kernel, grid=(width // tile,), in_specs=specs, out_specs=t...]
    pallas_call x8, Pallas kernels: 51.2 us -> 45.7 us  [product(): pl.pallas_call(kernel, grid_spec=pltpu.PrefetchScalarGridSpec(num_scalar_...]
    ppermute x4 -> x5, waiting for transfers between devices: 5.78 us -> 1.27 us  [to_core(): lax.ppermute(array, 'tensor', [(i, i ^ 1) for i in range(chips * CORES)])]
    ppermute x9, waiting for transfers between devices: 22.8 us -> 26.8 us  [along_dp(): lax.ppermute(array, 'dp', [(i, (i + shift) % ways) for i in range(ways)])]
    pallas_call x2, Pallas kernels: 6.14 us -> 3.61 us  [the longest x1 2.53 us: low_parts(): pl.pallas_call(kernel, in_specs=[SMEM] * 3 + [WHOLE] * (1 + ways) + [ANY]...]
  transfers between devices with their start and end apart: 16 -> 17, of which waited for: 6 -> 8; matrix products, arithmetic and copies ran while one was open for 0% -> 0% of each run, Pallas kernels for 45% -> 25%
where the time goes in v2:
time: 133 us
  Pallas kernels  58.6 us (44%)
  waiting for transfers between devices  46 us (35%)
  starting transfers between devices  25.9 us (19%)
  local copies, waits for them, and re-layouts  1.98 us (1%)
    pallas_call x8, Pallas kernels, product(): pl.pallas_call(kernel, grid_spec=pltpu.PrefetchScalarGridSpec(num_scalar_...  45.7 us
    ppermute x9, waiting for transfers between devices, along_dp(): lax.ppermute(array, 'dp', [(i, (i + shift) % ways) for i in range(ways)])  26.8 us
    ppermute x9, starting transfers between devices, along_dp(): lax.ppermute(array, 'dp', [(i, (i + shift) % ways) for i in range(ways)])  21 us
    ppermute x3, waiting for transfers between devices, to_chip(): lax.ppermute(array, 'tensor', [(i, (i + CORES * shift) % size) for i in r...  17.9 us
    pallas_call x1, Pallas kernels, pick(): pl.pallas_call(kernel, in_specs=[SMEM] * (ways + 1) + [ANY] * (2 + n_afte...  4.71 us
    pallas_call x2, Pallas kernels, finish(): pl.pallas_call(kernel, grid=(width // tile,), in_specs=specs, out_specs=t...  4.55 us
    ppermute x3, starting transfers between devices, to_chip(): lax.ppermute(array, 'tensor', [(i, (i + CORES * shift) % size) for i in r...  3.64 us
  transfers between devices with their start and end apart: 17, of which 8 were waited for; matrix products, arithmetic and copies ran while one was open for 0% of the time, Pallas kernels for 25%

profile of v2, /device:TPU:0, one launch (start us, length us, event | category | flops | bytes accessed | tf_op | source)
XLA Modules:
  0.0 132.8 jit_solution(2185076402472074615)
XLA Ops:
  0.0 0.1 pad_add_fusion.refs_0_
  0.1 1.8 %copy-done = bf16[704,2048]{1,0:T(8,128)(2,1)S(1)} copy-done((bf16[704,2048]{1,0:T(8,128)(2,1)S(1)}, bf16[704,2048]{1,0:T(8,128)(2,1)}, u32[]{:S(2)}) %copy-start) | copy-done | bytes 2883608
  1.9 4.1 %shard_map.73.refs_7_ = bf16[704,512]{1,0:T(8,128)(2,1)S(1)} custom-call(s32[2]{0:T(128)S(1)} %pad_add_fusion.refs_0_, bf16[704,2048]{1,0:T(8,128)(2,1)S(1)} %copy-done, bf16[2048,8192]{1,0:T(8,128)(2,1)} %refs_2_.15), custom_call_target="tpu_custom_call" | custom-call | flops 1000 | bytes 1000 | tf_op jit(solution)/shard_map/pallas_call | solution.py:68
  6.0 0.0 copy-start.1
  6.0 0.5 collective-permute-start.6
  6.5 2.6 %collective-permute-start.2 = (s32[1,16]{1,0:T(1,128)S(1)}, s32[1,16]{1,0:T(1,128)S(1)}, u32[]{:S(2)}, u32[]{:S(2)}) collective-permute-start(s32[1,16]{1,0:T(1,128)S(1)} %copy-done.5), channel_id=1, source_target_pairs={{0,4},{4,8},{8,12},{12,0},{1,5},{5,9},{9,13},{13,1},{2,6},{6,10},{... | collective-permute-start | bytes 200 | tf_op jit(solution)/shard_map/ppermute | solution.py:256
  9.1 2.6 %collective-permute-start.1 = (s32[1,16]{1,0:T(1,128)S(1)}, s32[1,16]{1,0:T(1,128)S(1)}, u32[]{:S(2)}, u32[]{:S(2)}) collective-permute-start(s32[1,16]{1,0:T(1,128)S(1)} %copy-done.5), channel_id=1, source_target_pairs={{0,8},{4,12},{8,0},{12,4},{1,9},{5,13},{9,1},{13,5},{2,10},{6,14},... | collective-permute-start | bytes 200 | tf_op jit(solution)/shard_map/ppermute | solution.py:256
  11.7 1.3 %collective-permute-start = (s32[1,16]{1,0:T(1,128)S(1)}, s32[1,16]{1,0:T(1,128)S(1)}, u32[]{:S(2)}, u32[]{:S(2)}) collective-permute-start(s32[1,16]{1,0:T(1,128)S(1)} %copy-done.5), channel_id=1, source_target_pairs={{0,12},{4,0},{8,4},{12,8},{1,13},{5,1},{9,5},{13,9},{2,14},{6,2},{... | collective-permute-start | bytes 200 | tf_op jit(solution)/shard_map/ppermute | solution.py:256
  13.1 0.5 collective-permute-done.1.refs_2_
  13.6 1.7 %collective-permute-done.refs_1_ = s32[1,16]{1,0:T(1,128)S(1)} collective-permute-done((s32[1,16]{1,0:T(1,128)S(1)}, s32[1,16]{1,0:T(1,128)S(1)}, u32[]{:S(2)}, u32[]{:S(2)}) %collective-permute-start) | collective-permute-done | bytes 96 | tf_op jit(solution)/shard_map/ppermute | solution.py:256
  15.3 4.7 %shard_map.74 = (bf16[80,2048]{1,0:T(8,128)(2,1)S(1)}, bf16[80,2048]{1,0:T(8,128)(2,1)S(1)}, bf16[80,2048]{1,0:T(8,128)(2,1)S(1)}, bf16[80,2048]{1,0:T(8,128)(2,...) custom-call(s32[1,16]{1,0:T(1,128)S(1)} %copy-done.5, ...), custom_call_target="tpu_custom_call" | custom-call | flops 1000 | bytes 1000 | tf_op jit(solution)/shard_map/pallas_call | solution.py:119
  20.0 0.0 collective-permute-done.6.refs_3_
  20.0 3.8 %shard_map.75.refs_3_ = bf16[704,512]{1,0:T(8,128)(2,1)S(1)} custom-call(s32[2]{0:T(128)S(1)} %pad_add_fusion.refs_0_, bf16[704,2048]{1,0:T(8,128)(2,1)S(1)} %copy-done.1, bf16[2048,8192]{1,0:T(8,128)(2,1)} %refs_2_.15, bf16[704,512]{1,0:T(8,128)(2,1)S(1)} %collective-permute-done.6.refs_3_, bf16[80,2048]{1,0:T(8,128)(2,1)S(1)} %get-tuple-element.16.refs_4_.refs_0_), custom_call_target="tpu_custom_call" | custom-call | flops 1000 | bytes 1000 | tf_op jit(solution)/shard_map/pallas_call | solution.py:68
  23.8 4.9 %shard_map.76.refs_3_ = bf16[704,768]{1,0:T(8,128)(2,1)S(1)} custom-call(s32[2]{0:T(128)S(1)} %pad_add_fusion.refs_0_, bf16[704,2048]{1,0:T(8,128)(2,1)S(1)} %copy-done.1, bf16[2048,8192]{1,0:T(8,128)(2,1)} %refs_2_.15, bf16[704,512]{1,0:T(8,128)(2,1)S(1)} %shard_map.75.refs_3_), custom_call_target="tpu_custom_call" | custom-call | flops 1000 | bytes 1000 | tf_op jit(solution)/shard_map/pallas_call | solution.py:68
  28.7 0.1 collective-permute-start.8
  28.8 4.9 %shard_map.77.refs_4_ = bf16[704,768]{1,0:T(8,128)(2,1)S(1)} custom-call(s32[2]{0:T(128)S(1)} %pad_add_fusion.refs_0_, bf16[704,2048]{1,0:T(8,128)(2,1)S(1)} %copy-done.1, bf16[2048,8192]{1,0:T(8,128)(2,1)} %refs_2_.15, bf16[704,768]{1,0:T(8,128)(2,1)S(1)} %shard_map.76.refs_3_), custom_call_target="tpu_custom_call" | custom-call | flops 1000 | bytes 1000 | tf_op jit(solution)/shard_map/pallas_call | solution.py:68
  33.7 0.6 collective-permute-start.7
  34.2 1.5 %collective-permute-start.9 = (bf16[704,512]{1,0:T(8,128)(2,1)S(1)}, bf16[704,512]{1,0:T(8,128)(2,1)S(1)}, u32[]{:S(2)}, u32[]{:S(2)}) collective-permute-start(bf16[704,512]{1,0:T(8,128)(2,1)S(1)} %shard_map.75.refs_3_), channel_id=1, source_target_pairs={{0,2},{1,3},{2,0},{3,1},{4,6},{5,7},{6,4},{7,5},{8,10},{9,11},{10,... | collective-permute-start | bytes 2162696 | tf_op jit(solution)/shard_map/ppermute | solution.py:263
  35.7 4.9 %shard_map.78.refs_5_ = bf16[704,1536]{1,0:T(8,128)(2,1)S(1)} custom-call(s32[2]{0:T(128)S(1)} %pad_add_fusion.refs_0_, bf16[704,2048]{1,0:T(8,128)(2,1)S(1)} %copy-done.1, bf16[2048,8192]{1,0:T(8,128)(2,1)} %refs_2_.15, bf16[704,768]{1,0:T(8,128)(2,1)S(1)} %collective-permute-done.8.refs_3_, bf16[704,768]{1,0:T(8,128)(2,1)S(1)} %shard_map.77.refs_4_), custom_call_target="tpu_custom_call" | custom-call | flops 1000 | bytes 1000 | tf_op jit(solution)/shard_map/pallas_call | solution.py:68
  40.7 0.1 copy.10.refs_4_
  40.8 0.0 collective-permute-done.7.refs_3_
  40.8 4.9 %shard_map.79.refs_3_ = bf16[704,1536]{1,0:T(8,128)(2,1)S(1)} custom-call(s32[2]{0:T(128)S(1)} %pad_add_fusion.refs_0_, bf16[704,2048]{1,0:T(8,128)(2,1)S(1)} %copy-done.1, bf16[2048,8192]{1,0:T(8,128)(2,1)} %refs_2_.15, bf16[704,768]{1,0:T(8,128)(2,1)S(1)} %collective-permute-done.7.refs_3_, ...), custom_call_target="tpu_custom_call", output_to_operand_aliasing={{}: (4, {})} | custom-call | flops 1000 | bytes 1000 | tf_op jit(solution)/shard_map/pallas_call | solution.py:68
  45.8 0.0 copy-start.6
  45.8 6.6 %collective-permute-done.9.refs_4_.refs_6_ = bf16[704,512]{1,0:T(8,128)(2,1)S(1)} collective-permute-done((bf16[704,512]{1,0:T(8,128)(2,1)S(1)}, bf16[704,512]{1,0:T(8,128)(2,1)S(1)}, u32[]{:S(2)}, u32[]{:S(2)}) %collective-permute-start.9) | collective-permute-done | bytes 720928 | tf_op jit(solution)/shard_map/ppermute | solution.py:263
  52.4 9.0 %shard_map.80.refs_4_ = bf16[704,2048]{1,0:T(8,128)(2,1)S(1)} custom-call(s32[2]{0:T(128)S(1)} %pad_add_fusion.refs_0_, bf16[704,2048]{1,0:T(8,128)(2,1)S(1)} %copy-done.1, bf16[2048,8192]{1,0:T(8,128)(2,1)} %refs_2_.15, bf16[704,1536]{1,0:T(8,128)(2,1)S(1)} %shard_map.79.refs_3_, bf16[704,512]{1,0:T(8,128)(2,1)S(1)} %collective-permute-done.9.refs_4_.refs_6_), custom_call_target="tpu_custom_call" | custom-call | flops 1000 | bytes 1000 | tf_op jit(solution)/shard_map/pallas_call | solution.py:68
  61.4 0.1 collective-permute-start.15
  61.5 1.6 %collective-permute-start.16 = (bf16[704,1536]{1,0:T(8,128)(2,1)S(1)}, bf16[704,1536]{1,0:T(8,128)(2,1)S(1)}, u32[]{:S(2)}, u32[]{:S(2)}) collective-permute-start(bf16[704,1536]{1,0:T(8,128)(2,1)S(1)} %shard_map.79.refs_3_), channel_id=1, source_target_pairs={{0,2},{1,3},{2,0},{3,1},{4,6},{5,7},{6,4},{7,5},{8,10},{9,11},{10,... | collective-permute-start | bytes 6488072 | tf_op jit(solution)/shard_map/ppermute | solution.py:263
  63.1 0.2 collective-permute-start.3
  63.3 3.5 %collective-permute-start.4 = (bf16[80,2048]{1,0:T(8,128)(2,1)S(1)}, bf16[80,2048]{1,0:T(8,128)(2,1)S(1)}, u32[]{:S(2)}, u32[]{:S(2)}) collective-permute-start(bf16[80,2048]{1,0:T(8,128)(2,1)S(1)} %get-tuple-element.18), channel_id=1, source_target_pairs={{0,8},{4,12},{8,0},{12,4},{1,9},{5,13},{9,1},{13,5},{2,10},{6,14},... | collective-permute-start | bytes 983048 | tf_op jit(solution)/shard_map/ppermute | solution.py:256
  66.8 0.1 collective-permute-start.5
  66.9 8.7 %collective-permute-done.3.refs_1_ = bf16[80,2048]{1,0:T(8,128)(2,1)S(1)} collective-permute-done((bf16[80,2048]{1,0:T(8,128)(2,1)S(1)}, bf16[80,2048]{1,0:T(8,128)(2,1)S(1)}, u32[]{:S(2)}, u32[]{:S(2)}) %collective-permute-start.3) | collective-permute-done | bytes 327712 | tf_op jit(solution)/shard_map/ppermute | solution.py:256
  75.6 13.3 %collective-permute-done.4.refs_2_ = bf16[80,2048]{1,0:T(8,128)(2,1)S(1)} collective-permute-done((bf16[80,2048]{1,0:T(8,128)(2,1)S(1)}, bf16[80,2048]{1,0:T(8,128)(2,1)S(1)}, u32[]{:S(2)}, u32[]{:S(2)}) %collective-permute-start.4) | collective-permute-done | bytes 327712 | tf_op jit(solution)/shard_map/ppermute | solution.py:256
  88.8 0.0 collective-permute-done.5.refs_3_
  88.8 2.5 %shard_map.81 = f32[16,704]{1,0:T(8,128)S(1)} custom-call(s32[1,16]{1,0:T(1,128)S(1)} %copy-done.6, s32[1,16]{1,0:T(1,128)S(1)} %copy-done.5, s32[384]{0:T(512)S(1)} %copy-done.4, bf16[704,2048]{1,0:T(8,128)(2,1)S(1)} %copy-done.1, bf16[80,2048]{1,0:T(8,128)(2,1)S(1)} %get-tuple-element.16.refs_4_.refs_0_, ...), custom_call_target="tpu_custom_call" | custom-call | flops 1000 | bytes 1000 | tf_op jit(solution)/shard_map/pallas_call | solution.py:172
  91.4 0.0 collective-permute-start.10
  91.4 1.3 collective-permute-done.10
  92.6 0.6 collective-permute-start.11
  93.2 7.4 %collective-permute-start.12 = (bf16[80,2048]{1,0:T(8,128)(2,1)S(1)}, bf16[80,2048]{1,0:T(8,128)(2,1)S(1)}, u32[]{:S(2)}, u32[]{:S(2)}) collective-permute-start(bf16[80,2048]{1,0:T(8,128)(2,1)S(1)} %get-tuple-element.22), channel_id=1, source_target_pairs={{0,4},{4,8},{8,12},{12,0},{1,5},{5,9},{9,13},{13,1},{2,6},{6,10},{... | collective-permute-start | bytes 983048 | tf_op jit(solution)/shard_map/ppermute | solution.py:256
  100.6 0.1 collective-permute-start.13
  100.7 11.3 %collective-permute-done.11.refs_1_ = f32[16,704]{1,0:T(8,128)S(1)} collective-permute-done((f32[16,704]{1,0:T(8,128)S(1)}, f32[16,704]{1,0:T(8,128)S(1)}, u32[]{:S(2)}, u32[]{:S(2)}) %collective-permute-start.11) | collective-permute-done | bytes 45088 | tf_op jit(solution)/shard_map/ppermute | solution.py:263
  112.0 3.1 %collective-permute-start.14 = (bf16[80,2048]{1,0:T(8,128)(2,1)S(1)}, bf16[80,2048]{1,0:T(8,128)(2,1)S(1)}, u32[]{:S(2)}, u32[]{:S(2)}) collective-permute-start(bf16[80,2048]{1,0:T(8,128)(2,1)S(1)} %get-tuple-element.26), channel_id=1, source_target_pairs={{0,12},{4,0},{8,4},{12,8},{1,13},{5,1},{9,5},{13,9},{2,14},{6,2},{... | collective-permute-start | bytes 983048 | tf_op jit(solution)/shard_map/ppermute | solution.py:256
  115.2 1.1 shard_map.82.refs_0_
  116.2 0.0 collective-permute-done.15.refs_3_
  116.3 9.2 %shard_map.83.refs_5_ = bf16[704,2048]{1,0:T(8,128)(2,1)S(1)} custom-call(s32[2]{0:T(128)S(1)} %pad_add_fusion.refs_0_, bf16[704,2048]{1,0:T(8,128)(2,1)S(1)} %copy-done.1, bf16[2048,8192]{1,0:T(8,128)(2,1)} %refs_2_.15, bf16[704,2048]{1,0:T(8,128)(2,1)S(1)} %collective-permute-done.15.refs_3_, f32[16,704]{1,0:T(8,128)S(1)} %add.4.refs_0_.refs_4_), custom_call_target="tpu_custom_call" | custom-call | flops 1000 | bytes 1000 | tf_op jit(solution)/shard_map/pallas_call | solution.py:68
  125.5 0.0 collective-permute-done.12.refs_2_
  125.5 2.7 %collective-permute-done.14.refs_4_ = bf16[80,2048]{1,0:T(8,128)(2,1)S(1)} collective-permute-done((bf16[80,2048]{1,0:T(8,128)(2,1)S(1)}, bf16[80,2048]{1,0:T(8,128)(2,1)S(1)}, u32[]{:S(2)}, u32[]{:S(2)}) %collective-permute-start.14) | collective-permute-done | bytes 327712 | tf_op jit(solution)/shard_map/ppermute | solution.py:256
  128.2 1.4 %shard_map.84.refs_7_ = bf16[704,2048]{1,0:T(8,128)(2,1)} custom-call(bf16[704,320]{1,0:T(8,128)(2,1)S(1)} %shard_map.82.refs_0_, bf16[80,2048]{1,0:T(8,128)(2,1)S(1)} %get-tuple-element.20.refs_1_, bf16[80,2048]{1,0:T(8,128)(2,1)S(1)} %collective-permute-done.12.refs_2_, bf16[80,2048]{1,0:T(8,128)(2,1)S(1)} %collective-permute-done.13.refs_3_, ...), custom_call_target="tpu_custom_call" | custom-call | flops 1000 | bytes 1000 | tf_op jit(solution)/shard_map/pallas_call | solution.py:235
  129.6 3.1 %shard_map.85 = bf16[704,2048]{1,0:T(8,128)(2,1)} custom-call(bf16[704,320]{1,0:T(8,128)(2,1)S(1)} %shard_map.82.refs_0_, bf16[80,2048]{1,0:T(8,128)(2,1)S(1)} %get-tuple-element.20.refs_1_, bf16[80,2048]{1,0:T(8,128)(2,1)S(1)} %collective-permute-done.12.refs_2_, ...), custom_call_target="tpu_custom_call", output_to_operand_aliasing={{}: (7, {})} | custom-call | flops 1000 | bytes 1000 | tf_op jit(solution)/shard_map/pallas_call | solution.py:235
  (16 shorter events, 0.0 us)
Async XLA Ops:
  0.1 1.8 %copy-start = (bf16[704,2048]{1,0:T(8,128)(2,1)S(1)}, bf16[704,2048]{1,0:T(8,128)(2,1)}, u32[]{:S(2)}) copy-start(bf16[704,2048]{1,0:T(8,128)(2,1)} %refs_1_.15) | copy-start | bytes 8650756
  1.9 4.6 %copy-start.5 = (s32[1,16]{1,0:T(1,128)S(1)}, s32[1,16]{1,0:T(1,128)}, u32[]{:S(2)}) copy-start(s32[1,16]{1,0:T(1,128)} %id_ref.3) | copy-start | bytes 196
  1.9 13.4 %copy-start.2 = (bf16[96,16,2048]{2,1,0:T(8,128)(2,1)S(1)}, bf16[96,16,2048]{2,1,0:T(8,128)(2,1)}, u32[]{:S(2)}) copy-start(bf16[96,16,2048]{2,1,0:T(8,128)(2,1)} %refs_5_.1) | copy-start | bytes 18874372
  1.9 13.4 %copy-start.3 = (bf16[96,16,2048]{2,1,0:T(8,128)(2,1)S(1)}, bf16[96,16,2048]{2,1,0:T(8,128)(2,1)}, u32[]{:S(2)}) copy-start(bf16[96,16,2048]{2,1,0:T(8,128)(2,1)} %refs_6_.1) | copy-start | bytes 18874372
  1.9 13.4 %copy-start.4 = (s32[384]{0:T(512)S(1)}, s32[384]{0:T(512)}, u32[]{:S(2)}) copy-start(s32[384]{0:T(512)} %row_ref.3) | copy-start | bytes 4612
  6.0 14.1 %copy-start.1 = (bf16[704,2048]{1,0:T(8,128)(2,1)S(1)}, bf16[704,2048]{1,0:T(8,128)(2,1)}, u32[]{:S(2)}) copy-start(bf16[704,2048]{1,0:T(8,128)(2,1)} %refs_1_.15) | copy-start | bytes 8650756
  6.0 14.0 %collective-permute-start.6 = (bf16[704,512]{1,0:T(8,128)(2,1)S(1)}, bf16[704,512]{1,0:T(8,128)(2,1)S(1)}, u32[]{:S(2)}, u32[]{:S(2)}) collective-permute-start(bf16[704,512]{1,0:T(8,128)(2,1)S(1)} %shard_map.73.refs_7_), channel_id=1, source_target_pairs={{0,1},{1,0},{2,3},{3,2},{4,5},{5,4},{6,7},{7,6},{8,9},{9,8},{10,11... | collective-permute-start | bytes 2162696 | tf_op jit(solution)/shard_map/ppermute | solution.py:259
  6.5 6.6 %collective-permute-start.2 = (s32[1,16]{1,0:T(1,128)S(1)}, s32[1,16]{1,0:T(1,128)S(1)}, u32[]{:S(2)}, u32[]{:S(2)}) collective-permute-start(s32[1,16]{1,0:T(1,128)S(1)} %copy-done.5), channel_id=1, source_target_pairs={{0,4},{4,8},{8,12},{12,0},{1,5},{5,9},{9,13},{13,1},{2,6},{6,10},{... | collective-permute-start | bytes 200 | tf_op jit(solution)/shard_map/ppermute | solution.py:256
  9.1 4.4 %collective-permute-start.1 = (s32[1,16]{1,0:T(1,128)S(1)}, s32[1,16]{1,0:T(1,128)S(1)}, u32[]{:S(2)}, u32[]{:S(2)}) collective-permute-start(s32[1,16]{1,0:T(1,128)S(1)} %copy-done.5), channel_id=1, source_target_pairs={{0,8},{4,12},{8,0},{12,4},{1,9},{5,13},{9,1},{13,5},{2,10},{6,14},... | collective-permute-start | bytes 200 | tf_op jit(solution)/shard_map/ppermute | solution.py:256
  11.7 3.5 %collective-permute-start = (s32[1,16]{1,0:T(1,128)S(1)}, s32[1,16]{1,0:T(1,128)S(1)}, u32[]{:S(2)}, u32[]{:S(2)}) collective-permute-start(s32[1,16]{1,0:T(1,128)S(1)} %copy-done.5), channel_id=1, source_target_pairs={{0,12},{4,0},{8,4},{12,8},{1,13},{5,1},{9,5},{13,9},{2,14},{6,2},{... | collective-permute-start | bytes 200 | tf_op jit(solution)/shard_map/ppermute | solution.py:256
  28.7 7.0 %collective-permute-start.8 = (bf16[704,768]{1,0:T(8,128)(2,1)S(1)}, bf16[704,768]{1,0:T(8,128)(2,1)S(1)}, u32[]{:S(2)}, u32[]{:S(2)}) collective-permute-start(bf16[704,768]{1,0:T(8,128)(2,1)S(1)} %shard_map.76.refs_3_), channel_id=1, source_target_pairs={{0,1},{1,0},{2,3},{3,2},{4,5},{5,4},{6,7},{7,6},{8,9},{9,8},{10,11... | collective-permute-start | bytes 3244040 | tf_op jit(solution)/shard_map/ppermute | solution.py:259
  33.7 7.1 %collective-permute-start.7 = (bf16[704,768]{1,0:T(8,128)(2,1)S(1)}, bf16[704,768]{1,0:T(8,128)(2,1)S(1)}, u32[]{:S(2)}, u32[]{:S(2)}) collective-permute-start(bf16[704,768]{1,0:T(8,128)(2,1)S(1)} %shard_map.77.refs_4_), channel_id=1, source_target_pairs={{0,1},{1,0},{2,3},{3,2},{4,5},{5,4},{6,7},{7,6},{8,9},{9,8},{10,11... | collective-permute-start | bytes 3244040 | tf_op jit(solution)/shard_map/ppermute | solution.py:259
  34.2 18.1 %collective-permute-start.9 = (bf16[704,512]{1,0:T(8,128)(2,1)S(1)}, bf16[704,512]{1,0:T(8,128)(2,1)S(1)}, u32[]{:S(2)}, u32[]{:S(2)}) collective-permute-start(bf16[704,512]{1,0:T(8,128)(2,1)S(1)} %shard_map.75.refs_3_), channel_id=1, source_target_pairs={{0,2},{1,3},{2,0},{3,1},{4,6},{5,7},{6,4},{7,5},{8,10},{9,11},{10,... | collective-permute-start | bytes 2162696 | tf_op jit(solution)/shard_map/ppermute | solution.py:263
  45.8 43.1 %copy-start.6 = (s32[1,16]{1,0:T(1,128)S(1)}, s32[1,16]{1,0:T(1,128)}, u32[]{:S(2)}) copy-start(s32[1,16]{1,0:T(1,128)} %counts_ref.3) | copy-start | bytes 196
  61.4 54.8 %collective-permute-start.15 = (bf16[704,2048]{1,0:T(8,128)(2,1)S(1)}, bf16[704,2048]{1,0:T(8,128)(2,1)S(1)}, u32[]{:S(2)}, u32[]{:S(2)}) collective-permute-start(bf16[704,2048]{1,0:T(8,128)(2,1)S(1)} %shard_map.80.refs_4_), channel_id=1, source_target_pairs={{0,1},{1,0},{2,3},{3,2},{4,5},{5,4},{6,7},{7,6},{8,9},{9,8},{10,11... | collective-permute-start | bytes 8650760 | tf_op jit(solution)/shard_map/ppermute | solution.py:259
  61.5 68.1 %collective-permute-start.16 = (bf16[704,1536]{1,0:T(8,128)(2,1)S(1)}, bf16[704,1536]{1,0:T(8,128)(2,1)S(1)}, u32[]{:S(2)}, u32[]{:S(2)}) collective-permute-start(bf16[704,1536]{1,0:T(8,128)(2,1)S(1)} %shard_map.79.refs_3_), channel_id=1, source_target_pairs={{0,2},{1,3},{2,0},{3,1},{4,6},{5,7},{6,4},{7,5},{8,10},{9,11},{10,... | collective-permute-start | bytes 6488072 | tf_op jit(solution)/shard_map/ppermute | solution.py:263
  63.1 12.5 %collective-permute-start.3 = (bf16[80,2048]{1,0:T(8,128)(2,1)S(1)}, bf16[80,2048]{1,0:T(8,128)(2,1)S(1)}, u32[]{:S(2)}, u32[]{:S(2)}) collective-permute-start(bf16[80,2048]{1,0:T(8,128)(2,1)S(1)} %get-tuple-element.17), channel_id=1, source_target_pairs={{0,4},{4,8},{8,12},{12,0},{1,5},{5,9},{9,13},{13,1},{2,6},{6,10},{... | collective-permute-start | bytes 983048 | tf_op jit(solution)/shard_map/ppermute | solution.py:256
  63.3 25.5 %collective-permute-start.4 = (bf16[80,2048]{1,0:T(8,128)(2,1)S(1)}, bf16[80,2048]{1,0:T(8,128)(2,1)S(1)}, u32[]{:S(2)}, u32[]{:S(2)}) collective-permute-start(bf16[80,2048]{1,0:T(8,128)(2,1)S(1)} %get-tuple-element.18), channel_id=1, source_target_pairs={{0,8},{4,12},{8,0},{12,4},{1,9},{5,13},{9,1},{13,5},{2,10},{6,14},... | collective-permute-start | bytes 983048 | tf_op jit(solution)/shard_map/ppermute | solution.py:256
  66.8 22.1 %collective-permute-start.5 = (bf16[80,2048]{1,0:T(8,128)(2,1)S(1)}, bf16[80,2048]{1,0:T(8,128)(2,1)S(1)}, u32[]{:S(2)}, u32[]{:S(2)}) collective-permute-start(bf16[80,2048]{1,0:T(8,128)(2,1)S(1)} %get-tuple-element.19), channel_id=1, source_target_pairs={{0,12},{4,0},{8,4},{12,8},{1,13},{5,1},{9,5},{13,9},{2,14},{6,2},{... | collective-permute-start | bytes 983048 | tf_op jit(solution)/shard_map/ppermute | solution.py:256
  91.4 1.3 collective-permute-start.10
  92.6 19.4 %collective-permute-start.11 = (f32[16,704]{1,0:T(8,128)S(1)}, f32[16,704]{1,0:T(8,128)S(1)}, u32[]{:S(2)}, u32[]{:S(2)}) collective-permute-start(f32[16,704]{1,0:T(8,128)S(1)} %add.4.refs_0_.refs_4_), channel_id=1, source_target_pairs={{0,2},{1,3},{2,0},{3,1},{4,6},{5,7},{6,4},{7,5},{8,10},{9,11},{10,... | collective-permute-start | bytes 135176 | tf_op jit(solution)/shard_map/ppermute | solution.py:263
  93.2 32.3 %collective-permute-start.12 = (bf16[80,2048]{1,0:T(8,128)(2,1)S(1)}, bf16[80,2048]{1,0:T(8,128)(2,1)S(1)}, u32[]{:S(2)}, u32[]{:S(2)}) collective-permute-start(bf16[80,2048]{1,0:T(8,128)(2,1)S(1)} %get-tuple-element.22), channel_id=1, source_target_pairs={{0,4},{4,8},{8,12},{12,0},{1,5},{5,9},{9,13},{13,1},{2,6},{6,10},{... | collective-permute-start | bytes 983048 | tf_op jit(solution)/shard_map/ppermute | solution.py:256
  100.6 24.9 %collective-permute-start.13 = (bf16[80,2048]{1,0:T(8,128)(2,1)S(1)}, bf16[80,2048]{1,0:T(8,128)(2,1)S(1)}, u32[]{:S(2)}, u32[]{:S(2)}) collective-permute-start(bf16[80,2048]{1,0:T(8,128)(2,1)S(1)} %get-tuple-element.24), channel_id=1, source_target_pairs={{0,8},{4,12},{8,0},{12,4},{1,9},{5,13},{9,1},{13,5},{2,10},{6,14},... | collective-permute-start | bytes 983048 | tf_op jit(solution)/shard_map/ppermute | solution.py:256
  112.0 16.2 %collective-permute-start.14 = (bf16[80,2048]{1,0:T(8,128)(2,1)S(1)}, bf16[80,2048]{1,0:T(8,128)(2,1)S(1)}, u32[]{:S(2)}, u32[]{:S(2)}) collective-permute-start(bf16[80,2048]{1,0:T(8,128)(2,1)S(1)} %get-tuple-element.26), channel_id=1, source_target_pairs={{0,12},{4,0},{8,4},{12,8},{1,13},{5,1},{9,5},{13,9},{2,14},{6,2},{... | collective-permute-start | bytes 983048 | tf_op jit(solution)/shard_map/ppermute | solution.py:256

commit v3 on v2

--- a/solution.py
+++ b/solution.py
@@ -14,27 +14,31 @@
 CORES = 2
 LANES = 128
 adapter_scale = 0.5
-VMEM_LIMIT = 20 * 1024 * 1024
+VMEM_LIMIT = 42 * 1024 * 1024
 
 ANY = pl.BlockSpec(memory_space=pl.ANY)
+HBM = pl.BlockSpec(memory_space=pltpu.HBM)
 SMEM = pl.BlockSpec(memory_space=pltpu.SMEM)
 WHOLE = pl.BlockSpec(memory_space=pltpu.VMEM)
 CHEAP = pl.CostEstimate(flops=1000, bytes_accessed=1000, transcendentals=0)
+
+def weigh(us):
+    return pl.CostEstimate(flops=int(us * 1.1e9) + 1000, bytes_accessed=1000, transcendentals=0)
 PARAMS = pltpu.CompilerParams(vmem_limit_bytes=VMEM_LIMIT)
 
 
 def chunks_of(width):
     if width % 2048:
-        return [(0, width)]
-    unit = width // 8
-    return [(0, 2 * unit), (2 * unit, 3 * unit), (5 * unit, 3 * unit)]
+        return (0, width), None
+    half = 1024
+    return (0, half), (half, width - half)
 
 
 def tile_of(start, width):
-    return next(t for t in (512, 384, 256, 128) if start % t == 0 and width % t == 0)
-
-
-def product(place, acts, weight, shift, same_core, start, width, chips, add=None, after=(), into=None, total=None, at=0):
+    return next(t for t in (512, 256, 128) if start % t == 0 and width % t == 0)
+
+
+def product(place, acts, weight, shift, same_core, start, width, chips, add=None, after=(), into=None, total=None, at=0, weight_of=CHEAP):
     rows, depth = acts.shape
     block = weight.shape[1] // (chips * CORES)
     tile = tile_of(math.gcd(start, at), width)
@@ -76,7 +80,7 @@
         out_shape=jax.ShapeDtypeStruct((rows, total or width), jnp.bfloat16),
         input_output_aliases=aliases,
         compiler_params=PARAMS,
-        cost_estimate=CHEAP,
+        cost_estimate=weight_of,
     )(place, *operands)
 
 
@@ -118,7 +122,7 @@
     shape = jax.ShapeDtypeStruct((cap * rank, width), jnp.bfloat16)
     outs = pl.pallas_call(
         kernel,
-        in_specs=[SMEM] * (ways + 1) + [ANY] * (2 + n_after),
+        in_specs=[SMEM] * (ways + 1) + [HBM] * 2 + [ANY] * n_after,
         out_specs=[WHOLE] * (2 * ways),
         out_shape=[shape] * (2 * ways),
         scratch_shapes=[pltpu.SMEM((ways * (cap + 1),), jnp.int32), pltpu.SemaphoreType.DMA((2 * ways,))],
@@ -175,7 +179,7 @@
         out_specs=WHOLE,
         out_shape=jax.ShapeDtypeStruct((RANK, rows), jnp.float32),
         compiler_params=PARAMS,
-        cost_estimate=CHEAP,
+        cost_estimate=weigh(3),
     )(counts, ids, store_row, acts, *downs, *after)
 
 
@@ -199,7 +203,7 @@
         out_specs=WHOLE,
         out_shape=jax.ShapeDtypeStruct((rows, wide), jnp.bfloat16),
         compiler_params=PARAMS,
-        cost_estimate=CHEAP,
+        cost_estimate=weigh(1),
     )(counts, ids, store_row, *parts)
 
 
@@ -240,8 +244,13 @@
         out_shape=jax.ShapeDtypeStruct((rows, full), jnp.bfloat16),
         input_output_aliases=aliases,
         compiler_params=PARAMS,
-        cost_estimate=CHEAP,
+        cost_estimate=weigh(8 if out is None else 1),
     )(*operands)
+
+
+def apart(live, function, *operands):
+    shapes = jax.eval_shape(function, *operands)
+    return lax.cond(live, function, lambda *_: jax.tree.map(lambda t: jnp.zeros(t.shape, t.dtype), shapes), *operands)
 
 
 def body(ways, chips, acts, weight, down, up, counts, ids, store_row):
@@ -263,8 +272,7 @@
         return lax.ppermute(array, "tensor", [(i, (i + CORES * shift) % size) for i in range(size)])
 
     mul = functools.partial(product, place, acts, weight, chips=chips)
-    head, *tail = chunks_of(block)
-    rest = block - head[1]
+    head, tail = chunks_of(block)
 
     all_ids = [ids] + [along_dp(ids, -s) for s in range(1, ways)]
     sent = mul(1, False, *head)
@@ -278,31 +286,38 @@
             crossed = to_core(mul(shift, False, *head, after=(last,)))
         last = mul(shift, True, *head, add=crossed, after=(last,))
         heads.append(to_chip(last, shift))
+
+    live = counts[0, 0] >= 0
+
+    def sums(acts, weight, place, last, shift, own):
+        mul = functools.partial(product, place, acts, weight, chips=chips)
+        last = mul(shift, False, *tail, after=(last,))
+        crossed = to_core(last)
+        if own:
+            last = mul(0, False, 0, block, after=(last,))
+            own_crossed = to_core(lax.optimization_barrier((last, crossed))[0])
+        summed = mul(shift, True, *tail, add=crossed, after=(last,))
+        return (summed, own_crossed) if own else (summed,)
+
     for shift in range(1, chips) if tail else ():
-        crossed, into = [], None
-        for start, width in tail:
-            last = mul(shift, False, start, width, after=(last,))
-            crossed.append(to_core(last))
-        for (start, width), add in zip(tail, crossed):
-            into = mul(shift, True, start, width, add=add, after=(last,), into=into, total=rest, at=start - head[1])
-            last = into
-        tails.append(to_chip(into, shift))
-
-    last = mul(0, False, 0, block, after=(last, *heads))
-    crossed = to_core(last)
-    low = low_parts(acts, far_downs, counts, ids, store_row, cap, per_owner, after=(last,))
+        own = shift == chips - 1
+        last, *others = apart(live, functools.partial(sums, shift=shift, own=own), acts, weight, place, last)
+        tails.append(to_chip(last, shift))
+    own_crossed = others[0] if tail else to_core(mul(0, False, 0, block, after=(last,)))
+
+    low = low_parts(acts, far_downs, counts, ids, store_row, cap, per_owner, after=(last, *heads))
     far_ups = [ups[0]]
     for s in range(1, ways):
-        held, _ = lax.optimization_barrier((ups[s], far_downs[s]))
+        held, _, _ = lax.optimization_barrier((ups[s], far_downs[s], last))
         far_ups.append(along_dp(held, s))
     chip_low = low + to_core(low)
     lows = [chip_low] + [to_chip(chip_low, shift) for shift in range(1, chips)]
-    base = mul(0, True, 0, block, add=crossed, after=(chip_low,))
+    base = mul(0, True, 0, block, add=own_crossed, after=(chip_low,), weight_of=weigh(0))
     low = spread(lows, counts, ids, store_row, ways, cap, per_owner)
 
     out = finish(None, base, 0, heads, low, far_ups, *head, block)
     if tail:
-        out = finish(out, base, 0, tails, low, far_ups, head[1], rest, block)
+        out = finish(out, base, 0, tails, low, far_ups, *tail, block)
     return out
 
 

time: 133 us -> 99.3 us (0.75)
  waiting for transfers between devices: 46 us -> 13.2 us
  local copies, waits for them, and re-layouts: 1.98 us -> 0.03 us
  starting transfers between devices: 25.9 us -> 27.8 us
    ppermute x9, waiting for transfers between devices: 26.8 us -> 6.66 us  [along_dp(): lax.ppermute(array, 'dp', [(i, (i + shift) % ways) for i in range(ways)])]
    ppermute x3, waiting for transfers between devices: 17.9 us -> 5.27 us  [to_chip(): lax.ppermute(array, 'tensor', [(i, (i + CORES * shift) % size) for i in r...]
    ppermute x9, starting transfers between devices: 21 us -> 24.5 us  [along_dp(): lax.ppermute(array, 'dp', [(i, (i + shift) % ways) for i in range(ways)])]
    pallas_call x8 -> x6, Pallas kernels: 45.7 us -> 43.3 us  [product(): pl.pallas_call(kernel, grid_spec=pltpu.PrefetchScalarGridSpec(num_scalar_...]
    unnamed x15 -> x14, local copies, waits for them, and re-layouts: 1.98 us -> 0.03 us
    ppermute x3, starting transfers between devices: 3.64 us -> 2.09 us  [to_chip(): lax.ppermute(array, 'tensor', [(i, (i + CORES * shift) % size) for i in r...]
    pallas_call x1, Pallas kernels: 2.53 us -> 3.96 us  [low_parts(): pl.pallas_call(kernel, in_specs=[SMEM] * 3 + [WHOLE] * (1 + ways) + [ANY]...]
  transfers between devices with their start and end apart: 17 -> 16, of which waited for: 8 -> 6; matrix products, arithmetic and copies ran while one was open for 0% -> 0% of each run, Pallas kernels for 25% -> 43%
where the time goes in v3:
time: 99.3 us; the launch traced here: 99 us
  Pallas kernels  57.7 us (58%)
  starting transfers between devices  27.8 us (28%)
  waiting for transfers between devices  13.2 us (13%)
    pallas_call x6, Pallas kernels, product(): pl.pallas_call(kernel, grid_spec=pltpu.PrefetchScalarGridSpec(num_scalar_...  43.3 us
    ppermute x9, starting transfers between devices, along_dp(): lax.ppermute(array, 'dp', [(i, (i + shift) % ways) for i in range(ways)])  24.5 us
    ppermute x9, waiting for transfers between devices, along_dp(): lax.ppermute(array, 'dp', [(i, (i + shift) % ways) for i in range(ways)])  6.66 us
    ppermute x3, waiting for transfers between devices, to_chip(): lax.ppermute(array, 'tensor', [(i, (i + CORES * shift) % size) for i in r...  5.27 us
    pallas_call x1, Pallas kernels, pick(): pl.pallas_call(kernel, in_specs=[SMEM] * (ways + 1) + [HBM] * 2 + [ANY] *...  4.87 us
    pallas_call x2, Pallas kernels, finish(): pl.pallas_call(kernel, grid=(width // tile,), in_specs=specs, out_specs=t...  4.55 us
    pallas_call x1, Pallas kernels, low_parts(): pl.pallas_call(kernel, in_specs=[SMEM] * 3 + [WHOLE] * (1 + ways) + [ANY]...  3.96 us
    ppermute x3, starting transfers between devices, to_chip(): lax.ppermute(array, 'tensor', [(i, (i + CORES * shift) % size) for i in r...  2.09 us
  transfers between devices with their start and end apart: 16, of which 6 were waited for; matrix products, arithmetic and copies ran while one was open for 0% of the time, Pallas kernels for 43%

profile of v3, /device:TPU:0, one launch (start us, length us, event | category | flops | bytes accessed | tf_op | source)
XLA Modules:
  0.0 99.0 jit_solution(11286723673909353295)
XLA Ops:
  0.0 0.1 pad_add_fusion.refs_0_
  0.1 6.8 %shard_map.73.refs_7_ = bf16[704,1024]{1,0:T(8,128)(2,1)S(1)} custom-call(s32[2]{0:T(128)S(1)} %pad_add_fusion.refs_0_, bf16[704,2048]{1,0:T(8,128)(2,1)} %refs_1_.5, bf16[2048,8192]{1,0:T(8,128)(2,1)} %refs_2_.5), custom_call_target="tpu_custom_call" | custom-call | flops 1000 | bytes 1000 | tf_op jit(solution)/shard_map/pallas_call | solution.py:72
  6.9 0.0 copy-start.3
  6.9 0.5 collective-permute-start.8
  7.4 4.7 %collective-permute-start.2 = (s32[1,16]{1,0:T(1,128)S(1)}, s32[1,16]{1,0:T(1,128)S(1)}, u32[]{:S(2)}, u32[]{:S(2)}) collective-permute-start(s32[1,16]{1,0:T(1,128)S(1)} %copy-done.1), channel_id=1, source_target_pairs={{0,12},{4,0},{8,4},{12,8},{1,13},{5,1},{9,5},{13,9},{2,14},{6,2},{... | collective-permute-start | bytes 200 | tf_op jit(solution)/shard_map/ppermute | solution.py:265
  12.1 0.0 collective-permute-start.3
  12.1 1.0 %collective-permute-start.4 = (s32[1,16]{1,0:T(1,128)S(1)}, s32[1,16]{1,0:T(1,128)S(1)}, u32[]{:S(2)}, u32[]{:S(2)}) collective-permute-start(s32[1,16]{1,0:T(1,128)S(1)} %copy-done.1), channel_id=1, source_target_pairs={{0,4},{4,8},{8,12},{12,0},{1,5},{5,9},{9,13},{13,1},{2,6},{6,10},{... | collective-permute-start | bytes 200 | tf_op jit(solution)/shard_map/ppermute | solution.py:265
  13.1 0.3 collective-permute-done.2.refs_1_
  13.4 3.1 %collective-permute-done.3.refs_2_ = s32[1,16]{1,0:T(1,128)S(1)} collective-permute-done((s32[1,16]{1,0:T(1,128)S(1)}, s32[1,16]{1,0:T(1,128)S(1)}, u32[]{:S(2)}, u32[]{:S(2)}) %collective-permute-start.3) | collective-permute-done | bytes 96 | tf_op jit(solution)/shard_map/ppermute | solution.py:265
  16.5 0.9 collective-permute-done.4.refs_3_
  17.4 0.0 slice-done.1
  17.4 4.9 %shard_map.74 = (bf16[80,2048]{1,0:T(8,128)(2,1)S(1)}, bf16[80,2048]{1,0:T(8,128)(2,1)S(1)}, bf16[80,2048]{1,0:T(8,128)(2,1)}, bf16[80,2048]{1,0:T(8,128)(2,1)},...) custom-call(s32[1,16]{1,0:T(1,128)S(1)} %copy-done.1, ...), custom_call_target="tpu_custom_call" | custom-call | flops 1000 | bytes 1000 | tf_op jit(solution)/shard_map/pallas_call | solution.py:123
  22.3 0.0 collective-permute-done.8.refs_3_
  22.3 0.0 copy-start.2
  22.3 6.3 %shard_map.75 = bf16[704,1024]{1,0:T(8,128)(2,1)} custom-call(s32[2]{0:T(128)S(1)} %pad_add_fusion.refs_0_, bf16[704,2048]{1,0:T(8,128)(2,1)S(1)} %copy-done.3, bf16[2048,8192]{1,0:T(8,128)(2,1)} %refs_2_.5, bf16[704,1024]{1,0:T(8,128)(2,1)S(1)} %collective-permute-done.8.refs_3_, bf16[80,2048]{1,0:T(8,128)(2,1)S(1)} %get-tuple-element.31.refs_4_.refs_0_), custom_call_target="tpu_custom_call" | custom-call | flops 1000 | bytes 1000 | tf_op jit(solution)/shard_map/pallas_call | solution.py:72
  28.7 1.5 %collective-permute-start.9 = (bf16[704,1024]{1,0:T(8,128)(2,1)}, bf16[704,1024]{1,0:T(8,128)(2,1)S(1)}, u32[]{:S(2)}, u32[]{:S(2)}) collective-permute-start(bf16[704,1024]{1,0:T(8,128)(2,1)} %shard_map.75), channel_id=1, source_target_pairs={{0,2},{1,3},{2,0},{3,1},{4,6},{5,7},{6,4},{7,5},{8,10},{9,11},{10,... | collective-permute-start | bytes 4325384 | tf_op jit(solution)/shard_map/ppermute | solution.py:272
  30.2 0.6 collective-permute-start.7
  30.7 0.6 collective-permute-start.6
  31.3 2.0 %collective-permute-start.5 = (bf16[80,2048]{1,0:T(8,128)(2,1)S(1)}, bf16[80,2048]{1,0:T(8,128)(2,1)}, u32[]{:S(2)}, u32[]{:S(2)}) collective-permute-start(bf16[80,2048]{1,0:T(8,128)(2,1)S(1)} %get-tuple-element.32), channel_id=1, source_target_pairs={{0,4},{4,8},{8,12},{12,0},{1,5},{5,9},{9,13},{13,1},{2,6},{6,10},{... | collective-permute-start | bytes 983048 | tf_op jit(solution)/shard_map/ppermute | solution.py:265
  33.4 21.6 %conditional.1 = (bf16[704,1024]{1,0:T(8,128)(2,1)}, bf16[704,2048]{1,0:T(8,128)(2,1)}) conditional(s32[]{:T(128)} %bitcast.2, () %tuple.17, (s32[2]{0:T(128)S(1)}, bf16[704,2048]{1,0:T(8,128)(2,1)S(1)}, bf16[2048,8192]{1,0:T(8,128)(2,1)}, bf16[704,1024]{1,0:T(8,128)(2,1)}) %tuple.24), branch_computations={%region_0.1_spmd, %region_1.2_spmd} | conditional | flops 3000 | bytes 17304600 | solution.py:253
  33.4 5.6 %branch_1_fun.3.refs_3_ = bf16[704,1024]{1,0:T(8,128)(2,1)S(1)} custom-call(s32[2]{0:T(128)S(1)} %get-tuple-element.13.refs_0_, bf16[704,2048]{1,0:T(8,128)(2,1)S(1)} %get-tuple-element.14.refs_1_, bf16[2048,8192]{1,0:T(8,128)(2,1)} %get-tuple-element.15.refs_2_, bf16[704,1024]{1,0:T(8,128)(2,1)} %get-tuple-element.16.refs_3_), custom_call_target="tpu_custom_call" | custom-call | flops 1000 | bytes 1000 | tf_op jit(solution)/shard_map/cond/branch_1_fun/pallas_call | solution.py:72
  39.0 0.1 collective-permute-start
  39.1 9.0 %branch_1_fun.4.refs_4_ = bf16[704,2048]{1,0:T(8,128)(2,1)S(1)} custom-call(s32[2]{0:T(128)S(1)} %get-tuple-element.13.refs_0_, bf16[704,2048]{1,0:T(8,128)(2,1)S(1)} %get-tuple-element.14.refs_1_, bf16[2048,8192]{1,0:T(8,128)(2,1)} %get-tuple-element.15.refs_2_, bf16[704,1024]{1,0:T(8,128)(2,1)S(1)} %branch_1_fun.3.refs_3_), custom_call_target="tpu_custom_call" | custom-call | flops 1000 | bytes 1000 | tf_op jit(solution)/shard_map/cond/branch_1_fun/pallas_call | solution.py:72
  48.0 0.0 collective-permute-done.refs_3_
  48.0 0.6 collective-permute-start.1
  48.6 6.4 %branch_1_fun.5 = bf16[704,1024]{1,0:T(8,128)(2,1)} custom-call(s32[2]{0:T(128)S(1)} %get-tuple-element.13.refs_0_, bf16[704,2048]{1,0:T(8,128)(2,1)S(1)} %get-tuple-element.14.refs_1_, bf16[2048,8192]{1,0:T(8,128)(2,1)} %get-tuple-element.15.refs_2_, bf16[704,1024]{1,0:T(8,128)(2,1)S(1)} %collective-permute-done.refs_3_, ...), custom_call_target="tpu_custom_call" | custom-call | flops 1000 | bytes 1000 | tf_op jit(solution)/shard_map/cond/branch_1_fun/pallas_call | solution.py:72
  55.0 0.0 collective-permute-done.1
  55.0 0.5 collective-permute-start.15
  55.5 0.0 collective-permute-done.7.refs_3_
  55.5 1.8 %collective-permute-start.14 = (bf16[80,2048]{1,0:T(8,128)(2,1)S(1)}, bf16[80,2048]{1,0:T(8,128)(2,1)S(1)}, u32[]{:S(2)}, u32[]{:S(2)}) collective-permute-start(bf16[80,2048]{1,0:T(8,128)(2,1)S(1)} %get-tuple-element.42), channel_id=1, source_target_pairs={{0,12},{4,0},{8,4},{12,8},{1,13},{5,1},{9,5},{13,9},{2,14},{6,2},{... | collective-permute-start | bytes 983048 | tf_op jit(solution)/shard_map/ppermute | solution.py:265
  57.3 2.3 %collective-permute-done.6.refs_2_ = bf16[80,2048]{1,0:T(8,128)(2,1)} collective-permute-done((bf16[80,2048]{1,0:T(8,128)(2,1)}, bf16[80,2048]{1,0:T(8,128)(2,1)}, u32[]{:S(2)}, u32[]{:S(2)}) %collective-permute-start.6) | collective-permute-done | bytes 327712 | tf_op jit(solution)/shard_map/ppermute | solution.py:265
  59.6 0.0 collective-permute-start.13
  59.6 0.0 collective-permute-done.5.refs_1_
  59.7 13.9 %collective-permute-start.12 = (bf16[80,2048]{1,0:T(8,128)(2,1)S(1)}, bf16[80,2048]{1,0:T(8,128)(2,1)S(1)}, u32[]{:S(2)}, u32[]{:S(2)}) collective-permute-start(bf16[80,2048]{1,0:T(8,128)(2,1)S(1)} %get-tuple-element.38), channel_id=1, source_target_pairs={{0,4},{4,8},{8,12},{12,0},{1,5},{5,9},{9,13},{13,1},{2,6},{6,10},{... | collective-permute-start | bytes 983048 | tf_op jit(solution)/shard_map/ppermute | solution.py:265
  73.5 0.0 collective-permute-done.9.refs_5_.refs_6_
  73.5 4.0 %shard_map.76 = f32[16,704]{1,0:T(8,128)S(1)} custom-call(s32[1,16]{1,0:T(1,128)S(1)} %copy-done.2, s32[1,16]{1,0:T(1,128)S(1)} %copy-done.1, s32[384]{0:T(512)S(1)} %copy-done, bf16[704,2048]{1,0:T(8,128)(2,1)} %refs_1_.5, bf16[80,2048]{1,0:T(8,128)(2,1)S(1)} %get-tuple-element.31.refs_4_.refs_0_, bf16[80,2048]{1,0:T(8,128)(2,1)} %collective-permute-done.5.refs_1_, ...), custom_call_target="tpu_custom_call" | custom-call | flops 3300001024 | bytes 1000 | tf_op jit(solution)/shard_map/pallas_call | solution.py:176
  77.5 0.0 collective-permute-start.10
  77.5 1.2 %collective-permute-done.10 = f32[16,704]{1,0:T(8,128)S(1)} collective-permute-done((f32[16,704]{1,0:T(8,128)S(1)}, f32[16,704]{1,0:T(8,128)S(1)}, u32[]{:S(2)}, u32[]{:S(2)}) %collective-permute-start.10) | collective-permute-done | bytes 45088 | tf_op jit(solution)/shard_map/ppermute | solution.py:268
  78.8 0.1 collective-permute-start.11
  78.8 9.2 %shard_map.78.refs_5_ = bf16[704,2048]{1,0:T(8,128)(2,1)S(1)} custom-call(s32[2]{0:T(128)S(1)} %pad_add_fusion.refs_0_, bf16[704,2048]{1,0:T(8,128)(2,1)S(1)} %copy-done.4, bf16[2048,8192]{1,0:T(8,128)(2,1)} %refs_2_.5, bf16[704,2048]{1,0:T(8,128)(2,1)} %get-tuple-element.43.refs_3_, f32[16,704]{1,0:T(8,128)S(1)} %add.4.refs_0_.refs_4_), custom_call_target="tpu_custom_call" | custom-call | flops 1000 | bytes 1000 | tf_op jit(solution)/shard_map/pallas_call | solution.py:72
  88.1 5.3 %collective-permute-done.11.refs_1_ = f32[16,704]{1,0:T(8,128)S(1)} collective-permute-done((f32[16,704]{1,0:T(8,128)S(1)}, f32[16,704]{1,0:T(8,128)S(1)}, u32[]{:S(2)}, u32[]{:S(2)}) %collective-permute-start.11) | collective-permute-done | bytes 45088 | tf_op jit(solution)/shard_map/ppermute | solution.py:272
  93.3 1.1 %shard_map.77.refs_0_ = bf16[704,320]{1,0:T(8,128)(2,1)S(1)} custom-call(s32[1,16]{1,0:T(1,128)S(1)} %copy-done.2, s32[1,16]{1,0:T(1,128)S(1)} %copy-done.1, s32[384]{0:T(512)S(1)} %copy-done, f32[16,704]{1,0:T(8,128)S(1)} %add.4.refs_0_.refs_4_, f32[16,704]{1,0:T(8,128)S(1)} %collective-permute-done.11.refs_1_), custom_call_target="tpu_custom_call" | custom-call | flops 1100001024 | bytes 1000 | tf_op jit(solution)/shard_map/pallas_call | solution.py:200
  94.4 0.0 collective-permute-done.14.refs_4_
  94.4 0.0 collective-permute-done.13.refs_3_
  94.5 0.0 collective-permute-done.12.refs_2_
  94.5 2.3 %shard_map.79.refs_7_ = bf16[704,2048]{1,0:T(8,128)(2,1)} custom-call(bf16[704,320]{1,0:T(8,128)(2,1)S(1)} %shard_map.77.refs_0_, bf16[80,2048]{1,0:T(8,128)(2,1)S(1)} %get-tuple-element.36.refs_1_, bf16[80,2048]{1,0:T(8,128)(2,1)S(1)} %collective-permute-done.12.refs_2_, bf16[80,2048]{1,0:T(8,128)(2,1)S(1)} %collective-permute-done.13.refs_3_, ...), custom_call_target="tpu_custom_call" | custom-call | flops 8800001024 | bytes 1000 | tf_op jit(solution)/shard_map/pallas_call | solution.py:239
  96.7 0.0 collective-permute-done.15.refs_6_
  96.7 2.3 %shard_map.80 = bf16[704,2048]{1,0:T(8,128)(2,1)} custom-call(bf16[704,320]{1,0:T(8,128)(2,1)S(1)} %shard_map.77.refs_0_, bf16[80,2048]{1,0:T(8,128)(2,1)S(1)} %get-tuple-element.36.refs_1_, bf16[80,2048]{1,0:T(8,128)(2,1)S(1)} %collective-permute-done.12.refs_2_, ...), custom_call_target="tpu_custom_call", output_to_operand_aliasing={{}: (7, {})} | custom-call | flops 1100001024 | bytes 1000 | tf_op jit(solution)/shard_map/pallas_call | solution.py:239
  (13 shorter events, 0.0 us)
Async XLA Ops:
  0.0 17.4 %slice-start = ((s8[6291456]{0:T(1024)(128)(4,1)}), s8[4194304]{0:T(1024)(128)(4,1)S(1)}, s32[]{:S(2)}) async-start(s8[6291456]{0:T(1024)(128)(4,1)} %bitcast.4), calls=%async_computation | async-start | bytes 8388608
  0.1 7.3 %copy-start.1 = (s32[1,16]{1,0:T(1,128)S(1)}, s32[1,16]{1,0:T(1,128)}, u32[]{:S(2)}) copy-start(s32[1,16]{1,0:T(1,128)} %id_ref.3) | copy-start | bytes 196
  0.1 17.3 %slice-start.1 = ((s8[6291456]{0:T(1024)(128)(4,1)}), s8[2097152]{0:T(1024)(128)(4,1)S(1)}, s32[]{:S(2)}) async-start(s8[6291456]{0:T(1024)(128)(4,1)} %bitcast.4), calls=%async_computation.1 | async-start | bytes 4194304
  0.1 17.3 %copy-start = (s32[384]{0:T(512)S(1)}, s32[384]{0:T(512)}, u32[]{:S(2)}) copy-start(s32[384]{0:T(512)} %row_ref.3) | copy-start | bytes 4612
  6.9 15.5 %copy-start.3 = (bf16[704,2048]{1,0:T(8,128)(2,1)S(1)}, bf16[704,2048]{1,0:T(8,128)(2,1)}, u32[]{:S(2)}) copy-start(bf16[704,2048]{1,0:T(8,128)(2,1)} %refs_1_.5) | copy-start | bytes 8650756
  6.9 15.4 %collective-permute-start.8 = (bf16[704,1024]{1,0:T(8,128)(2,1)S(1)}, bf16[704,1024]{1,0:T(8,128)(2,1)S(1)}, u32[]{:S(2)}, u32[]{:S(2)}) collective-permute-start(bf16[704,1024]{1,0:T(8,128)(2,1)S(1)} %shard_map.73.refs_7_), channel_id=1, source_target_pairs={{0,1},{1,0},{2,3},{3,2},{4,5},{5,4},{6,7},{7,6},{8,9},{9,8},{10,11... | collective-permute-start | bytes 4325384 | tf_op jit(solution)/shard_map/ppermute | solution.py:268
  7.4 6.0 %collective-permute-start.2 = (s32[1,16]{1,0:T(1,128)S(1)}, s32[1,16]{1,0:T(1,128)S(1)}, u32[]{:S(2)}, u32[]{:S(2)}) collective-permute-start(s32[1,16]{1,0:T(1,128)S(1)} %copy-done.1), channel_id=1, source_target_pairs={{0,12},{4,0},{8,4},{12,8},{1,13},{5,1},{9,5},{13,9},{2,14},{6,2},{... | collective-permute-start | bytes 200 | tf_op jit(solution)/shard_map/ppermute | solution.py:265
  12.1 4.4 %collective-permute-start.3 = (s32[1,16]{1,0:T(1,128)S(1)}, s32[1,16]{1,0:T(1,128)S(1)}, u32[]{:S(2)}, u32[]{:S(2)}) collective-permute-start(s32[1,16]{1,0:T(1,128)S(1)} %copy-done.1), channel_id=1, source_target_pairs={{0,8},{4,12},{8,0},{12,4},{1,9},{5,13},{9,1},{13,5},{2,10},{6,14},... | collective-permute-start | bytes 200 | tf_op jit(solution)/shard_map/ppermute | solution.py:265
  12.1 5.3 %collective-permute-start.4 = (s32[1,16]{1,0:T(1,128)S(1)}, s32[1,16]{1,0:T(1,128)S(1)}, u32[]{:S(2)}, u32[]{:S(2)}) collective-permute-start(s32[1,16]{1,0:T(1,128)S(1)} %copy-done.1), channel_id=1, source_target_pairs={{0,4},{4,8},{8,12},{12,0},{1,5},{5,9},{9,13},{13,1},{2,6},{6,10},{... | collective-permute-start | bytes 200 | tf_op jit(solution)/shard_map/ppermute | solution.py:265
  22.3 11.0 %copy-start.2 = (s32[1,16]{1,0:T(1,128)S(1)}, s32[1,16]{1,0:T(1,128)}, u32[]{:S(2)}) copy-start(s32[1,16]{1,0:T(1,128)} %counts_ref.3) | copy-start | bytes 196
  28.7 44.8 %collective-permute-start.9 = (bf16[704,1024]{1,0:T(8,128)(2,1)}, bf16[704,1024]{1,0:T(8,128)(2,1)S(1)}, u32[]{:S(2)}, u32[]{:S(2)}) collective-permute-start(bf16[704,1024]{1,0:T(8,128)(2,1)} %shard_map.75), channel_id=1, source_target_pairs={{0,2},{1,3},{2,0},{3,1},{4,6},{5,7},{6,4},{7,5},{8,10},{9,11},{10,... | collective-permute-start | bytes 4325384 | tf_op jit(solution)/shard_map/ppermute | solution.py:272
  30.2 25.3 %collective-permute-start.7 = (bf16[80,2048]{1,0:T(8,128)(2,1)}, bf16[80,2048]{1,0:T(8,128)(2,1)}, u32[]{:S(2)}, u32[]{:S(2)}) collective-permute-start(bf16[80,2048]{1,0:T(8,128)(2,1)} %get-tuple-element.34), channel_id=1, source_target_pairs={{0,12},{4,0},{8,4},{12,8},{1,13},{5,1},{9,5},{13,9},{2,14},{6,2},{... | collective-permute-start | bytes 983048 | tf_op jit(solution)/shard_map/ppermute | solution.py:265
  30.7 28.9 %collective-permute-start.6 = (bf16[80,2048]{1,0:T(8,128)(2,1)}, bf16[80,2048]{1,0:T(8,128)(2,1)}, u32[]{:S(2)}, u32[]{:S(2)}) collective-permute-start(bf16[80,2048]{1,0:T(8,128)(2,1)} %get-tuple-element.33), channel_id=1, source_target_pairs={{0,8},{4,12},{8,0},{12,4},{1,9},{5,13},{9,1},{13,5},{2,10},{6,14},... | collective-permute-start | bytes 983048 | tf_op jit(solution)/shard_map/ppermute | solution.py:265
  31.3 28.3 %collective-permute-start.5 = (bf16[80,2048]{1,0:T(8,128)(2,1)S(1)}, bf16[80,2048]{1,0:T(8,128)(2,1)}, u32[]{:S(2)}, u32[]{:S(2)}) collective-permute-start(bf16[80,2048]{1,0:T(8,128)(2,1)S(1)} %get-tuple-element.32), channel_id=1, source_target_pairs={{0,4},{4,8},{8,12},{12,0},{1,5},{5,9},{9,13},{13,1},{2,6},{6,10},{... | collective-permute-start | bytes 983048 | tf_op jit(solution)/shard_map/ppermute | solution.py:265
  39.0 9.1 %collective-permute-start = (bf16[704,1024]{1,0:T(8,128)(2,1)S(1)}, bf16[704,1024]{1,0:T(8,128)(2,1)S(1)}, u32[]{:S(2)}, u32[]{:S(2)}) collective-permute-start(bf16[704,1024]{1,0:T(8,128)(2,1)S(1)} %branch_1_fun.3.refs_3_), channel_id=1, source_target_pairs={{0,1},{1,0},{2,3},{3,2},{4,5},{5,4},{6,7},{7,6},{8,9},{9,8},{10,11... | collective-permute-start | bytes 4325384 | tf_op jit(solution)/shard_map/cond/branch_1_fun/ppermute | solution.py:268
  48.0 6.9 %collective-permute-start.1 = (bf16[704,2048]{1,0:T(8,128)(2,1)S(1)}, bf16[704,2048]{1,0:T(8,128)(2,1)}, u32[]{:S(2)}, u32[]{:S(2)}) collective-permute-start(bf16[704,2048]{1,0:T(8,128)(2,1)S(1)} %branch_1_fun.4.refs_4_), channel_id=1, source_target_pairs={{0,1},{1,0},{2,3},{3,2},{4,5},{5,4},{6,7},{7,6},{8,9},{9,8},{10,11... | collective-permute-start | bytes 8650760 | tf_op jit(solution)/shard_map/cond/branch_1_fun/ppermute | solution.py:268
  55.0 41.8 %collective-permute-start.15 = (bf16[704,1024]{1,0:T(8,128)(2,1)}, bf16[704,1024]{1,0:T(8,128)(2,1)S(1)}, u32[]{:S(2)}, u32[]{:S(2)}) collective-permute-start(bf16[704,1024]{1,0:T(8,128)(2,1)} %get-tuple-element.35.refs_4_), channel_id=1, source_target_pairs={{0,2},{1,3},{2,0},{3,1},{4,6},{5,7},{6,4},{7,5},{8,10},{9,11},{10,... | collective-permute-start | bytes 4325384 | tf_op jit(solution)/shard_map/ppermute | solution.py:272
  55.5 38.9 %collective-permute-start.14 = (bf16[80,2048]{1,0:T(8,128)(2,1)S(1)}, bf16[80,2048]{1,0:T(8,128)(2,1)S(1)}, u32[]{:S(2)}, u32[]{:S(2)}) collective-permute-start(bf16[80,2048]{1,0:T(8,128)(2,1)S(1)} %get-tuple-element.42), channel_id=1, source_target_pairs={{0,12},{4,0},{8,4},{12,8},{1,13},{5,1},{9,5},{13,9},{2,14},{6,2},{... | collective-permute-start | bytes 983048 | tf_op jit(solution)/shard_map/ppermute | solution.py:265
  59.6 34.8 %collective-permute-start.13 = (bf16[80,2048]{1,0:T(8,128)(2,1)S(1)}, bf16[80,2048]{1,0:T(8,128)(2,1)S(1)}, u32[]{:S(2)}, u32[]{:S(2)}) collective-permute-start(bf16[80,2048]{1,0:T(8,128)(2,1)S(1)} %get-tuple-element.40), channel_id=1, source_target_pairs={{0,8},{4,12},{8,0},{12,4},{1,9},{5,13},{9,1},{13,5},{2,10},{6,14},... | collective-permute-start | bytes 983048 | tf_op jit(solution)/shard_map/ppermute | solution.py:265
  59.7 19.2 %copy-start.4 = (bf16[704,2048]{1,0:T(8,128)(2,1)S(1)}, bf16[704,2048]{1,0:T(8,128)(2,1)}, u32[]{:S(2)}) copy-start(bf16[704,2048]{1,0:T(8,128)(2,1)} %refs_1_.5) | copy-start | bytes 8650756
  59.7 34.8 %collective-permute-start.12 = (bf16[80,2048]{1,0:T(8,128)(2,1)S(1)}, bf16[80,2048]{1,0:T(8,128)(2,1)S(1)}, u32[]{:S(2)}, u32[]{:S(2)}) collective-permute-start(bf16[80,2048]{1,0:T(8,128)(2,1)S(1)} %get-tuple-element.38), channel_id=1, source_target_pairs={{0,4},{4,8},{8,12},{12,0},{1,5},{5,9},{9,13},{13,1},{2,6},{6,10},{... | collective-permute-start | bytes 983048 | tf_op jit(solution)/shard_map/ppermute | solution.py:265
  77.5 1.3 %collective-permute-start.10 = (f32[16,704]{1,0:T(8,128)S(1)}, f32[16,704]{1,0:T(8,128)S(1)}, u32[]{:S(2)}, u32[]{:S(2)}) collective-permute-start(f32[16,704]{1,0:T(8,128)S(1)} %shard_map.76), channel_id=1, source_target_pairs={{0,1},{1,0},{2,3},{3,2},{4,5},{5,4},{6,7},{7,6},{8,9},{9,8},{10,11... | collective-permute-start | bytes 135176 | tf_op jit(solution)/shard_map/ppermute | solution.py:268
  78.8 14.6 %collective-permute-start.11 = (f32[16,704]{1,0:T(8,128)S(1)}, f32[16,704]{1,0:T(8,128)S(1)}, u32[]{:S(2)}, u32[]{:S(2)}) collective-permute-start(f32[16,704]{1,0:T(8,128)S(1)} %add.4.refs_0_.refs_4_), channel_id=1, source_target_pairs={{0,2},{1,3},{2,0},{3,1},{4,6},{5,7},{6,4},{7,5},{8,10},{9,11},{10,... | collective-permute-start | bytes 135176 | tf_op jit(solution)/shard_map/ppermute | solution.py:272

commit v4 on v3

--- a/solution.py
+++ b/solution.py
@@ -84,37 +84,31 @@
     )(place, *operands)
 
 
-def pick(ids, store_row, down, up, ways, cap, after=()):
-    per_owner, rank, width = down.shape
-    n_after = len(after)
+def pick(ids, store_row, stores, ways, cap, after=()):
+    per_owner, rank, width = stores[0].shape
+    n_after, n_stores = len(after), len(stores)
 
     def kernel(*refs):
         id_refs, row_ref = refs[:ways], refs[ways]
-        stores = refs[ways + 1 : ways + 3]
-        outs = refs[ways + 3 + n_after : -2]
-        slots, sems = refs[-2:]
+        store_refs = refs[ways + 1 : ways + 1 + n_stores]
+        outs, sems = refs[ways + 1 + n_stores + n_after : -1], refs[-1]
         me = lax.axis_index("dp")
         for s in range(ways):
-            for k in range(cap + 1):
-                slots[s * (cap + 1) + k] = 0
-            used = jnp.int32(0)
+            used, chosen = jnp.int32(0), [jnp.int32(0)] * cap
             for j in range(SEGMENTS):
-                row = row_ref[id_refs[s][0, j]]
-                local = row - me * per_owner
+                local = row_ref[id_refs[s][0, j]] - me * per_owner
                 mine = jnp.logical_and(local >= 0, local < per_owner)
-                place = s * (cap + 1) + jnp.where(mine, jnp.minimum(used, cap), cap)
-                slots[place] = jnp.where(mine, local, 0)
+                for k in range(min(cap, j + 1)):
+                    chosen[k] = jnp.where(jnp.logical_and(mine, used == k), local, chosen[k])
                 used = used + mine.astype(jnp.int32)
-        for which in range(2):
-            for s in range(ways):
-                out = outs[which * ways + s]
+            for which in range(n_stores):
                 for k in range(cap):
                     pltpu.make_async_copy(
-                        stores[which].at[slots[s * (cap + 1) + k]],
-                        out.at[pl.ds(k * rank, rank)],
+                        store_refs[which].at[chosen[k]],
+                        outs[which * ways + s].at[pl.ds(k * rank, rank)],
                         sems.at[which * ways + s],
                     ).start()
-        for which in range(2):
+        for which in range(n_stores):
             for s in range(ways):
                 out = outs[which * ways + s]
                 pltpu.make_async_copy(out, out, sems.at[which * ways + s]).wait()
@@ -122,14 +116,14 @@
     shape = jax.ShapeDtypeStruct((cap * rank, width), jnp.bfloat16)
     outs = pl.pallas_call(
         kernel,
-        in_specs=[SMEM] * (ways + 1) + [HBM] * 2 + [ANY] * n_after,
-        out_specs=[WHOLE] * (2 * ways),
-        out_shape=[shape] * (2 * ways),
-        scratch_shapes=[pltpu.SMEM((ways * (cap + 1),), jnp.int32), pltpu.SemaphoreType.DMA((2 * ways,))],
+        in_specs=[SMEM] * (ways + 1) + [HBM] * n_stores + [ANY] * n_after,
+        out_specs=[WHOLE] * (n_stores * ways),
+        out_shape=[shape] * (n_stores * ways),
+        scratch_shapes=[pltpu.SemaphoreType.DMA((n_stores * ways,))],
         compiler_params=PARAMS,
         cost_estimate=CHEAP,
-    )(*ids, store_row, down, up, *after)
-    return outs[:ways], outs[ways:]
+    )(*ids, store_row, *stores, *after)
+    return outs
 
 
 def slot_mask(shape, counts_ref, id_ref, row_ref, ways, cap, per_owner):
@@ -179,73 +173,66 @@
         out_specs=WHOLE,
         out_shape=jax.ShapeDtypeStruct((RANK, rows), jnp.float32),
         compiler_params=PARAMS,
-        cost_estimate=weigh(3),
+        cost_estimate=weigh(20),
     )(counts, ids, store_row, acts, *downs, *after)
 
 
-def spread(parts, counts, ids, store_row, ways, cap, per_owner):
-    rows = parts[0].shape[1]
-    wide = ways * cap * RANK
+def finish(lows, ups, base, sends, counts, ids, store_row, cap, per_owner):
+    rows, block = base.shape
+    ways, depth = len(ups), ups[0].shape[0]
+    wide = ways * depth
+    tile = math.gcd(*[send[0].shape[1] for send in sends], 512)
+    n_low = len(lows)
 
     def kernel(counts_ref, id_ref, row_ref, *refs):
-        mask = slot_mask((rows, wide), counts_ref, id_ref, row_ref, ways, cap, per_owner)
-        low = refs[0][...]
-        for ref in refs[1:-1]:
-            low = low + ref[...]
-        low = lax.dot_general(
-            low.astype(jnp.bfloat16), rank_of(wide), (((0,), (0,)), ((), ())), preferred_element_type=jnp.float32
-        )
-        refs[-1][...] = jnp.where(mask, low, 0.0).astype(jnp.bfloat16)
-
+        low_refs, up_refs = refs[:n_low], refs[n_low : n_low + ways][::-1]
+        base_ref, *sent_refs = refs[n_low + ways : -2]
+        out_ref, low_ref = refs[-2:]
+        step = pl.program_id(0)
+
+        @pl.when(step == 0)
+        def _():
+            mask = slot_mask((rows, wide), counts_ref, id_ref, row_ref, ways, cap, per_owner)
+            low = low_refs[0][...]
+            for ref in low_refs[1:]:
+                low = low + ref[...]
+            low = lax.dot_general(
+                low.astype(jnp.bfloat16), rank_of(wide), (((0,), (0,)), ((), ())), preferred_element_type=jnp.float32
+            )
+            low_ref[...] = jnp.where(mask, low, 0.0).astype(jnp.bfloat16)
+
+        def write(arrived):
+            blocks = jnp.concatenate([ref[...] for ref in up_refs], axis=0)
+            delta = jnp.dot(low_ref[...], blocks, preferred_element_type=jnp.float32)
+            total = base_ref[...].astype(jnp.float32)
+            for ref in arrived:
+                total = total + ref[...].astype(jnp.float32)
+            out_ref[...] = (total + adapter_scale * delta).astype(jnp.bfloat16)
+
+        first, at = 0, 0
+        for send in sends:
+            steps, arrived = send[0].shape[1] // tile, sent_refs[at : at + len(send)]
+            pl.when(jnp.logical_and(step >= first, step < first + steps))(functools.partial(write, arrived))
+            first, at = first + steps, at + len(send)
+
+    here = pl.BlockSpec((rows, tile), lambda j: (0, j))
+    specs = [SMEM] * 3 + [WHOLE] * n_low + [pl.BlockSpec((depth, tile), lambda j: (0, j))] * ways + [here]
+    first = 0
+    for send in sends:
+        steps = send[0].shape[1] // tile
+        index = lambda j, first=first, steps=steps: (0, jnp.clip(j - first, 0, steps - 1))
+        specs += [pl.BlockSpec((rows, tile), index)] * len(send)
+        first += steps
     return pl.pallas_call(
         kernel,
-        in_specs=[SMEM] * 3 + [WHOLE] * len(parts),
-        out_specs=WHOLE,
-        out_shape=jax.ShapeDtypeStruct((rows, wide), jnp.bfloat16),
+        grid=(block // tile,),
+        in_specs=specs,
+        out_specs=here,
+        out_shape=jax.ShapeDtypeStruct((rows, block), jnp.bfloat16),
+        scratch_shapes=[pltpu.VMEM((rows, wide), jnp.bfloat16)],
         compiler_params=PARAMS,
-        cost_estimate=weigh(1),
-    )(counts, ids, store_row, *parts)
-
-
-def finish(out, bases, base_start, arrived, low, ups, start, width, full):
-    rows, wide = low.shape
-    tile = tile_of(start, width)
-    first = start // tile
-    ways = len(ups)
-    depth = ups[0].shape[0]
-
-    def kernel(*refs):
-        out_ref = refs[-1]
-        low_ref, up_refs = refs[0], refs[1 : 1 + ways]
-        total = refs[1 + ways][...].astype(jnp.float32)
-        for ref in refs[2 + ways : 2 + ways + len(arrived)]:
-            total = total + ref[...].astype(jnp.float32)
-        blocks = jnp.concatenate([ref[...] for ref in up_refs], axis=0)
-        delta = jnp.dot(low_ref[...], blocks, preferred_element_type=jnp.float32)
-        out_ref[...] = (total + adapter_scale * delta).astype(jnp.bfloat16)
-
-    here = pl.BlockSpec((rows, tile), lambda j: (0, j))
-    there = pl.BlockSpec((rows, tile), lambda j: (0, first + j))
-    base_first = (start - base_start) // tile
-    specs = [WHOLE]
-    specs += [pl.BlockSpec((depth, tile), lambda j: (0, first + j))] * ways
-    specs += [pl.BlockSpec((rows, tile), lambda j: (0, base_first + j))] + [here] * len(arrived)
-    operands = [low, *ups, bases, *arrived]
-    aliases = {}
-    if out is not None:
-        aliases = {len(operands): 0}
-        operands.append(out)
-        specs.append(ANY)
-    return pl.pallas_call(
-        kernel,
-        grid=(width // tile,),
-        in_specs=specs,
-        out_specs=there,
-        out_shape=jax.ShapeDtypeStruct((rows, full), jnp.bfloat16),
-        input_output_aliases=aliases,
-        compiler_params=PARAMS,
-        cost_estimate=weigh(8 if out is None else 1),
-    )(*operands)
+        cost_estimate=CHEAP,
+    )(counts, ids, store_row, *lows, *ups[::-1], base, *[array for send in sends for array in send])
 
 
 def apart(live, function, *operands):
@@ -277,15 +264,15 @@
     all_ids = [ids] + [along_dp(ids, -s) for s in range(1, ways)]
     sent = mul(1, False, *head)
     crossed = to_core(sent)
-    downs, ups = pick(all_ids, store_row, down, up, ways, cap, after=(sent,))
-    far_downs = [downs[0]] + [along_dp(downs[s], s) for s in range(1, ways)]
-
-    heads, tails, last = [], [], downs[0]
+    heads, tails, last = [], [], sent
     for shift in range(1, chips):
         if shift > 1:
             crossed = to_core(mul(shift, False, *head, after=(last,)))
-        last = mul(shift, True, *head, add=crossed, after=(last,))
+        last = mul(shift, True, *head, add=crossed)
         heads.append(to_chip(last, shift))
+    downs = pick(all_ids, store_row, [down], ways, cap, after=(last,))
+    far_downs = [downs[0]] + [along_dp(downs[s], s) for s in range(1, ways)]
+    last = downs[0]
 
     live = counts[0, 0] >= 0
 
@@ -306,19 +293,16 @@
     own_crossed = others[0] if tail else to_core(mul(0, False, 0, block, after=(last,)))
 
     low = low_parts(acts, far_downs, counts, ids, store_row, cap, per_owner, after=(last, *heads))
+    ups = pick(all_ids, store_row, [up], ways, cap, after=(last,))
     far_ups = [ups[0]]
     for s in range(1, ways):
-        held, _, _ = lax.optimization_barrier((ups[s], far_downs[s], last))
+        held, *_ = lax.optimization_barrier((ups[s], last, far_downs[s]))
         far_ups.append(along_dp(held, s))
     chip_low = low + to_core(low)
     lows = [chip_low] + [to_chip(chip_low, shift) for shift in range(1, chips)]
     base = mul(0, True, 0, block, add=own_crossed, after=(chip_low,), weight_of=weigh(0))
-    low = spread(lows, counts, ids, store_row, ways, cap, per_owner)
-
-    out = finish(None, base, 0, heads, low, far_ups, *head, block)
-    if tail:
-        out = finish(out, base, 0, tails, low, far_ups, *tail, block)
-    return out
+    sends = [heads, tails] if tail else [heads]
+    return finish(lows, far_ups, base, sends, counts, ids, store_row, cap, per_owner)
 
 
 def solution(mesh):

time: 99.3 us -> 97.2 us (0.979); the launches traced: 99 us -> 95.5 us
  starting transfers between devices: 27.8 us -> 20.9 us
  local copies, waits for them, and re-layouts: 0.03 us -> 2.82 us
  waiting for transfers between devices: 13.2 us -> 14.4 us
    ppermute x9, starting transfers between devices: 24.5 us -> 14.7 us  [along_dp(): lax.ppermute(array, 'dp', [(i, (i + shift) % ways) for i in range(ways)])]
    ppermute x3, starting transfers between devices: 2.09 us -> 5 us  [to_chip(): lax.ppermute(array, 'tensor', [(i, (i + CORES * shift) % size) for i in r...]
    ppermute x4, waiting for transfers between devices: 1.25 us -> 4.11 us  [to_core(): lax.ppermute(array, 'tensor', [(i, i ^ 1) for i in range(chips * CORES)])]
    unnamed x14 -> x16, local copies, waits for them, and re-layouts: 0.03 us -> 2.82 us
    ppermute x3, waiting for transfers between devices: 5.27 us -> 3.21 us  [to_chip(): lax.ppermute(array, 'tensor', [(i, (i + CORES * shift) % size) for i in r...]
    pallas_call x4 -> x3, Pallas kernels: 10.5 us -> 11.6 us  [the longest x2 6.59 us: pick(): pl.pallas_call(kernel, in_specs=[SMEM] * (ways + 1) + [HBM] * n_stores +...]
  transfers between devices with their start and end apart: 16 -> 16, of which waited for: 6 -> 7; matrix products, arithmetic and copies ran while one was open for 0% -> 0% of each run, Pallas kernels for 43% -> 42%
where the time goes in v4:
time: 97.2 us; the launch traced here: 95.5 us
  Pallas kernels  57.1 us (59%)
  starting transfers between devices  20.9 us (22%)
  waiting for transfers between devices  14.4 us (15%)
  local copies, waits for them, and re-layouts  2.82 us (3%)
    pallas_call x6, Pallas kernels, product(): pl.pallas_call(kernel, grid_spec=pltpu.PrefetchScalarGridSpec(num_scalar_...  42.4 us
    ppermute x9, starting transfers between devices, along_dp(): lax.ppermute(array, 'dp', [(i, (i + shift) % ways) for i in range(ways)])  14.7 us
    ppermute x9, waiting for transfers between devices, along_dp(): lax.ppermute(array, 'dp', [(i, (i + shift) % ways) for i in range(ways)])  7.03 us
    pallas_call x2, Pallas kernels, pick(): pl.pallas_call(kernel, in_specs=[SMEM] * (ways + 1) + [HBM] * n_stores +...  6.59 us
    ppermute x3, starting transfers between devices, to_chip(): lax.ppermute(array, 'tensor', [(i, (i + CORES * shift) % size) for i in r...  5 us
    pallas_call x1, Pallas kernels, finish(): pl.pallas_call(kernel, grid=(block // tile,), in_specs=specs, out_specs=h...  4.96 us
    ppermute x4, waiting for transfers between devices, to_core(): lax.ppermute(array, 'tensor', [(i, i ^ 1) for i in range(chips * CORES)])  4.11 us
    ppermute x3, waiting for transfers between devices, to_chip(): lax.ppermute(array, 'tensor', [(i, (i + CORES * shift) % size) for i in r...  3.21 us
  transfers between devices with their start and end apart: 16, of which 7 were waited for; matrix products, arithmetic and copies ran while one was open for 0% of the time, Pallas kernels for 42%

profile of v4, /device:TPU:0, one launch (start us, length us, event | category | flops | bytes accessed | tf_op | source)
XLA Modules:
  0.0 95.5 jit_solution(15348440881902552905)
XLA Ops:
  0.0 0.1 pad_add_fusion.refs_0_
  0.1 6.7 %shard_map.73 = bf16[704,1024]{1,0:T(8,128)(2,1)S(1)} custom-call(s32[2]{0:T(128)S(1)} %pad_add_fusion.refs_0_, bf16[704,2048]{1,0:T(8,128)(2,1)} %refs_1_.5, bf16[2048,8192]{1,0:T(8,128)(2,1)} %refs_2_.5), custom_call_target="tpu_custom_call" | custom-call | flops 1000 | bytes 1000 | tf_op jit(solution)/shard_map/pallas_call | solution.py:72
  6.8 0.0 copy-start.2
  6.8 0.0 slice-start.1
  6.8 0.0 copy-start.1
  6.8 0.5 collective-permute-start.5
  7.4 2.8 %collective-permute-done.5.refs_3_ = bf16[704,1024]{1,0:T(8,128)(2,1)S(1)} collective-permute-done((bf16[704,1024]{1,0:T(8,128)(2,1)S(1)}, bf16[704,1024]{1,0:T(8,128)(2,1)S(1)}, u32[]{:S(2)}, u32[]{:S(2)}) %collective-permute-start.5) | collective-permute-done | bytes 1441824 | tf_op jit(solution)/shard_map/ppermute | solution.py:255
  10.2 5.6 %shard_map.74.refs_6_ = bf16[704,1024]{1,0:T(8,128)(2,1)S(1)} custom-call(s32[2]{0:T(128)S(1)} %pad_add_fusion.refs_0_, bf16[704,2048]{1,0:T(8,128)(2,1)S(1)} %copy-done.4, bf16[2048,8192]{1,0:T(8,128)(2,1)} %refs_2_.5, bf16[704,1024]{1,0:T(8,128)(2,1)S(1)} %collective-permute-done.5.refs_3_), custom_call_target="tpu_custom_call" | custom-call | flops 1000 | bytes 1000 | tf_op jit(solution)/shard_map/pallas_call | solution.py:72
  15.8 0.0 copy-start.3
  15.8 2.9 %collective-permute-start.9 = (bf16[704,1024]{1,0:T(8,128)(2,1)S(1)}, bf16[704,1024]{1,0:T(8,128)(2,1)S(1)}, u32[]{:S(2)}, u32[]{:S(2)}) collective-permute-start(bf16[704,1024]{1,0:T(8,128)(2,1)S(1)} %shard_map.74.refs_6_), channel_id=1, source_target_pairs={{0,2},{1,3},{2,0},{3,1},{4,6},{5,7},{6,4},{7,5},{8,10},{9,11},{10,... | collective-permute-start | bytes 4325384 | tf_op jit(solution)/shard_map/ppermute | solution.py:259
  18.8 1.6 %collective-permute-start.4 = (s32[1,16]{1,0:T(1,128)S(1)}, s32[1,16]{1,0:T(1,128)S(1)}, u32[]{:S(2)}, u32[]{:S(2)}) collective-permute-start(s32[1,16]{1,0:T(1,128)S(1)} %copy-done.2), channel_id=1, source_target_pairs={{0,4},{4,8},{8,12},{12,0},{1,5},{5,9},{9,13},{13,1},{2,6},{6,10},{... | collective-permute-start | bytes 200 | tf_op jit(solution)/shard_map/ppermute | solution.py:252
  20.3 2.6 %collective-permute-start.3 = (s32[1,16]{1,0:T(1,128)S(1)}, s32[1,16]{1,0:T(1,128)S(1)}, u32[]{:S(2)}, u32[]{:S(2)}) collective-permute-start(s32[1,16]{1,0:T(1,128)S(1)} %copy-done.2), channel_id=1, source_target_pairs={{0,8},{4,12},{8,0},{12,4},{1,9},{5,13},{9,1},{13,5},{2,10},{6,14},... | collective-permute-start | bytes 200 | tf_op jit(solution)/shard_map/ppermute | solution.py:252
  22.9 1.4 %collective-permute-start.2 = (s32[1,16]{1,0:T(1,128)S(1)}, s32[1,16]{1,0:T(1,128)S(1)}, u32[]{:S(2)}, u32[]{:S(2)}) collective-permute-start(s32[1,16]{1,0:T(1,128)S(1)} %copy-done.2), channel_id=1, source_target_pairs={{0,12},{4,0},{8,4},{12,8},{1,13},{5,1},{9,5},{13,9},{2,14},{6,2},{... | collective-permute-start | bytes 200 | tf_op jit(solution)/shard_map/ppermute | solution.py:252
  24.3 0.0 collective-permute-done.4.refs_3_
  24.3 0.5 collective-permute-done.3.refs_2_
  24.8 1.7 %collective-permute-done.2.refs_1_ = s32[1,16]{1,0:T(1,128)S(1)} collective-permute-done((s32[1,16]{1,0:T(1,128)S(1)}, s32[1,16]{1,0:T(1,128)S(1)}, u32[]{:S(2)}, u32[]{:S(2)}) %collective-permute-start.2) | collective-permute-done | bytes 96 | tf_op jit(solution)/shard_map/ppermute | solution.py:252
  26.5 3.8 %shard_map.75 = (bf16[80,2048]{1,0:T(8,128)(2,1)}, bf16[80,2048]{1,0:T(8,128)(2,1)}, bf16[80,2048]{1,0:T(8,128)(2,1)}, bf16[80,2048]{1,0:T(8,128)(2,1)}) custom-call(s32[1,16]{1,0:T(1,128)S(1)} %copy-done.2, s32[1,16]{1,0:T(1,128)S(1)} %collective-permute-done.2.refs_1_, s32[1,16]{1,0:T(1,128)S(1)} %collective-permute-done.3.refs_2_, ...), custom_call_target="tpu_custom_call" | custom-call | flops 1000 | bytes 1000 | tf_op jit(solution)/shard_map/pallas_call | solution.py:117
  30.3 3.2 %collective-permute-start.8 = (bf16[80,2048]{1,0:T(8,128)(2,1)}, bf16[80,2048]{1,0:T(8,128)(2,1)S(1)}, u32[]{:S(2)}, u32[]{:S(2)}) collective-permute-start(bf16[80,2048]{1,0:T(8,128)(2,1)} %get-tuple-element.34), channel_id=1, source_target_pairs={{0,12},{4,0},{8,4},{12,8},{1,13},{5,1},{9,5},{13,9},{2,14},{6,2},{... | collective-permute-start | bytes 983048 | tf_op jit(solution)/shard_map/ppermute | solution.py:252
  33.5 0.0 collective-permute-start.7
  33.5 0.6 collective-permute-start.6
  34.2 21.6 %conditional.1 = (bf16[704,1024]{1,0:T(8,128)(2,1)}, bf16[704,2048]{1,0:T(8,128)(2,1)}) conditional(s32[]{:T(128)} %bitcast.2, () %tuple.17, (s32[2]{0:T(128)S(1)}, bf16[704,2048]{1,0:T(8,128)(2,1)S(1)}, bf16[2048,8192]{1,0:T(8,128)(2,1)}, bf16[80,2048]{1,0:T(8,128)(2,1)}) %tuple.24), branch_computations={%region_0.1_spmd, %region_1.2_spmd} | conditional | flops 3000 | bytes 17304600 | solution.py:240
  34.2 5.6 %branch_1_fun.3.refs_3_ = bf16[704,1024]{1,0:T(8,128)(2,1)S(1)} custom-call(s32[2]{0:T(128)S(1)} %get-tuple-element.13.refs_0_, bf16[704,2048]{1,0:T(8,128)(2,1)S(1)} %get-tuple-element.14.refs_1_, bf16[2048,8192]{1,0:T(8,128)(2,1)} %get-tuple-element.15.refs_2_, bf16[80,2048]{1,0:T(8,128)(2,1)} %get-tuple-element.16.refs_3_), custom_call_target="tpu_custom_call" | custom-call | flops 1000 | bytes 1000 | tf_op jit(solution)/shard_map/cond/branch_1_fun/pallas_call | solution.py:72
  39.8 0.1 collective-permute-start
  39.8 9.0 %branch_1_fun.4.refs_4_ = bf16[704,2048]{1,0:T(8,128)(2,1)S(1)} custom-call(s32[2]{0:T(128)S(1)} %get-tuple-element.13.refs_0_, bf16[704,2048]{1,0:T(8,128)(2,1)S(1)} %get-tuple-element.14.refs_1_, bf16[2048,8192]{1,0:T(8,128)(2,1)} %get-tuple-element.15.refs_2_, bf16[704,1024]{1,0:T(8,128)(2,1)S(1)} %branch_1_fun.3.refs_3_), custom_call_target="tpu_custom_call" | custom-call | flops 1000 | bytes 1000 | tf_op jit(solution)/shard_map/cond/branch_1_fun/pallas_call | solution.py:72
  48.8 0.0 collective-permute-done.refs_3_
  48.8 0.6 collective-permute-start.1
  49.4 6.3 %branch_1_fun.5 = bf16[704,1024]{1,0:T(8,128)(2,1)} custom-call(s32[2]{0:T(128)S(1)} %get-tuple-element.13.refs_0_, bf16[704,2048]{1,0:T(8,128)(2,1)S(1)} %get-tuple-element.14.refs_1_, bf16[2048,8192]{1,0:T(8,128)(2,1)} %get-tuple-element.15.refs_2_, bf16[704,1024]{1,0:T(8,128)(2,1)S(1)} %collective-permute-done.refs_3_, ...), custom_call_target="tpu_custom_call" | custom-call | flops 1000 | bytes 1000 | tf_op jit(solution)/shard_map/cond/branch_1_fun/pallas_call | solution.py:72
  55.7 0.0 collective-permute-done.1
  55.7 0.5 collective-permute-start.15
  56.3 2.8 %copy-done = bf16[96,16,2048]{2,1,0:T(8,128)(2,1)S(1)} copy-done((bf16[96,16,2048]{2,1,0:T(8,128)(2,1)S(1)}, bf16[96,16,2048]{2,1,0:T(8,128)(2,1)}, u32[]{:S(2)}) %copy-start) | copy-done | bytes 6291480
  59.1 2.8 %shard_map.77 = (bf16[80,2048]{1,0:T(8,128)(2,1)S(1)}, bf16[80,2048]{1,0:T(8,128)(2,1)S(1)}, bf16[80,2048]{1,0:T(8,128)(2,1)S(1)}, bf16[80,2048]{1,0:T(8,128)(2,1)S(1)}) custom-call(s32[1,16]{1,0:T(1,128)S(1)} %copy-done.2, s32[1,16]{1,0:T(1,128)S(1)} %collective-permute-done.2.refs_1_, s32[1,16]{1,0:T(1,128)S(1)} %collective-permute-done.3.refs_2_, ...), custom_call_target="tpu_custom_call" | custom-call | flops 1000 | bytes 1000 | tf_op jit(solution)/shard_map/pallas_call | solution.py:117
  61.9 0.0 collective-permute-done.8.refs_3_
  61.9 0.0 collective-permute-done.7.refs_2_
  61.9 0.0 collective-permute-done.6.refs_1_
  61.9 2.9 %collective-permute-start.14 = (bf16[80,2048]{1,0:T(8,128)(2,1)S(1)}, bf16[80,2048]{1,0:T(8,128)(2,1)S(1)}, u32[]{:S(2)}, u32[]{:S(2)}) collective-permute-start(bf16[80,2048]{1,0:T(8,128)(2,1)S(1)} %get-tuple-element.41), channel_id=1, source_target_pairs={{0,4},{4,8},{8,12},{12,0},{1,5},{5,9},{9,13},{13,1},{2,6},{6,10},{... | collective-permute-start | bytes 983048 | tf_op jit(solution)/shard_map/ppermute | solution.py:252
  64.8 0.9 collective-permute-start.13
  65.7 1.5 %collective-permute-start.12 = (bf16[80,2048]{1,0:T(8,128)(2,1)S(1)}, bf16[80,2048]{1,0:T(8,128)(2,1)S(1)}, u32[]{:S(2)}, u32[]{:S(2)}) collective-permute-start(bf16[80,2048]{1,0:T(8,128)(2,1)S(1)} %get-tuple-element.37), channel_id=1, source_target_pairs={{0,12},{4,0},{8,4},{12,8},{1,13},{5,1},{9,5},{13,9},{2,14},{6,2},{... | collective-permute-start | bytes 983048 | tf_op jit(solution)/shard_map/ppermute | solution.py:252
  67.3 0.0 collective-permute-done.9.refs_5_.refs_7_
  67.3 3.1 %shard_map.76 = f32[16,704]{1,0:T(8,128)S(1)} custom-call(s32[1,16]{1,0:T(1,128)S(1)} %copy-done.3, s32[1,16]{1,0:T(1,128)S(1)} %copy-done.2, s32[384]{0:T(512)S(1)} %copy-done.1, bf16[704,2048]{1,0:T(8,128)(2,1)S(1)} %copy-done.5, bf16[80,2048]{1,0:T(8,128)(2,1)} %get-tuple-element.31.refs_0_, bf16[80,2048]{1,0:T(8,128)(2,1)} %collective-permute-done.6.refs_1_, ...), custom_call_target="tpu_custom_call" | custom-call | flops 22000001024 | bytes 1000 | tf_op jit(solution)/shard_map/pallas_call | solution.py:170
  70.4 0.0 collective-permute-start.10
  70.4 1.3 %collective-permute-done.10 = f32[16,704]{1,0:T(8,128)S(1)} collective-permute-done((f32[16,704]{1,0:T(8,128)S(1)}, f32[16,704]{1,0:T(8,128)S(1)}, u32[]{:S(2)}, u32[]{:S(2)}) %collective-permute-start.10) | collective-permute-done | bytes 45088 | tf_op jit(solution)/shard_map/ppermute | solution.py:255
  71.7 1.6 %collective-permute-start.11 = (f32[16,704]{1,0:T(8,128)S(1)}, f32[16,704]{1,0:T(8,128)S(1)}, u32[]{:S(2)}, u32[]{:S(2)}) collective-permute-start(f32[16,704]{1,0:T(8,128)S(1)} %add.4.refs_4_.refs_0_), channel_id=1, source_target_pairs={{0,2},{1,3},{2,0},{3,1},{4,6},{5,7},{6,4},{7,5},{8,10},{9,11},{10,... | collective-permute-start | bytes 135176 | tf_op jit(solution)/shard_map/ppermute | solution.py:259
  73.2 9.2 %shard_map.78.refs_6_ = bf16[704,2048]{1,0:T(8,128)(2,1)S(1)} custom-call(s32[2]{0:T(128)S(1)} %pad_add_fusion.refs_0_, bf16[704,2048]{1,0:T(8,128)(2,1)S(1)} %copy-done.5, bf16[2048,8192]{1,0:T(8,128)(2,1)} %refs_2_.5, bf16[704,2048]{1,0:T(8,128)(2,1)} %get-tuple-element.43.refs_3_, f32[16,704]{1,0:T(8,128)S(1)} %add.4.refs_4_.refs_0_), custom_call_target="tpu_custom_call" | custom-call | flops 1000 | bytes 1000 | tf_op jit(solution)/shard_map/pallas_call | solution.py:72
  82.5 0.0 collective-permute-done.14.refs_4_
  82.5 4.8 %collective-permute-done.13.refs_3_ = bf16[80,2048]{1,0:T(8,128)(2,1)S(1)} collective-permute-done((bf16[80,2048]{1,0:T(8,128)(2,1)S(1)}, bf16[80,2048]{1,0:T(8,128)(2,1)S(1)}, u32[]{:S(2)}, u32[]{:S(2)}) %collective-permute-start.13) | collective-permute-done | bytes 327712 | tf_op jit(solution)/shard_map/ppermute | solution.py:252
  87.3 2.7 %collective-permute-done.15.refs_8_ = bf16[704,1024]{1,0:T(8,128)(2,1)S(1)} collective-permute-done((bf16[704,1024]{1,0:T(8,128)(2,1)}, bf16[704,1024]{1,0:T(8,128)(2,1)S(1)}, u32[]{:S(2)}, u32[]{:S(2)}) %collective-permute-start.15) | collective-permute-done | bytes 1441824 | tf_op jit(solution)/shard_map/ppermute | solution.py:259
  90.0 0.5 collective-permute-done.11.refs_1_
  90.5 5.0 %shard_map.79 = bf16[704,2048]{1,0:T(8,128)(2,1)} custom-call(s32[1,16]{1,0:T(1,128)S(1)} %copy-done.3, s32[1,16]{1,0:T(1,128)S(1)} %copy-done.2, s32[384]{0:T(512)S(1)} %copy-done.1, f32[16,704]{1,0:T(8,128)S(1)} %add.4.refs_4_.refs_0_, f32[16,704]{1,0:T(8,128)S(1)} %collective-permute-done.11.refs_1_, ...), custom_call_target="tpu_custom_call" | custom-call | flops 1000 | bytes 1000 | tf_op jit(solution)/shard_map/pallas_call | solution.py:226
  (14 shorter events, 0.0 us)
Async XLA Ops:
  0.1 10.2 %copy-start.4 = (bf16[704,2048]{1,0:T(8,128)(2,1)S(1)}, bf16[704,2048]{1,0:T(8,128)(2,1)}, u32[]{:S(2)}) copy-start(bf16[704,2048]{1,0:T(8,128)(2,1)} %refs_1_.5) | copy-start | bytes 8650756
  0.1 26.4 %slice-start = ((s8[6291456]{0:T(1024)(128)(4,1)}), s8[4194304]{0:T(1024)(128)(4,1)S(1)}, s32[]{:S(2)}) async-start(s8[6291456]{0:T(1024)(128)(4,1)} %bitcast.4), calls=%async_computation | async-start | bytes 8388608
  6.8 11.9 %copy-start.2 = (s32[1,16]{1,0:T(1,128)S(1)}, s32[1,16]{1,0:T(1,128)}, u32[]{:S(2)}) copy-start(s32[1,16]{1,0:T(1,128)} %id_ref.3) | copy-start | bytes 196
  6.8 19.6 %slice-start.1 = ((s8[6291456]{0:T(1024)(128)(4,1)}), s8[2097152]{0:T(1024)(128)(4,1)S(1)}, s32[]{:S(2)}) async-start(s8[6291456]{0:T(1024)(128)(4,1)} %bitcast.4), calls=%async_computation.1 | async-start | bytes 4194304
  6.8 19.6 %copy-start.1 = (s32[384]{0:T(512)S(1)}, s32[384]{0:T(512)}, u32[]{:S(2)}) copy-start(s32[384]{0:T(512)} %row_ref.3) | copy-start | bytes 4612
  6.8 3.4 %collective-permute-start.5 = (bf16[704,1024]{1,0:T(8,128)(2,1)S(1)}, bf16[704,1024]{1,0:T(8,128)(2,1)S(1)}, u32[]{:S(2)}, u32[]{:S(2)}) collective-permute-start(bf16[704,1024]{1,0:T(8,128)(2,1)S(1)} %shard_map.73), channel_id=1, source_target_pairs={{0,1},{1,0},{2,3},{3,2},{4,5},{5,4},{6,7},{7,6},{8,9},{9,8},{10,11... | collective-permute-start | bytes 4325384 | tf_op jit(solution)/shard_map/ppermute | solution.py:255
  15.8 18.3 %copy-start.3 = (s32[1,16]{1,0:T(1,128)S(1)}, s32[1,16]{1,0:T(1,128)}, u32[]{:S(2)}) copy-start(s32[1,16]{1,0:T(1,128)} %counts_ref.3) | copy-start | bytes 196
  15.8 51.4 %collective-permute-start.9 = (bf16[704,1024]{1,0:T(8,128)(2,1)S(1)}, bf16[704,1024]{1,0:T(8,128)(2,1)S(1)}, u32[]{:S(2)}, u32[]{:S(2)}) collective-permute-start(bf16[704,1024]{1,0:T(8,128)(2,1)S(1)} %shard_map.74.refs_6_), channel_id=1, source_target_pairs={{0,2},{1,3},{2,0},{3,1},{4,6},{5,7},{6,4},{7,5},{8,10},{9,11},{10,... | collective-permute-start | bytes 4325384 | tf_op jit(solution)/shard_map/ppermute | solution.py:259
  18.8 5.5 %collective-permute-start.4 = (s32[1,16]{1,0:T(1,128)S(1)}, s32[1,16]{1,0:T(1,128)S(1)}, u32[]{:S(2)}, u32[]{:S(2)}) collective-permute-start(s32[1,16]{1,0:T(1,128)S(1)} %copy-done.2), channel_id=1, source_target_pairs={{0,4},{4,8},{8,12},{12,0},{1,5},{5,9},{9,13},{13,1},{2,6},{6,10},{... | collective-permute-start | bytes 200 | tf_op jit(solution)/shard_map/ppermute | solution.py:252
  20.3 4.4 %collective-permute-start.3 = (s32[1,16]{1,0:T(1,128)S(1)}, s32[1,16]{1,0:T(1,128)S(1)}, u32[]{:S(2)}, u32[]{:S(2)}) collective-permute-start(s32[1,16]{1,0:T(1,128)S(1)} %copy-done.2), channel_id=1, source_target_pairs={{0,8},{4,12},{8,0},{12,4},{1,9},{5,13},{9,1},{13,5},{2,10},{6,14},... | collective-permute-start | bytes 200 | tf_op jit(solution)/shard_map/ppermute | solution.py:252
  22.9 3.5 %collective-permute-start.2 = (s32[1,16]{1,0:T(1,128)S(1)}, s32[1,16]{1,0:T(1,128)S(1)}, u32[]{:S(2)}, u32[]{:S(2)}) collective-permute-start(s32[1,16]{1,0:T(1,128)S(1)} %copy-done.2), channel_id=1, source_target_pairs={{0,12},{4,0},{8,4},{12,8},{1,13},{5,1},{9,5},{13,9},{2,14},{6,2},{... | collective-permute-start | bytes 200 | tf_op jit(solution)/shard_map/ppermute | solution.py:252
  30.3 31.6 %collective-permute-start.8 = (bf16[80,2048]{1,0:T(8,128)(2,1)}, bf16[80,2048]{1,0:T(8,128)(2,1)S(1)}, u32[]{:S(2)}, u32[]{:S(2)}) collective-permute-start(bf16[80,2048]{1,0:T(8,128)(2,1)} %get-tuple-element.34), channel_id=1, source_target_pairs={{0,12},{4,0},{8,4},{12,8},{1,13},{5,1},{9,5},{13,9},{2,14},{6,2},{... | collective-permute-start | bytes 983048 | tf_op jit(solution)/shard_map/ppermute | solution.py:252
  33.5 28.4 %collective-permute-start.7 = (bf16[80,2048]{1,0:T(8,128)(2,1)}, bf16[80,2048]{1,0:T(8,128)(2,1)}, u32[]{:S(2)}, u32[]{:S(2)}) collective-permute-start(bf16[80,2048]{1,0:T(8,128)(2,1)} %get-tuple-element.33), channel_id=1, source_target_pairs={{0,8},{4,12},{8,0},{12,4},{1,9},{5,13},{9,1},{13,5},{2,10},{6,14},... | collective-permute-start | bytes 983048 | tf_op jit(solution)/shard_map/ppermute | solution.py:252
  33.5 28.4 %collective-permute-start.6 = (bf16[80,2048]{1,0:T(8,128)(2,1)}, bf16[80,2048]{1,0:T(8,128)(2,1)}, u32[]{:S(2)}, u32[]{:S(2)}) collective-permute-start(bf16[80,2048]{1,0:T(8,128)(2,1)} %get-tuple-element.32), channel_id=1, source_target_pairs={{0,4},{4,8},{8,12},{12,0},{1,5},{5,9},{9,13},{13,1},{2,6},{6,10},{... | collective-permute-start | bytes 983048 | tf_op jit(solution)/shard_map/ppermute | solution.py:252
  39.8 9.1 %collective-permute-start = (bf16[704,1024]{1,0:T(8,128)(2,1)S(1)}, bf16[704,1024]{1,0:T(8,128)(2,1)S(1)}, u32[]{:S(2)}, u32[]{:S(2)}) collective-permute-start(bf16[704,1024]{1,0:T(8,128)(2,1)S(1)} %branch_1_fun.3.refs_3_), channel_id=1, source_target_pairs={{0,1},{1,0},{2,3},{3,2},{4,5},{5,4},{6,7},{7,6},{8,9},{9,8},{10,11... | collective-permute-start | bytes 4325384 | tf_op jit(solution)/shard_map/cond/branch_1_fun/ppermute | solution.py:255
  48.8 6.9 %collective-permute-start.1 = (bf16[704,2048]{1,0:T(8,128)(2,1)S(1)}, bf16[704,2048]{1,0:T(8,128)(2,1)}, u32[]{:S(2)}, u32[]{:S(2)}) collective-permute-start(bf16[704,2048]{1,0:T(8,128)(2,1)S(1)} %branch_1_fun.4.refs_4_), channel_id=1, source_target_pairs={{0,1},{1,0},{2,3},{3,2},{4,5},{5,4},{6,7},{7,6},{8,9},{9,8},{10,11... | collective-permute-start | bytes 8650760 | tf_op jit(solution)/shard_map/cond/branch_1_fun/ppermute | solution.py:255
  55.7 34.2 %collective-permute-start.15 = (bf16[704,1024]{1,0:T(8,128)(2,1)}, bf16[704,1024]{1,0:T(8,128)(2,1)S(1)}, u32[]{:S(2)}, u32[]{:S(2)}) collective-permute-start(bf16[704,1024]{1,0:T(8,128)(2,1)} %get-tuple-element.35.refs_4_.refs_6_), channel_id=1, source_target_pairs={{0,2},{1,3},{2,0},{3,1},{4,6},{5,7},{6,4},{7,5},{8,10},{9,11},{10,... | collective-permute-start | bytes 4325384 | tf_op jit(solution)/shard_map/ppermute | solution.py:259
  56.3 2.8 %copy-start = (bf16[96,16,2048]{2,1,0:T(8,128)(2,1)S(1)}, bf16[96,16,2048]{2,1,0:T(8,128)(2,1)}, u32[]{:S(2)}) copy-start(bf16[96,16,2048]{2,1,0:T(8,128)(2,1)} %refs_5_.3) | copy-start | bytes 18874372
  59.1 8.2 %copy-start.5 = (bf16[704,2048]{1,0:T(8,128)(2,1)S(1)}, bf16[704,2048]{1,0:T(8,128)(2,1)}, u32[]{:S(2)}) copy-start(bf16[704,2048]{1,0:T(8,128)(2,1)} %refs_1_.5) | copy-start | bytes 8650756
  61.9 20.5 %collective-permute-start.14 = (bf16[80,2048]{1,0:T(8,128)(2,1)S(1)}, bf16[80,2048]{1,0:T(8,128)(2,1)S(1)}, u32[]{:S(2)}, u32[]{:S(2)}) collective-permute-start(bf16[80,2048]{1,0:T(8,128)(2,1)S(1)} %get-tuple-element.41), channel_id=1, source_target_pairs={{0,4},{4,8},{8,12},{12,0},{1,5},{5,9},{9,13},{13,1},{2,6},{6,10},{... | collective-permute-start | bytes 983048 | tf_op jit(solution)/shard_map/ppermute | solution.py:252
  64.8 22.5 %collective-permute-start.13 = (bf16[80,2048]{1,0:T(8,128)(2,1)S(1)}, bf16[80,2048]{1,0:T(8,128)(2,1)S(1)}, u32[]{:S(2)}, u32[]{:S(2)}) collective-permute-start(bf16[80,2048]{1,0:T(8,128)(2,1)S(1)} %get-tuple-element.39), channel_id=1, source_target_pairs={{0,8},{4,12},{8,0},{12,4},{1,9},{5,13},{9,1},{13,5},{2,10},{6,14},... | collective-permute-start | bytes 983048 | tf_op jit(solution)/shard_map/ppermute | solution.py:252
  65.7 21.6 %collective-permute-start.12 = (bf16[80,2048]{1,0:T(8,128)(2,1)S(1)}, bf16[80,2048]{1,0:T(8,128)(2,1)S(1)}, u32[]{:S(2)}, u32[]{:S(2)}) collective-permute-start(bf16[80,2048]{1,0:T(8,128)(2,1)S(1)} %get-tuple-element.37), channel_id=1, source_target_pairs={{0,12},{4,0},{8,4},{12,8},{1,13},{5,1},{9,5},{13,9},{2,14},{6,2},{... | collective-permute-start | bytes 983048 | tf_op jit(solution)/shard_map/ppermute | solution.py:252
  70.4 1.3 %collective-permute-start.10 = (f32[16,704]{1,0:T(8,128)S(1)}, f32[16,704]{1,0:T(8,128)S(1)}, u32[]{:S(2)}, u32[]{:S(2)}) collective-permute-start(f32[16,704]{1,0:T(8,128)S(1)} %shard_map.76), channel_id=1, source_target_pairs={{0,1},{1,0},{2,3},{3,2},{4,5},{5,4},{6,7},{7,6},{8,9},{9,8},{10,11... | collective-permute-start | bytes 135176 | tf_op jit(solution)/shard_map/ppermute | solution.py:255
  71.7 18.8 %collective-permute-start.11 = (f32[16,704]{1,0:T(8,128)S(1)}, f32[16,704]{1,0:T(8,128)S(1)}, u32[]{:S(2)}, u32[]{:S(2)}) collective-permute-start(f32[16,704]{1,0:T(8,128)S(1)} %add.4.refs_4_.refs_0_), channel_id=1, source_target_pairs={{0,2},{1,3},{2,0},{3,1},{4,6},{5,7},{6,4},{7,5},{8,10},{9,11},{10,... | collective-permute-start | bytes 135176 | tf_op jit(solution)/shard_map/ppermute | solution.py:259

commit v5 on v4

--- a/solution.py
+++ b/solution.py
@@ -14,7 +14,7 @@
 CORES = 2
 LANES = 128
 adapter_scale = 0.5
-VMEM_LIMIT = 42 * 1024 * 1024
+VMEM_LIMIT = 34 * 1024 * 1024
 
 ANY = pl.BlockSpec(memory_space=pl.ANY)
 HBM = pl.BlockSpec(memory_space=pltpu.HBM)
@@ -120,7 +120,7 @@
         out_specs=[WHOLE] * (n_stores * ways),
         out_shape=[shape] * (n_stores * ways),
         scratch_shapes=[pltpu.SemaphoreType.DMA((n_stores * ways,))],
-        compiler_params=PARAMS,
+        compiler_params=pltpu.CompilerParams(vmem_limit_bytes=50 * 1024 * 1024),
         cost_estimate=CHEAP,
     )(*ids, store_row, *stores, *after)
     return outs
@@ -181,7 +181,7 @@
     rows, block = base.shape
     ways, depth = len(ups), ups[0].shape[0]
     wide = ways * depth
-    tile = math.gcd(*[send[0].shape[1] for send in sends], 512)
+    tile = math.gcd(*[send[0].shape[1] for send in sends], 1024)
     n_low = len(lows)
 
     def kernel(counts_ref, id_ref, row_ref, *refs):

time: 97.2 us -> 94.7 us (0.974); the launches traced: 95.5 us -> 94.4 us
  waiting for transfers between devices: 14.4 us -> 17.8 us
  local copies, waits for them, and re-layouts: 2.82 us -> 0.03 us
  Pallas kernels: 57.1 us -> 55.4 us
    ppermute x3, waiting for transfers between devices: 3.21 us -> 6.59 us  [to_chip(): lax.ppermute(array, 'tensor', [(i, (i + CORES * shift) % size) for i in r...]
    unnamed x16 -> x10, local copies, waits for them, and re-layouts: 2.82 us -> 0.03 us
    pallas_call x2, Pallas kernels: 6.59 us -> 5.5 us  [pick(): pl.pallas_call(kernel, in_specs=[SMEM] * (ways + 1) + [HBM] * n_stores +...]
    ppermute x9, starting transfers between devices: 14.7 us -> 15.7 us  [along_dp(): lax.ppermute(array, 'dp', [(i, (i + shift) % ways) for i in range(ways)])]
  transfers between devices with their start and end apart: 16 -> 16, of which waited for: 7 -> 8; matrix products, arithmetic and copies ran while one was open for 0% -> 0% of each run, Pallas kernels for 42% -> 41%
where the time goes in v5:
time: 94.7 us; the launch traced here: 94.4 us
  Pallas kernels  55.4 us (59%)
  starting transfers between devices  20.9 us (22%)
  waiting for transfers between devices  17.8 us (19%)
    pallas_call x6, Pallas kernels, product(): pl.pallas_call(kernel, grid_spec=pltpu.PrefetchScalarGridSpec(num_scalar_...  42.4 us
    ppermute x9, starting transfers between devices, along_dp(): lax.ppermute(array, 'dp', [(i, (i + shift) % ways) for i in range(ways)])  15.7 us
    ppermute x9, waiting for transfers between devices, along_dp(): lax.ppermute(array, 'dp', [(i, (i + shift) % ways) for i in range(ways)])  7.09 us
    ppermute x3, waiting for transfers between devices, to_chip(): lax.ppermute(array, 'tensor', [(i, (i + CORES * shift) % size) for i in r...  6.59 us
    pallas_call x2, Pallas kernels, pick(): pl.pallas_call(kernel, in_specs=[SMEM] * (ways + 1) + [HBM] * n_stores +...  5.5 us
    pallas_call x1, Pallas kernels, finish(): pl.pallas_call(kernel, grid=(block // tile,), in_specs=specs, out_specs=h...  4.32 us
    ppermute x4, waiting for transfers between devices, to_core(): lax.ppermute(array, 'tensor', [(i, i ^ 1) for i in range(chips * CORES)])  4.11 us
    ppermute x3, starting transfers between devices, to_chip(): lax.ppermute(array, 'tensor', [(i, (i + CORES * shift) % size) for i in r...  4.05 us
  transfers between devices with their start and end apart: 16, of which 8 were waited for; matrix products, arithmetic and copies ran while one was open for 0% of the time, Pallas kernels for 41%

profile of v5, /device:TPU:0, one launch (start us, length us, event | category | flops | bytes accessed | tf_op | source)
XLA Modules:
  0.0 94.4 jit_solution(1383873242805214932)
XLA Ops:
  0.0 0.1 pad_add_fusion.refs_0_
  0.1 6.7 %shard_map.73 = bf16[704,1024]{1,0:T(8,128)(2,1)S(1)} custom-call(s32[2]{0:T(128)S(1)} %pad_add_fusion.refs_0_, bf16[704,2048]{1,0:T(8,128)(2,1)} %refs_1_.5, bf16[2048,8192]{1,0:T(8,128)(2,1)} %refs_2_.5), custom_call_target="tpu_custom_call" | custom-call | flops 1000 | bytes 1000 | tf_op jit(solution)/shard_map/pallas_call | solution.py:72
  6.8 0.0 copy-start.1
  6.8 0.0 copy-start
  6.8 0.5 collective-permute-start.5
  7.4 2.8 %collective-permute-done.5.refs_3_ = bf16[704,1024]{1,0:T(8,128)(2,1)S(1)} collective-permute-done((bf16[704,1024]{1,0:T(8,128)(2,1)S(1)}, bf16[704,1024]{1,0:T(8,128)(2,1)S(1)}, u32[]{:S(2)}, u32[]{:S(2)}) %collective-permute-start.5) | collective-permute-done | bytes 1441824 | tf_op jit(solution)/shard_map/ppermute | solution.py:255
  10.2 0.0 copy-done.3
  10.2 5.6 %shard_map.74.refs_6_ = bf16[704,1024]{1,0:T(8,128)(2,1)S(1)} custom-call(s32[2]{0:T(128)S(1)} %pad_add_fusion.refs_0_, bf16[704,2048]{1,0:T(8,128)(2,1)S(1)} %copy-done.3, bf16[2048,8192]{1,0:T(8,128)(2,1)} %refs_2_.5, bf16[704,1024]{1,0:T(8,128)(2,1)S(1)} %collective-permute-done.5.refs_3_), custom_call_target="tpu_custom_call" | custom-call | flops 1000 | bytes 1000 | tf_op jit(solution)/shard_map/pallas_call | solution.py:72
  15.8 0.0 copy-start.2
  15.8 2.9 %collective-permute-start.9 = (bf16[704,1024]{1,0:T(8,128)(2,1)S(1)}, bf16[704,1024]{1,0:T(8,128)(2,1)S(1)}, u32[]{:S(2)}, u32[]{:S(2)}) collective-permute-start(bf16[704,1024]{1,0:T(8,128)(2,1)S(1)} %shard_map.74.refs_6_), channel_id=1, source_target_pairs={{0,2},{1,3},{2,0},{3,1},{4,6},{5,7},{6,4},{7,5},{8,10},{9,11},{10,... | collective-permute-start | bytes 4325384 | tf_op jit(solution)/shard_map/ppermute | solution.py:259
  18.7 1.6 %collective-permute-start.4 = (s32[1,16]{1,0:T(1,128)S(1)}, s32[1,16]{1,0:T(1,128)S(1)}, u32[]{:S(2)}, u32[]{:S(2)}) collective-permute-start(s32[1,16]{1,0:T(1,128)S(1)} %copy-done.1), channel_id=1, source_target_pairs={{0,4},{4,8},{8,12},{12,0},{1,5},{5,9},{9,13},{13,1},{2,6},{6,10},{... | collective-permute-start | bytes 200 | tf_op jit(solution)/shard_map/ppermute | solution.py:252
  20.3 2.6 %collective-permute-start.3 = (s32[1,16]{1,0:T(1,128)S(1)}, s32[1,16]{1,0:T(1,128)S(1)}, u32[]{:S(2)}, u32[]{:S(2)}) collective-permute-start(s32[1,16]{1,0:T(1,128)S(1)} %copy-done.1), channel_id=1, source_target_pairs={{0,8},{4,12},{8,0},{12,4},{1,9},{5,13},{9,1},{13,5},{2,10},{6,14},... | collective-permute-start | bytes 200 | tf_op jit(solution)/shard_map/ppermute | solution.py:252
  22.9 1.3 %collective-permute-start.2 = (s32[1,16]{1,0:T(1,128)S(1)}, s32[1,16]{1,0:T(1,128)S(1)}, u32[]{:S(2)}, u32[]{:S(2)}) collective-permute-start(s32[1,16]{1,0:T(1,128)S(1)} %copy-done.1), channel_id=1, source_target_pairs={{0,12},{4,0},{8,4},{12,8},{1,13},{5,1},{9,5},{13,9},{2,14},{6,2},{... | collective-permute-start | bytes 200 | tf_op jit(solution)/shard_map/ppermute | solution.py:252
  24.3 0.0 collective-permute-done.4.refs_3_
  24.3 0.5 collective-permute-done.3.refs_2_
  24.8 1.7 %collective-permute-done.2.refs_1_ = s32[1,16]{1,0:T(1,128)S(1)} collective-permute-done((s32[1,16]{1,0:T(1,128)S(1)}, s32[1,16]{1,0:T(1,128)S(1)}, u32[]{:S(2)}, u32[]{:S(2)}) %collective-permute-start.2) | collective-permute-done | bytes 96 | tf_op jit(solution)/shard_map/ppermute | solution.py:252
  26.5 3.3 %shard_map.75 = (bf16[80,2048]{1,0:T(8,128)(2,1)}, bf16[80,2048]{1,0:T(8,128)(2,1)}, bf16[80,2048]{1,0:T(8,128)(2,1)}, bf16[80,2048]{1,0:T(8,128)(2,1)}) custom-call(s32[1,16]{1,0:T(1,128)S(1)} %copy-done.1, s32[1,16]{1,0:T(1,128)S(1)} %collective-permute-done.2.refs_1_, s32[1,16]{1,0:T(1,128)S(1)} %collective-permute-done.3.refs_2_, ...), custom_call_target="tpu_custom_call" | custom-call | flops 1000 | bytes 1000 | tf_op jit(solution)/shard_map/pallas_call | solution.py:117
  29.7 3.3 %collective-permute-start.8 = (bf16[80,2048]{1,0:T(8,128)(2,1)}, bf16[80,2048]{1,0:T(8,128)(2,1)S(1)}, u32[]{:S(2)}, u32[]{:S(2)}) collective-permute-start(bf16[80,2048]{1,0:T(8,128)(2,1)} %get-tuple-element.34), channel_id=1, source_target_pairs={{0,12},{4,0},{8,4},{12,8},{1,13},{5,1},{9,5},{13,9},{2,14},{6,2},{... | collective-permute-start | bytes 983048 | tf_op jit(solution)/shard_map/ppermute | solution.py:252
  33.0 0.0 collective-permute-start.7
  33.0 0.6 collective-permute-start.6
  33.7 21.6 %conditional.1 = (bf16[704,1024]{1,0:T(8,128)(2,1)}, bf16[704,2048]{1,0:T(8,128)(2,1)}) conditional(s32[]{:T(128)} %bitcast.2, () %tuple.17, (s32[2]{0:T(128)S(1)}, bf16[704,2048]{1,0:T(8,128)(2,1)S(1)}, bf16[2048,8192]{1,0:T(8,128)(2,1)}, bf16[80,2048]{1,0:T(8,128)(2,1)}) %tuple.24), branch_computations={%region_0.1_spmd, %region_1.2_spmd} | conditional | flops 3000 | bytes 17304600 | solution.py:240
  33.7 5.6 %branch_1_fun.3.refs_3_ = bf16[704,1024]{1,0:T(8,128)(2,1)S(1)} custom-call(s32[2]{0:T(128)S(1)} %get-tuple-element.13.refs_0_, bf16[704,2048]{1,0:T(8,128)(2,1)S(1)} %get-tuple-element.14.refs_1_, bf16[2048,8192]{1,0:T(8,128)(2,1)} %get-tuple-element.15.refs_2_, bf16[80,2048]{1,0:T(8,128)(2,1)} %get-tuple-element.16.refs_3_), custom_call_target="tpu_custom_call" | custom-call | flops 1000 | bytes 1000 | tf_op jit(solution)/shard_map/cond/branch_1_fun/pallas_call | solution.py:72
  39.3 0.1 collective-permute-start
  39.4 9.0 %branch_1_fun.4.refs_4_ = bf16[704,2048]{1,0:T(8,128)(2,1)S(1)} custom-call(s32[2]{0:T(128)S(1)} %get-tuple-element.13.refs_0_, bf16[704,2048]{1,0:T(8,128)(2,1)S(1)} %get-tuple-element.14.refs_1_, bf16[2048,8192]{1,0:T(8,128)(2,1)} %get-tuple-element.15.refs_2_, bf16[704,1024]{1,0:T(8,128)(2,1)S(1)} %branch_1_fun.3.refs_3_), custom_call_target="tpu_custom_call" | custom-call | flops 1000 | bytes 1000 | tf_op jit(solution)/shard_map/cond/branch_1_fun/pallas_call | solution.py:72
  48.4 0.0 collective-permute-done.refs_3_
  48.4 0.6 collective-permute-start.1
  48.9 6.3 %branch_1_fun.5 = bf16[704,1024]{1,0:T(8,128)(2,1)} custom-call(s32[2]{0:T(128)S(1)} %get-tuple-element.13.refs_0_, bf16[704,2048]{1,0:T(8,128)(2,1)S(1)} %get-tuple-element.14.refs_1_, bf16[2048,8192]{1,0:T(8,128)(2,1)} %get-tuple-element.15.refs_2_, bf16[704,1024]{1,0:T(8,128)(2,1)S(1)} %collective-permute-done.refs_3_, ...), custom_call_target="tpu_custom_call" | custom-call | flops 1000 | bytes 1000 | tf_op jit(solution)/shard_map/cond/branch_1_fun/pallas_call | solution.py:72
  55.3 0.0 collective-permute-done.1
  55.3 0.5 collective-permute-start.15
  55.8 2.2 %shard_map.77 = (bf16[80,2048]{1,0:T(8,128)(2,1)S(1)}, bf16[80,2048]{1,0:T(8,128)(2,1)S(1)}, bf16[80,2048]{1,0:T(8,128)(2,1)S(1)}, bf16[80,2048]{1,0:T(8,128)(2,1)S(1)}) custom-call(s32[1,16]{1,0:T(1,128)S(1)} %copy-done.1, s32[1,16]{1,0:T(1,128)S(1)} %collective-permute-done.2.refs_1_, s32[1,16]{1,0:T(1,128)S(1)} %collective-permute-done.3.refs_2_, ...), custom_call_target="tpu_custom_call" | custom-call | flops 1000 | bytes 1000 | tf_op jit(solution)/shard_map/pallas_call | solution.py:117
  58.1 0.0 collective-permute-done.8.refs_3_
  58.1 0.9 collective-permute-done.7.refs_2_
  58.9 0.0 collective-permute-done.6.refs_1_
  59.0 2.0 %collective-permute-start.14 = (bf16[80,2048]{1,0:T(8,128)(2,1)S(1)}, bf16[80,2048]{1,0:T(8,128)(2,1)S(1)}, u32[]{:S(2)}, u32[]{:S(2)}) collective-permute-start(bf16[80,2048]{1,0:T(8,128)(2,1)S(1)} %get-tuple-element.41), channel_id=1, source_target_pairs={{0,4},{4,8},{8,12},{12,0},{1,5},{5,9},{9,13},{13,1},{2,6},{6,10},{... | collective-permute-start | bytes 983048 | tf_op jit(solution)/shard_map/ppermute | solution.py:252
  61.0 1.3 %collective-permute-start.13 = (bf16[80,2048]{1,0:T(8,128)(2,1)S(1)}, bf16[80,2048]{1,0:T(8,128)(2,1)S(1)}, u32[]{:S(2)}, u32[]{:S(2)}) collective-permute-start(bf16[80,2048]{1,0:T(8,128)(2,1)S(1)} %get-tuple-element.39), channel_id=1, source_target_pairs={{0,8},{4,12},{8,0},{12,4},{1,9},{5,13},{9,1},{13,5},{2,10},{6,14},... | collective-permute-start | bytes 983048 | tf_op jit(solution)/shard_map/ppermute | solution.py:252
  62.3 2.9 %collective-permute-start.12 = (bf16[80,2048]{1,0:T(8,128)(2,1)S(1)}, bf16[80,2048]{1,0:T(8,128)(2,1)S(1)}, u32[]{:S(2)}, u32[]{:S(2)}) collective-permute-start(bf16[80,2048]{1,0:T(8,128)(2,1)S(1)} %get-tuple-element.37), channel_id=1, source_target_pairs={{0,12},{4,0},{8,4},{12,8},{1,13},{5,1},{9,5},{13,9},{2,14},{6,2},{... | collective-permute-start | bytes 983048 | tf_op jit(solution)/shard_map/ppermute | solution.py:252
  65.2 0.0 collective-permute-done.9.refs_5_.refs_7_
  65.2 3.1 %shard_map.76 = f32[16,704]{1,0:T(8,128)S(1)} custom-call(s32[1,16]{1,0:T(1,128)S(1)} %copy-done.2, s32[1,16]{1,0:T(1,128)S(1)} %copy-done.1, s32[384]{0:T(512)S(1)} %copy-done, bf16[704,2048]{1,0:T(8,128)(2,1)S(1)} %copy-done.4, bf16[80,2048]{1,0:T(8,128)(2,1)} %get-tuple-element.31.refs_0_, bf16[80,2048]{1,0:T(8,128)(2,1)} %collective-permute-done.6.refs_1_, ...), custom_call_target="tpu_custom_call" | custom-call | flops 22000001024 | bytes 1000 | tf_op jit(solution)/shard_map/pallas_call | solution.py:170
  68.4 0.0 collective-permute-start.10
  68.4 1.3 %collective-permute-done.10 = f32[16,704]{1,0:T(8,128)S(1)} collective-permute-done((f32[16,704]{1,0:T(8,128)S(1)}, f32[16,704]{1,0:T(8,128)S(1)}, u32[]{:S(2)}, u32[]{:S(2)}) %collective-permute-start.10) | collective-permute-done | bytes 45088 | tf_op jit(solution)/shard_map/ppermute | solution.py:255
  69.6 0.6 collective-permute-start.11
  70.2 9.2 %shard_map.78.refs_6_ = bf16[704,2048]{1,0:T(8,128)(2,1)S(1)} custom-call(s32[2]{0:T(128)S(1)} %pad_add_fusion.refs_0_, bf16[704,2048]{1,0:T(8,128)(2,1)S(1)} %copy-done.4, bf16[2048,8192]{1,0:T(8,128)(2,1)} %refs_2_.5, bf16[704,2048]{1,0:T(8,128)(2,1)} %get-tuple-element.43.refs_3_, f32[16,704]{1,0:T(8,128)S(1)} %add.4.refs_4_.refs_0_), custom_call_target="tpu_custom_call" | custom-call | flops 1000 | bytes 1000 | tf_op jit(solution)/shard_map/pallas_call | solution.py:72
  79.5 0.0 collective-permute-done.14.refs_4_
  79.5 4.0 %collective-permute-done.13.refs_3_ = bf16[80,2048]{1,0:T(8,128)(2,1)S(1)} collective-permute-done((bf16[80,2048]{1,0:T(8,128)(2,1)S(1)}, bf16[80,2048]{1,0:T(8,128)(2,1)S(1)}, u32[]{:S(2)}, u32[]{:S(2)}) %collective-permute-start.13) | collective-permute-done | bytes 327712 | tf_op jit(solution)/shard_map/ppermute | solution.py:252
  83.5 0.0 collective-permute-done.12.refs_2_
  83.5 6.1 %collective-permute-done.15.refs_8_ = bf16[704,1024]{1,0:T(8,128)(2,1)S(1)} collective-permute-done((bf16[704,1024]{1,0:T(8,128)(2,1)}, bf16[704,1024]{1,0:T(8,128)(2,1)S(1)}, u32[]{:S(2)}, u32[]{:S(2)}) %collective-permute-start.15) | collective-permute-done | bytes 1441824 | tf_op jit(solution)/shard_map/ppermute | solution.py:259
  89.5 0.5 collective-permute-done.11.refs_1_
  90.1 4.3 %shard_map.79 = bf16[704,2048]{1,0:T(8,128)(2,1)} custom-call(s32[1,16]{1,0:T(1,128)S(1)} %copy-done.2, s32[1,16]{1,0:T(1,128)S(1)} %copy-done.1, s32[384]{0:T(512)S(1)} %copy-done, f32[16,704]{1,0:T(8,128)S(1)} %add.4.refs_4_.refs_0_, f32[16,704]{1,0:T(8,128)S(1)} %collective-permute-done.11.refs_1_, bf16[80,2048]{1,0:T(8,128)(2,1)S(1)} %collective-permute-done.12.refs_2_, ...), custom_call_target="tpu_custom_call" | custom-call | flops 1000 | bytes 1000 | tf_op jit(solution)/shard_map/pallas_call | solution.py:226
  (7 shorter events, 0.0 us)
Async XLA Ops:
  0.1 10.1 %copy-start.3 = (bf16[704,2048]{1,0:T(8,128)(2,1)S(1)}, bf16[704,2048]{1,0:T(8,128)(2,1)}, u32[]{:S(2)}) copy-start(bf16[704,2048]{1,0:T(8,128)(2,1)} %refs_1_.5) | copy-start | bytes 8650756
  6.8 11.9 %copy-start.1 = (s32[1,16]{1,0:T(1,128)S(1)}, s32[1,16]{1,0:T(1,128)}, u32[]{:S(2)}) copy-start(s32[1,16]{1,0:T(1,128)} %id_ref.3) | copy-start | bytes 196
  6.8 19.6 %copy-start = (s32[384]{0:T(512)S(1)}, s32[384]{0:T(512)}, u32[]{:S(2)}) copy-start(s32[384]{0:T(512)} %row_ref.3) | copy-start | bytes 4612
  6.8 3.4 %collective-permute-start.5 = (bf16[704,1024]{1,0:T(8,128)(2,1)S(1)}, bf16[704,1024]{1,0:T(8,128)(2,1)S(1)}, u32[]{:S(2)}, u32[]{:S(2)}) collective-permute-start(bf16[704,1024]{1,0:T(8,128)(2,1)S(1)} %shard_map.73), channel_id=1, source_target_pairs={{0,1},{1,0},{2,3},{3,2},{4,5},{5,4},{6,7},{7,6},{8,9},{9,8},{10,11... | collective-permute-start | bytes 4325384 | tf_op jit(solution)/shard_map/ppermute | solution.py:255
  15.8 17.8 %copy-start.2 = (s32[1,16]{1,0:T(1,128)S(1)}, s32[1,16]{1,0:T(1,128)}, u32[]{:S(2)}) copy-start(s32[1,16]{1,0:T(1,128)} %counts_ref.3) | copy-start | bytes 196
  15.8 49.4 %collective-permute-start.9 = (bf16[704,1024]{1,0:T(8,128)(2,1)S(1)}, bf16[704,1024]{1,0:T(8,128)(2,1)S(1)}, u32[]{:S(2)}, u32[]{:S(2)}) collective-permute-start(bf16[704,1024]{1,0:T(8,128)(2,1)S(1)} %shard_map.74.refs_6_), channel_id=1, source_target_pairs={{0,2},{1,3},{2,0},{3,1},{4,6},{5,7},{6,4},{7,5},{8,10},{9,11},{10,... | collective-permute-start | bytes 4325384 | tf_op jit(solution)/shard_map/ppermute | solution.py:259
  18.7 5.5 %collective-permute-start.4 = (s32[1,16]{1,0:T(1,128)S(1)}, s32[1,16]{1,0:T(1,128)S(1)}, u32[]{:S(2)}, u32[]{:S(2)}) collective-permute-start(s32[1,16]{1,0:T(1,128)S(1)} %copy-done.1), channel_id=1, source_target_pairs={{0,4},{4,8},{8,12},{12,0},{1,5},{5,9},{9,13},{13,1},{2,6},{6,10},{... | collective-permute-start | bytes 200 | tf_op jit(solution)/shard_map/ppermute | solution.py:252
  20.3 4.4 %collective-permute-start.3 = (s32[1,16]{1,0:T(1,128)S(1)}, s32[1,16]{1,0:T(1,128)S(1)}, u32[]{:S(2)}, u32[]{:S(2)}) collective-permute-start(s32[1,16]{1,0:T(1,128)S(1)} %copy-done.1), channel_id=1, source_target_pairs={{0,8},{4,12},{8,0},{12,4},{1,9},{5,13},{9,1},{13,5},{2,10},{6,14},... | collective-permute-start | bytes 200 | tf_op jit(solution)/shard_map/ppermute | solution.py:252
  22.9 3.5 %collective-permute-start.2 = (s32[1,16]{1,0:T(1,128)S(1)}, s32[1,16]{1,0:T(1,128)S(1)}, u32[]{:S(2)}, u32[]{:S(2)}) collective-permute-start(s32[1,16]{1,0:T(1,128)S(1)} %copy-done.1), channel_id=1, source_target_pairs={{0,12},{4,0},{8,4},{12,8},{1,13},{5,1},{9,5},{13,9},{2,14},{6,2},{... | collective-permute-start | bytes 200 | tf_op jit(solution)/shard_map/ppermute | solution.py:252
  29.7 28.3 %collective-permute-start.8 = (bf16[80,2048]{1,0:T(8,128)(2,1)}, bf16[80,2048]{1,0:T(8,128)(2,1)S(1)}, u32[]{:S(2)}, u32[]{:S(2)}) collective-permute-start(bf16[80,2048]{1,0:T(8,128)(2,1)} %get-tuple-element.34), channel_id=1, source_target_pairs={{0,12},{4,0},{8,4},{12,8},{1,13},{5,1},{9,5},{13,9},{2,14},{6,2},{... | collective-permute-start | bytes 983048 | tf_op jit(solution)/shard_map/ppermute | solution.py:252
  33.0 25.9 %collective-permute-start.7 = (bf16[80,2048]{1,0:T(8,128)(2,1)}, bf16[80,2048]{1,0:T(8,128)(2,1)}, u32[]{:S(2)}, u32[]{:S(2)}) collective-permute-start(bf16[80,2048]{1,0:T(8,128)(2,1)} %get-tuple-element.33), channel_id=1, source_target_pairs={{0,8},{4,12},{8,0},{12,4},{1,9},{5,13},{9,1},{13,5},{2,10},{6,14},... | collective-permute-start | bytes 983048 | tf_op jit(solution)/shard_map/ppermute | solution.py:252
  33.0 25.9 %collective-permute-start.6 = (bf16[80,2048]{1,0:T(8,128)(2,1)}, bf16[80,2048]{1,0:T(8,128)(2,1)}, u32[]{:S(2)}, u32[]{:S(2)}) collective-permute-start(bf16[80,2048]{1,0:T(8,128)(2,1)} %get-tuple-element.32), channel_id=1, source_target_pairs={{0,4},{4,8},{8,12},{12,0},{1,5},{5,9},{9,13},{13,1},{2,6},{6,10},{... | collective-permute-start | bytes 983048 | tf_op jit(solution)/shard_map/ppermute | solution.py:252
  39.3 9.1 %collective-permute-start = (bf16[704,1024]{1,0:T(8,128)(2,1)S(1)}, bf16[704,1024]{1,0:T(8,128)(2,1)S(1)}, u32[]{:S(2)}, u32[]{:S(2)}) collective-permute-start(bf16[704,1024]{1,0:T(8,128)(2,1)S(1)} %branch_1_fun.3.refs_3_), channel_id=1, source_target_pairs={{0,1},{1,0},{2,3},{3,2},{4,5},{5,4},{6,7},{7,6},{8,9},{9,8},{10,11... | collective-permute-start | bytes 4325384 | tf_op jit(solution)/shard_map/cond/branch_1_fun/ppermute | solution.py:255
  48.4 6.9 %collective-permute-start.1 = (bf16[704,2048]{1,0:T(8,128)(2,1)S(1)}, bf16[704,2048]{1,0:T(8,128)(2,1)}, u32[]{:S(2)}, u32[]{:S(2)}) collective-permute-start(bf16[704,2048]{1,0:T(8,128)(2,1)S(1)} %branch_1_fun.4.refs_4_), channel_id=1, source_target_pairs={{0,1},{1,0},{2,3},{3,2},{4,5},{5,4},{6,7},{7,6},{8,9},{9,8},{10,11... | collective-permute-start | bytes 8650760 | tf_op jit(solution)/shard_map/cond/branch_1_fun/ppermute | solution.py:255
  55.3 9.9 %copy-start.4 = (bf16[704,2048]{1,0:T(8,128)(2,1)S(1)}, bf16[704,2048]{1,0:T(8,128)(2,1)}, u32[]{:S(2)}) copy-start(bf16[704,2048]{1,0:T(8,128)(2,1)} %refs_1_.5) | copy-start | bytes 8650756
  55.3 34.2 %collective-permute-start.15 = (bf16[704,1024]{1,0:T(8,128)(2,1)}, bf16[704,1024]{1,0:T(8,128)(2,1)S(1)}, u32[]{:S(2)}, u32[]{:S(2)}) collective-permute-start(bf16[704,1024]{1,0:T(8,128)(2,1)} %get-tuple-element.35.refs_4_.refs_6_), channel_id=1, source_target_pairs={{0,2},{1,3},{2,0},{3,1},{4,6},{5,7},{6,4},{7,5},{8,10},{9,11},{10,... | collective-permute-start | bytes 4325384 | tf_op jit(solution)/shard_map/ppermute | solution.py:259
  59.0 20.5 %collective-permute-start.14 = (bf16[80,2048]{1,0:T(8,128)(2,1)S(1)}, bf16[80,2048]{1,0:T(8,128)(2,1)S(1)}, u32[]{:S(2)}, u32[]{:S(2)}) collective-permute-start(bf16[80,2048]{1,0:T(8,128)(2,1)S(1)} %get-tuple-element.41), channel_id=1, source_target_pairs={{0,4},{4,8},{8,12},{12,0},{1,5},{5,9},{9,13},{13,1},{2,6},{6,10},{... | collective-permute-start | bytes 983048 | tf_op jit(solution)/shard_map/ppermute | solution.py:252
  61.0 22.5 %collective-permute-start.13 = (bf16[80,2048]{1,0:T(8,128)(2,1)S(1)}, bf16[80,2048]{1,0:T(8,128)(2,1)S(1)}, u32[]{:S(2)}, u32[]{:S(2)}) collective-permute-start(bf16[80,2048]{1,0:T(8,128)(2,1)S(1)} %get-tuple-element.39), channel_id=1, source_target_pairs={{0,8},{4,12},{8,0},{12,4},{1,9},{5,13},{9,1},{13,5},{2,10},{6,14},... | collective-permute-start | bytes 983048 | tf_op jit(solution)/shard_map/ppermute | solution.py:252
  62.3 21.2 %collective-permute-start.12 = (bf16[80,2048]{1,0:T(8,128)(2,1)S(1)}, bf16[80,2048]{1,0:T(8,128)(2,1)S(1)}, u32[]{:S(2)}, u32[]{:S(2)}) collective-permute-start(bf16[80,2048]{1,0:T(8,128)(2,1)S(1)} %get-tuple-element.37), channel_id=1, source_target_pairs={{0,12},{4,0},{8,4},{12,8},{1,13},{5,1},{9,5},{13,9},{2,14},{6,2},{... | collective-permute-start | bytes 983048 | tf_op jit(solution)/shard_map/ppermute | solution.py:252
  68.4 1.3 %collective-permute-start.10 = (f32[16,704]{1,0:T(8,128)S(1)}, f32[16,704]{1,0:T(8,128)S(1)}, u32[]{:S(2)}, u32[]{:S(2)}) collective-permute-start(f32[16,704]{1,0:T(8,128)S(1)} %shard_map.76), channel_id=1, source_target_pairs={{0,1},{1,0},{2,3},{3,2},{4,5},{5,4},{6,7},{7,6},{8,9},{9,8},{10,11... | collective-permute-start | bytes 135176 | tf_op jit(solution)/shard_map/ppermute | solution.py:255
  69.6 20.4 %collective-permute-start.11 = (f32[16,704]{1,0:T(8,128)S(1)}, f32[16,704]{1,0:T(8,128)S(1)}, u32[]{:S(2)}, u32[]{:S(2)}) collective-permute-start(f32[16,704]{1,0:T(8,128)S(1)} %add.4.refs_4_.refs_0_), channel_id=1, source_target_pairs={{0,2},{1,3},{2,0},{3,1},{4,6},{5,7},{6,4},{7,5},{8,10},{9,11},{10,... | collective-permute-start | bytes 135176 | tf_op jit(solution)/shard_map/ppermute | solution.py:259

commit v6 on v5

--- a/solution.py
+++ b/solution.py
@@ -38,10 +38,11 @@
     return next(t for t in (512, 256, 128) if start % t == 0 and width % t == 0)
 
 
-def product(place, acts, weight, shift, same_core, start, width, chips, add=None, after=(), into=None, total=None, at=0, weight_of=CHEAP):
+def product(place, acts, weight, shift, same_core, start, width, chips, add=None, after=(), weight_of=CHEAP):
     rows, depth = acts.shape
     block = weight.shape[1] // (chips * CORES)
-    tile = tile_of(math.gcd(start, at), width)
+    adds = [] if add is None else [add]
+    tile = tile_of(start, width)
     stride, first = block // tile, start // tile
 
     def columns(j, place_ref):
@@ -52,39 +53,29 @@
     def kernel(*refs):
         acts_ref, weight_ref = refs[1], refs[2]
         value = jnp.dot(acts_ref[...], weight_ref[...], preferred_element_type=jnp.float32)
-        if add is not None:
+        if adds:
             value = value + refs[3][...].astype(jnp.float32)
         refs[-1][...] = value.astype(jnp.bfloat16)
 
-    operands = [acts, weight]
+    operands = [acts, weight, *adds, *after]
     specs = [WHOLE, pl.BlockSpec((depth, tile), columns)]
-    if add is not None:
-        operands.append(add)
-        specs.append(pl.BlockSpec((rows, tile), lambda j, p: (0, j)))
-    aliases = {}
-    if into is not None:
-        aliases = {len(operands) + 1: 0}
-        operands.append(into)
-        specs.append(ANY)
-    operands += list(after)
+    specs += [pl.BlockSpec((rows, tile), lambda j, p: (0, j))] * len(adds)
     specs += [ANY] * len(after)
-    place_at = at // tile
     return pl.pallas_call(
         kernel,
         grid_spec=pltpu.PrefetchScalarGridSpec(
             num_scalar_prefetch=1,
             grid=(width // tile,),
             in_specs=specs,
-            out_specs=pl.BlockSpec((rows, tile), lambda j, p: (0, place_at + j)),
+            out_specs=pl.BlockSpec((rows, tile), lambda j, p: (0, j)),
         ),
-        out_shape=jax.ShapeDtypeStruct((rows, total or width), jnp.bfloat16),
-        input_output_aliases=aliases,
+        out_shape=jax.ShapeDtypeStruct((rows, width), jnp.bfloat16),
         compiler_params=PARAMS,
         cost_estimate=weight_of,
     )(place, *operands)
 
 
-def pick(ids, store_row, stores, ways, cap, after=()):
+def pick(ids, store_row, stores, ways, cap, after=(), weight_of=CHEAP):
     per_owner, rank, width = stores[0].shape
     n_after, n_stores = len(after), len(stores)
 
@@ -121,7 +112,7 @@
         out_shape=[shape] * (n_stores * ways),
         scratch_shapes=[pltpu.SemaphoreType.DMA((n_stores * ways,))],
         compiler_params=pltpu.CompilerParams(vmem_limit_bytes=50 * 1024 * 1024),
-        cost_estimate=CHEAP,
+        cost_estimate=weight_of,
     )(*ids, store_row, *stores, *after)
     return outs
 
@@ -177,8 +168,8 @@
     )(counts, ids, store_row, acts, *downs, *after)
 
 
-def finish(lows, ups, base, sends, counts, ids, store_row, cap, per_owner):
-    rows, block = base.shape
+def finish(lows, ups, sends, counts, ids, store_row, cap, per_owner):
+    rows, block = lows[0].shape[1], sum(send[0].shape[1] for send in sends)
     ways, depth = len(ups), ups[0].shape[0]
     wide = ways * depth
     tile = math.gcd(*[send[0].shape[1] for send in sends], 1024)
@@ -186,7 +177,7 @@
 
     def kernel(counts_ref, id_ref, row_ref, *refs):
         low_refs, up_refs = refs[:n_low], refs[n_low : n_low + ways][::-1]
-        base_ref, *sent_refs = refs[n_low + ways : -2]
+        sent_refs = refs[n_low + ways : -2]
         out_ref, low_ref = refs[-2:]
         step = pl.program_id(0)
 
@@ -204,8 +195,8 @@
         def write(arrived):
             blocks = jnp.concatenate([ref[...] for ref in up_refs], axis=0)
             delta = jnp.dot(low_ref[...], blocks, preferred_element_type=jnp.float32)
-            total = base_ref[...].astype(jnp.float32)
-            for ref in arrived:
+            total = arrived[0][...].astype(jnp.float32)
+            for ref in arrived[1:]:
                 total = total + ref[...].astype(jnp.float32)
             out_ref[...] = (total + adapter_scale * delta).astype(jnp.bfloat16)
 
@@ -216,7 +207,7 @@
             first, at = first + steps, at + len(send)
 
     here = pl.BlockSpec((rows, tile), lambda j: (0, j))
-    specs = [SMEM] * 3 + [WHOLE] * n_low + [pl.BlockSpec((depth, tile), lambda j: (0, j))] * ways + [here]
+    specs = [SMEM] * 3 + [WHOLE] * n_low + [pl.BlockSpec((depth, tile), lambda j: (0, j))] * ways
     first = 0
     for send in sends:
         steps = send[0].shape[1] // tile
@@ -232,7 +223,7 @@
         scratch_shapes=[pltpu.VMEM((rows, wide), jnp.bfloat16)],
         compiler_params=PARAMS,
         cost_estimate=CHEAP,
-    )(counts, ids, store_row, *lows, *ups[::-1], base, *[array for send in sends for array in send])
+    )(counts, ids, store_row, *lows, *ups[::-1], *[array for send in sends for array in send])
 
 
 def apart(live, function, *operands):
@@ -281,28 +272,41 @@
         last = mul(shift, False, *tail, after=(last,))
         crossed = to_core(last)
         if own:
-            last = mul(0, False, 0, block, after=(last,))
+            last = mul(0, False, 0, block // 2, after=(last,))
             own_crossed = to_core(lax.optimization_barrier((last, crossed))[0])
         summed = mul(shift, True, *tail, add=crossed, after=(last,))
         return (summed, own_crossed) if own else (summed,)
+
+    def rest(acts, weight, place, chip_low, crossed):
+        mul = functools.partial(product, place, acts, weight, 0, chips=chips)
+        half = block // 2
+        last = mul(False, half, half, after=(chip_low,))
+        second = to_core(last)
+        first = mul(True, 0, half, add=crossed, after=(last,))
+        lows = [to_chip(lax.optimization_barrier((chip_low, second, first))[0], shift) for shift in range(1, chips)]
+        return first, mul(True, half, half, add=second, after=(first,)), *lows
 
     for shift in range(1, chips) if tail else ():
         own = shift == chips - 1
         last, *others = apart(live, functools.partial(sums, shift=shift, own=own), acts, weight, place, last)
         tails.append(to_chip(last, shift))
-    own_crossed = others[0] if tail else to_core(mul(0, False, 0, block, after=(last,)))
+    ups = pick(all_ids, store_row, [up], ways, cap, after=(last,), weight_of=weigh(0))
+    if not tail:
+        others = [to_core(mul(0, False, 0, block, after=(last,)))]
 
     low = low_parts(acts, far_downs, counts, ids, store_row, cap, per_owner, after=(last, *heads))
-    ups = pick(all_ids, store_row, [up], ways, cap, after=(last,))
     far_ups = [ups[0]]
     for s in range(1, ways):
         held, *_ = lax.optimization_barrier((ups[s], last, far_downs[s]))
         far_ups.append(along_dp(held, s))
     chip_low = low + to_core(low)
-    lows = [chip_low] + [to_chip(chip_low, shift) for shift in range(1, chips)]
-    base = mul(0, True, 0, block, add=own_crossed, after=(chip_low,), weight_of=weigh(0))
-    sends = [heads, tails] if tail else [heads]
-    return finish(lows, far_ups, base, sends, counts, ids, store_row, cap, per_owner)
+    if tail:
+        first, second, *lows = apart(live, rest, acts, weight, place, chip_low, others[0])
+        sends = [[first, *heads], [second, *tails]]
+    else:
+        lows = [to_chip(chip_low, shift) for shift in range(1, chips)]
+        sends = [[mul(0, True, 0, block, add=others[0], after=(chip_low,)), *heads]]
+    return finish([chip_low, *lows], far_ups, sends, counts, ids, store_row, cap, per_owner)
 
 
 def solution(mesh):

time: 94.7 us -> 103 us (1.088)
  Pallas kernels: 55.4 us -> 62.7 us
  waiting for transfers between devices: 17.8 us -> 10.6 us
  starting transfers between devices: 20.9 us -> 27.8 us
    ppermute x9, starting transfers between devices: 15.7 us -> 22.9 us  [along_dp(): lax.ppermute(array, 'dp', [(i, (i + shift) % ways) for i in range(ways)])]
    ppermute x3, waiting for transfers between devices: 6.59 us -> 0.01 us  [to_chip(): lax.ppermute(array, 'tensor', [(i, (i + CORES * shift) % size) for i in r...]
    pallas_call x6 -> x8, Pallas kernels: 42.4 us -> 47.6 us  [product(): pl.pallas_call(kernel, grid_spec=pltpu.PrefetchScalarGridSpec(num_scalar_...]
    pallas_call x1, Pallas kernels: 4.32 us -> 5.66 us  [finish(): pl.pallas_call(kernel, grid=(block // tile,), in_specs=specs, out_specs=h...]
    ppermute x4 -> x5, waiting for transfers between devices: 4.11 us -> 4.11 us  [to_core(): lax.ppermute(array, 'tensor', [(i, i ^ 1) for i in range(chips * CORES)])]
  transfers between devices with their start and end apart: 16 -> 17, of which waited for: 8 -> 6; matrix products, arithmetic and copies ran while one was open for 0% -> 0% of each run, Pallas kernels for 41% -> 44%
where the time goes in v6:
time: 103 us; the launch traced here: 102 us
  Pallas kernels  62.7 us (61%)
  starting transfers between devices  27.8 us (27%)
  waiting for transfers between devices  10.6 us (10%)
    pallas_call x8, Pallas kernels, product(): pl.pallas_call(kernel, grid_spec=pltpu.PrefetchScalarGridSpec(num_scalar_...  47.6 us
    ppermute x9, starting transfers between devices, along_dp(): lax.ppermute(array, 'dp', [(i, (i + shift) % ways) for i in range(ways)])  22.9 us
    ppermute x9, waiting for transfers between devices, along_dp(): lax.ppermute(array, 'dp', [(i, (i + shift) % ways) for i in range(ways)])  6.52 us
    pallas_call x2, Pallas kernels, pick(): pl.pallas_call(kernel, in_specs=[SMEM] * (ways + 1) + [HBM] * n_stores +...  6.39 us
    pallas_call x1, Pallas kernels, finish(): pl.pallas_call(kernel, grid=(block // tile,), in_specs=specs, out_specs=h...  5.66 us
    ppermute x5, waiting for transfers between devices, to_core(): lax.ppermute(array, 'tensor', [(i, i ^ 1) for i in range(chips * CORES)])  4.11 us
    ppermute x3, starting transfers between devices, to_chip(): lax.ppermute(array, 'tensor', [(i, (i + CORES * shift) % size) for i in r...  3.51 us
    pallas_call x1, Pallas kernels, low_parts(): pl.pallas_call(kernel, in_specs=[SMEM] * 3 + [WHOLE] * (1 + ways) + [ANY]...  3.1 us
  transfers between devices with their start and end apart: 17, of which 6 were waited for; matrix products, arithmetic and copies ran while one was open for 0% of the time, Pallas kernels for 44%

profile of v6, /device:TPU:0, one launch (start us, length us, event | category | flops | bytes accessed | tf_op | source)
XLA Modules:
  0.0 102.1 jit_solution(16486385523435979373)
XLA Ops:
  0.0 0.1 pad_add_fusion.refs_0_
  0.1 6.7 %shard_map.73 = bf16[704,1024]{1,0:T(8,128)(2,1)S(1)} custom-call(s32[2]{0:T(128)S(1)} %pad_add_fusion.refs_0_, bf16[704,2048]{1,0:T(8,128)(2,1)} %acts_ref.1, bf16[2048,8192]{1,0:T(8,128)(2,1)} %refs_2_.3), custom_call_target="tpu_custom_call" | custom-call | flops 1000 | bytes 1000 | tf_op jit(solution)/shard_map/pallas_call | solution.py:64
  6.8 0.0 copy-start.1
  6.8 0.0 copy-start
  6.8 0.5 collective-permute-start.7
  7.4 2.8 %collective-permute-done.7.refs_3_ = bf16[704,1024]{1,0:T(8,128)(2,1)S(1)} collective-permute-done((bf16[704,1024]{1,0:T(8,128)(2,1)S(1)}, bf16[704,1024]{1,0:T(8,128)(2,1)S(1)}, u32[]{:S(2)}, u32[]{:S(2)}) %collective-permute-start.7) | collective-permute-done | bytes 1441824 | tf_op jit(solution)/shard_map/ppermute | solution.py:246
  10.2 5.6 %shard_map.74.refs_6_ = bf16[704,1024]{1,0:T(8,128)(2,1)S(1)} custom-call(s32[2]{0:T(128)S(1)} %pad_add_fusion.refs_0_, bf16[704,2048]{1,0:T(8,128)(2,1)S(1)} %copy-done.3, bf16[2048,8192]{1,0:T(8,128)(2,1)} %refs_2_.3, bf16[704,1024]{1,0:T(8,128)(2,1)S(1)} %collective-permute-done.7.refs_3_), custom_call_target="tpu_custom_call" | custom-call | flops 1000 | bytes 1000 | tf_op jit(solution)/shard_map/pallas_call | solution.py:64
  15.8 0.0 copy-start.2
  15.8 2.9 %collective-permute-start.11 = (bf16[704,1024]{1,0:T(8,128)(2,1)S(1)}, bf16[704,1024]{1,0:T(8,128)(2,1)S(1)}, u32[]{:S(2)}, u32[]{:S(2)}) collective-permute-start(bf16[704,1024]{1,0:T(8,128)(2,1)S(1)} %shard_map.74.refs_6_), channel_id=1, source_target_pairs={{0,2},{1,3},{2,0},{3,1},{4,6},{5,7},{6,4},{7,5},{8,10},{9,11},{10,... | collective-permute-start | bytes 4325384 | tf_op jit(solution)/shard_map/ppermute | solution.py:250
  18.7 3.6 %collective-permute-start.4 = (s32[1,16]{1,0:T(1,128)S(1)}, s32[1,16]{1,0:T(1,128)S(1)}, u32[]{:S(2)}, u32[]{:S(2)}) collective-permute-start(s32[1,16]{1,0:T(1,128)S(1)} %copy-done.1), channel_id=1, source_target_pairs={{0,12},{4,0},{8,4},{12,8},{1,13},{5,1},{9,5},{13,9},{2,14},{6,2},{... | collective-permute-start | bytes 200 | tf_op jit(solution)/shard_map/ppermute | solution.py:243
  22.3 0.0 collective-permute-start.5
  22.4 1.0 collective-permute-start.6
  23.4 0.3 collective-permute-done.4.refs_1_
  23.6 3.1 %collective-permute-done.5.refs_2_ = s32[1,16]{1,0:T(1,128)S(1)} collective-permute-done((s32[1,16]{1,0:T(1,128)S(1)}, s32[1,16]{1,0:T(1,128)S(1)}, u32[]{:S(2)}, u32[]{:S(2)}) %collective-permute-start.5) | collective-permute-done | bytes 96 | tf_op jit(solution)/shard_map/ppermute | solution.py:243
  26.8 0.9 collective-permute-done.6.refs_3_
  27.7 3.2 %shard_map.75 = (bf16[80,2048]{1,0:T(8,128)(2,1)S(1)}, bf16[80,2048]{1,0:T(8,128)(2,1)}, bf16[80,2048]{1,0:T(8,128)(2,1)}, bf16[80,2048]{1,0:T(8,128)(2,1)}) custom-call(s32[1,16]{1,0:T(1,128)S(1)} %copy-done.1, s32[1,16]{1,0:T(1,128)S(1)} %collective-permute-done.4.refs_1_, s32[1,16]{1,0:T(1,128)S(1)} %collective-permute-done.5.refs_2_, ...), custom_call_target="tpu_custom_call" | custom-call | flops 1000 | bytes 1000 | tf_op jit(solution)/shard_map/pallas_call | solution.py:108
  30.9 0.6 collective-permute-start.10
  31.5 0.6 collective-permute-start.9
  32.2 1.9 %collective-permute-start.8 = (bf16[80,2048]{1,0:T(8,128)(2,1)}, bf16[80,2048]{1,0:T(8,128)(2,1)}, u32[]{:S(2)}, u32[]{:S(2)}) collective-permute-start(bf16[80,2048]{1,0:T(8,128)(2,1)} %get-tuple-element.51), channel_id=1, source_target_pairs={{0,4},{4,8},{8,12},{12,0},{1,5},{5,9},{9,13},{13,1},{2,6},{6,10},{... | collective-permute-start | bytes 983048 | tf_op jit(solution)/shard_map/ppermute | solution.py:243
  34.2 18.2 %conditional.2 = (bf16[704,1024]{1,0:T(8,128)(2,1)}, bf16[704,1024]{1,0:T(8,128)(2,1)}) conditional(s32[]{:T(128)} %bitcast.2, () %tuple.26, (s32[2]{0:T(128)S(1)}, bf16[704,2048]{1,0:T(8,128)(2,1)S(1)}, bf16[2048,8192]{1,0:T(8,128)(2,1)}, bf16[80,2048]{1,0:T(8,128)(2,1)S(1)}) %tuple.37), branch_computations={%region_0.1_spmd, %region_1.2_spmd} | conditional | flops 3000 | bytes 11537432 | solution.py:231
  34.2 5.6 %branch_1_fun.6.refs_3_ = bf16[704,1024]{1,0:T(8,128)(2,1)S(1)} custom-call(s32[2]{0:T(128)S(1)} %get-tuple-element.23.refs_0_, bf16[704,2048]{1,0:T(8,128)(2,1)S(1)} %get-tuple-element.24.refs_1_, bf16[2048,8192]{1,0:T(8,128)(2,1)} %get-tuple-element.25.refs_2_, bf16[80,2048]{1,0:T(8,128)(2,1)S(1)} %get-tuple-element.26.refs_3_), custom_call_target="tpu_custom_call" | custom-call | flops 1000 | bytes 1000 | tf_op jit(solution)/shard_map/cond/branch_1_fun/pallas_call | solution.py:64
  39.8 0.1 collective-permute-start
  39.8 5.6 %branch_1_fun.7.refs_4_ = bf16[704,1024]{1,0:T(8,128)(2,1)S(1)} custom-call(s32[2]{0:T(128)S(1)} %get-tuple-element.23.refs_0_, bf16[704,2048]{1,0:T(8,128)(2,1)S(1)} %get-tuple-element.24.refs_1_, bf16[2048,8192]{1,0:T(8,128)(2,1)} %get-tuple-element.25.refs_2_, bf16[704,1024]{1,0:T(8,128)(2,1)S(1)} %branch_1_fun.6.refs_3_), custom_call_target="tpu_custom_call" | custom-call | flops 1000 | bytes 1000 | tf_op jit(solution)/shard_map/cond/branch_1_fun/pallas_call | solution.py:64
  45.4 0.0 collective-permute-done.refs_3_
  45.4 0.6 collective-permute-start.1
  46.0 6.3 %branch_1_fun.8 = bf16[704,1024]{1,0:T(8,128)(2,1)} custom-call(s32[2]{0:T(128)S(1)} %get-tuple-element.23.refs_0_, bf16[704,2048]{1,0:T(8,128)(2,1)S(1)} %get-tuple-element.24.refs_1_, bf16[2048,8192]{1,0:T(8,128)(2,1)} %get-tuple-element.25.refs_2_, bf16[704,1024]{1,0:T(8,128)(2,1)S(1)} %collective-permute-done.refs_3_, ...), custom_call_target="tpu_custom_call" | custom-call | flops 1000 | bytes 1000 | tf_op jit(solution)/shard_map/cond/branch_1_fun/pallas_call | solution.py:64
  52.3 0.6 collective-permute-start.16
  52.9 3.2 %shard_map.77 = (bf16[80,2048]{1,0:T(8,128)(2,1)S(1)}, bf16[80,2048]{1,0:T(8,128)(2,1)}, bf16[80,2048]{1,0:T(8,128)(2,1)}, bf16[80,2048]{1,0:T(8,128)(2,1)}) custom-call(s32[1,16]{1,0:T(1,128)S(1)} %copy-done.1, s32[1,16]{1,0:T(1,128)S(1)} %collective-permute-done.4.refs_1_, s32[1,16]{1,0:T(1,128)S(1)} %collective-permute-done.5.refs_2_, ...), custom_call_target="tpu_custom_call" | custom-call | flops 1000 | bytes 1000 | tf_op jit(solution)/shard_map/pallas_call | solution.py:108
  56.1 0.0 collective-permute-done.10.refs_3_
  56.2 1.9 %collective-permute-start.13 = (bf16[80,2048]{1,0:T(8,128)(2,1)}, bf16[80,2048]{1,0:T(8,128)(2,1)S(1)}, u32[]{:S(2)}, u32[]{:S(2)}) collective-permute-start(bf16[80,2048]{1,0:T(8,128)(2,1)} %get-tuple-element.58), channel_id=1, source_target_pairs={{0,12},{4,0},{8,4},{12,8},{1,13},{5,1},{9,5},{13,9},{2,14},{6,2},{... | collective-permute-start | bytes 983048 | tf_op jit(solution)/shard_map/ppermute | solution.py:243
  58.1 2.2 %collective-permute-done.9.refs_2_ = bf16[80,2048]{1,0:T(8,128)(2,1)} collective-permute-done((bf16[80,2048]{1,0:T(8,128)(2,1)}, bf16[80,2048]{1,0:T(8,128)(2,1)}, u32[]{:S(2)}, u32[]{:S(2)}) %collective-permute-start.9) | collective-permute-done | bytes 327712 | tf_op jit(solution)/shard_map/ppermute | solution.py:243
  60.3 0.0 collective-permute-start.14
  60.3 0.0 collective-permute-done.8.refs_1_
  60.3 13.1 %collective-permute-start.15 = (bf16[80,2048]{1,0:T(8,128)(2,1)}, bf16[80,2048]{1,0:T(8,128)(2,1)}, u32[]{:S(2)}, u32[]{:S(2)}) collective-permute-start(bf16[80,2048]{1,0:T(8,128)(2,1)} %get-tuple-element.62), channel_id=1, source_target_pairs={{0,4},{4,8},{8,12},{12,0},{1,5},{5,9},{9,13},{13,1},{2,6},{6,10},{... | collective-permute-start | bytes 983048 | tf_op jit(solution)/shard_map/ppermute | solution.py:243
  73.4 3.1 %shard_map.76 = f32[16,704]{1,0:T(8,128)S(1)} custom-call(s32[1,16]{1,0:T(1,128)S(1)} %copy-done.2, s32[1,16]{1,0:T(1,128)S(1)} %copy-done.1, s32[384]{0:T(512)S(1)} %copy-done, bf16[704,2048]{1,0:T(8,128)(2,1)S(1)} %copy-done.4, bf16[80,2048]{1,0:T(8,128)(2,1)S(1)} %copy-done.7, bf16[80,2048]{1,0:T(8,128)(2,1)} %collective-permute-done.8.refs_1_, ...), custom_call_target="tpu_custom_call" | custom-call | flops 22000001024 | bytes 1000 | tf_op jit(solution)/shard_map/pallas_call | solution.py:161
  76.5 0.0 collective-permute-start.12
  76.5 1.3 %collective-permute-done.12 = f32[16,704]{1,0:T(8,128)S(1)} collective-permute-done((f32[16,704]{1,0:T(8,128)S(1)}, f32[16,704]{1,0:T(8,128)S(1)}, u32[]{:S(2)}, u32[]{:S(2)}) %collective-permute-start.12) | collective-permute-done | bytes 45088 | tf_op jit(solution)/shard_map/ppermute | solution.py:246
  77.8 0.6 copy-done.5
  78.4 18.0 %conditional.3 = (bf16[704,1024]{1,0:T(8,128)(2,1)}, bf16[704,1024]{1,0:T(8,128)(2,1)S(1)}, f32[16,704]{1,0:T(8,128)}) conditional(s32[]{:T(128)} %bitcast.2, () %tuple.28, (s32[2]{0:T(128)S(1)}, bf16[704,2048]{1,0:T(8,128)(2,1)S(1)}, bf16[2048,8192]{1,0:T(8,128)(2,1)}, f32[16,704]{1,0:T(8,128)S(1)}, bf16[704,1024]{1,0:T(8,128)(2,1)}) %tuple.38), branch_computations={%region_2.3_spmd, %region_3.4_spmd} | conditional | flops 3000 | bytes 5950496 | solution.py:231
  78.4 5.6 %branch_1_fun.9.refs_4_ = bf16[704,1024]{1,0:T(8,128)(2,1)S(1)} custom-call(s32[2]{0:T(128)S(1)} %get-tuple-element.28.refs_0_, bf16[704,2048]{1,0:T(8,128)(2,1)S(1)} %get-tuple-element.29.refs_1_, bf16[2048,8192]{1,0:T(8,128)(2,1)} %get-tuple-element.30.refs_2_, f32[16,704]{1,0:T(8,128)S(1)} %get-tuple-element.33.refs_3_), custom_call_target="tpu_custom_call" | custom-call | flops 1000 | bytes 1000 | tf_op jit(solution)/shard_map/cond/branch_1_fun/pallas_call | solution.py:64
  84.0 0.2 collective-permute-start.2
  84.2 6.6 %branch_1_fun.10.refs_4_ = bf16[704,1024]{1,0:T(8,128)(2,1)} custom-call(s32[2]{0:T(128)S(1)} %get-tuple-element.28.refs_0_, bf16[704,2048]{1,0:T(8,128)(2,1)S(1)} %get-tuple-element.29.refs_1_, bf16[2048,8192]{1,0:T(8,128)(2,1)} %get-tuple-element.30.refs_2_, bf16[704,1024]{1,0:T(8,128)(2,1)} %get-tuple-element.31.refs_3_, ...), custom_call_target="tpu_custom_call" | custom-call | flops 1000 | bytes 1000 | tf_op jit(solution)/shard_map/cond/branch_1_fun/pallas_call | solution.py:64
  90.8 5.6 %branch_1_fun.11 = bf16[704,1024]{1,0:T(8,128)(2,1)S(1)} custom-call(s32[2]{0:T(128)S(1)} %get-tuple-element.28.refs_0_, bf16[704,2048]{1,0:T(8,128)(2,1)S(1)} %get-tuple-element.29.refs_1_, bf16[2048,8192]{1,0:T(8,128)(2,1)} %get-tuple-element.30.refs_2_, bf16[704,1024]{1,0:T(8,128)(2,1)S(1)} %collective-permute-done.2.refs_3_, ...), custom_call_target="tpu_custom_call" | custom-call | flops 1000 | bytes 1000 | tf_op jit(solution)/shard_map/cond/branch_1_fun/pallas_call | solution.py:64
  96.4 0.0 collective-permute-done.3
  96.4 0.0 collective-permute-done.13.refs_2_
  96.5 0.0 collective-permute-done.14.refs_3_
  96.5 0.0 collective-permute-done.16.refs_9_
  96.5 5.7 %shard_map.78 = bf16[704,2048]{1,0:T(8,128)(2,1)} custom-call(s32[1,16]{1,0:T(1,128)S(1)} %copy-done.2, s32[1,16]{1,0:T(1,128)S(1)} %copy-done.1, s32[384]{0:T(512)S(1)} %copy-done, f32[16,704]{1,0:T(8,128)} %copy-done.5, f32[16,704]{1,0:T(8,128)} %get-tuple-element.56.refs_1_, bf16[80,2048]{1,0:T(8,128)(2,1)S(1)} %collective-permute-done.13.refs_2_, ...), custom_call_target="tpu_custom_call" | custom-call | flops 1000 | bytes 1000 | tf_op jit(solution)/shard_map/pallas_call | solution.py:217
  (18 shorter events, 0.0 us)
Async XLA Ops:
  0.1 10.1 %copy-start.3 = (bf16[704,2048]{1,0:T(8,128)(2,1)S(1)}, bf16[704,2048]{1,0:T(8,128)(2,1)}, u32[]{:S(2)}) copy-start(bf16[704,2048]{1,0:T(8,128)(2,1)} %acts_ref.1) | copy-start | bytes 8650756
  6.8 11.9 %copy-start.1 = (s32[1,16]{1,0:T(1,128)S(1)}, s32[1,16]{1,0:T(1,128)}, u32[]{:S(2)}) copy-start(s32[1,16]{1,0:T(1,128)} %id_ref.3) | copy-start | bytes 196
  6.8 20.9 %copy-start = (s32[384]{0:T(512)S(1)}, s32[384]{0:T(512)}, u32[]{:S(2)}) copy-start(s32[384]{0:T(512)} %row_ref.3) | copy-start | bytes 4612
  6.8 3.4 %collective-permute-start.7 = (bf16[704,1024]{1,0:T(8,128)(2,1)S(1)}, bf16[704,1024]{1,0:T(8,128)(2,1)S(1)}, u32[]{:S(2)}, u32[]{:S(2)}) collective-permute-start(bf16[704,1024]{1,0:T(8,128)(2,1)S(1)} %shard_map.73), channel_id=1, source_target_pairs={{0,1},{1,0},{2,3},{3,2},{4,5},{5,4},{6,7},{7,6},{8,9},{9,8},{10,11... | collective-permute-start | bytes 4325384 | tf_op jit(solution)/shard_map/ppermute | solution.py:246
  15.8 18.3 %copy-start.2 = (s32[1,16]{1,0:T(1,128)S(1)}, s32[1,16]{1,0:T(1,128)}, u32[]{:S(2)}) copy-start(s32[1,16]{1,0:T(1,128)} %counts_ref.3) | copy-start | bytes 196
  15.8 57.6 %collective-permute-start.11 = (bf16[704,1024]{1,0:T(8,128)(2,1)S(1)}, bf16[704,1024]{1,0:T(8,128)(2,1)S(1)}, u32[]{:S(2)}, u32[]{:S(2)}) collective-permute-start(bf16[704,1024]{1,0:T(8,128)(2,1)S(1)} %shard_map.74.refs_6_), channel_id=1, source_target_pairs={{0,2},{1,3},{2,0},{3,1},{4,6},{5,7},{6,4},{7,5},{8,10},{9,11},{10,... | collective-permute-start | bytes 4325384 | tf_op jit(solution)/shard_map/ppermute | solution.py:250
  18.7 4.9 %collective-permute-start.4 = (s32[1,16]{1,0:T(1,128)S(1)}, s32[1,16]{1,0:T(1,128)S(1)}, u32[]{:S(2)}, u32[]{:S(2)}) collective-permute-start(s32[1,16]{1,0:T(1,128)S(1)} %copy-done.1), channel_id=1, source_target_pairs={{0,12},{4,0},{8,4},{12,8},{1,13},{5,1},{9,5},{13,9},{2,14},{6,2},{... | collective-permute-start | bytes 200 | tf_op jit(solution)/shard_map/ppermute | solution.py:243
  22.3 4.4 %collective-permute-start.5 = (s32[1,16]{1,0:T(1,128)S(1)}, s32[1,16]{1,0:T(1,128)S(1)}, u32[]{:S(2)}, u32[]{:S(2)}) collective-permute-start(s32[1,16]{1,0:T(1,128)S(1)} %copy-done.1), channel_id=1, source_target_pairs={{0,8},{4,12},{8,0},{12,4},{1,9},{5,13},{9,1},{13,5},{2,10},{6,14},... | collective-permute-start | bytes 200 | tf_op jit(solution)/shard_map/ppermute | solution.py:243
  22.4 5.3 %collective-permute-start.6 = (s32[1,16]{1,0:T(1,128)S(1)}, s32[1,16]{1,0:T(1,128)S(1)}, u32[]{:S(2)}, u32[]{:S(2)}) collective-permute-start(s32[1,16]{1,0:T(1,128)S(1)} %copy-done.1), channel_id=1, source_target_pairs={{0,4},{4,8},{8,12},{12,0},{1,5},{5,9},{9,13},{13,1},{2,6},{6,10},{... | collective-permute-start | bytes 200 | tf_op jit(solution)/shard_map/ppermute | solution.py:243
  30.9 3.3 %copy-start.6 = (bf16[80,2048]{1,0:T(8,128)(2,1)}, bf16[80,2048]{1,0:T(8,128)(2,1)S(1)}, u32[]{:S(2)}) copy-start(bf16[80,2048]{1,0:T(8,128)(2,1)S(1)} %get-tuple-element.50.refs_0_) | copy-start | bytes 983044
  30.9 25.3 %collective-permute-start.10 = (bf16[80,2048]{1,0:T(8,128)(2,1)}, bf16[80,2048]{1,0:T(8,128)(2,1)}, u32[]{:S(2)}, u32[]{:S(2)}) collective-permute-start(bf16[80,2048]{1,0:T(8,128)(2,1)} %get-tuple-element.53), channel_id=1, source_target_pairs={{0,12},{4,0},{8,4},{12,8},{1,13},{5,1},{9,5},{13,9},{2,14},{6,2},{... | collective-permute-start | bytes 983048 | tf_op jit(solution)/shard_map/ppermute | solution.py:243
  31.5 28.8 %collective-permute-start.9 = (bf16[80,2048]{1,0:T(8,128)(2,1)}, bf16[80,2048]{1,0:T(8,128)(2,1)}, u32[]{:S(2)}, u32[]{:S(2)}) collective-permute-start(bf16[80,2048]{1,0:T(8,128)(2,1)} %get-tuple-element.52), channel_id=1, source_target_pairs={{0,8},{4,12},{8,0},{12,4},{1,9},{5,13},{9,1},{13,5},{2,10},{6,14},... | collective-permute-start | bytes 983048 | tf_op jit(solution)/shard_map/ppermute | solution.py:243
  32.2 28.1 %collective-permute-start.8 = (bf16[80,2048]{1,0:T(8,128)(2,1)}, bf16[80,2048]{1,0:T(8,128)(2,1)}, u32[]{:S(2)}, u32[]{:S(2)}) collective-permute-start(bf16[80,2048]{1,0:T(8,128)(2,1)} %get-tuple-element.51), channel_id=1, source_target_pairs={{0,4},{4,8},{8,12},{12,0},{1,5},{5,9},{9,13},{13,1},{2,6},{6,10},{... | collective-permute-start | bytes 983048 | tf_op jit(solution)/shard_map/ppermute | solution.py:243
  39.8 5.7 %collective-permute-start = (bf16[704,1024]{1,0:T(8,128)(2,1)S(1)}, bf16[704,1024]{1,0:T(8,128)(2,1)S(1)}, u32[]{:S(2)}, u32[]{:S(2)}) collective-permute-start(bf16[704,1024]{1,0:T(8,128)(2,1)S(1)} %branch_1_fun.6.refs_3_), channel_id=1, source_target_pairs={{0,1},{1,0},{2,3},{3,2},{4,5},{5,4},{6,7},{7,6},{8,9},{9,8},{10,11... | collective-permute-start | bytes 4325384 | tf_op jit(solution)/shard_map/cond/branch_1_fun/ppermute | solution.py:246
  45.4 6.9 %collective-permute-start.1 = (bf16[704,1024]{1,0:T(8,128)(2,1)S(1)}, bf16[704,1024]{1,0:T(8,128)(2,1)}, u32[]{:S(2)}, u32[]{:S(2)}) collective-permute-start(bf16[704,1024]{1,0:T(8,128)(2,1)S(1)} %branch_1_fun.7.refs_4_), channel_id=1, source_target_pairs={{0,1},{1,0},{2,3},{3,2},{4,5},{5,4},{6,7},{7,6},{8,9},{9,8},{10,11... | collective-permute-start | bytes 4325384 | tf_op jit(solution)/shard_map/cond/branch_1_fun/ppermute | solution.py:246
  52.3 21.1 %copy-start.4 = (bf16[704,2048]{1,0:T(8,128)(2,1)S(1)}, bf16[704,2048]{1,0:T(8,128)(2,1)}, u32[]{:S(2)}) copy-start(bf16[704,2048]{1,0:T(8,128)(2,1)} %acts_ref.1) | copy-start | bytes 8650756
  52.3 21.1 %copy-start.7 = (bf16[80,2048]{1,0:T(8,128)(2,1)S(1)}, bf16[80,2048]{1,0:T(8,128)(2,1)}, u32[]{:S(2)}) copy-start(bf16[80,2048]{1,0:T(8,128)(2,1)} %copy-done.6) | copy-start | bytes 983044
  52.3 44.1 %collective-permute-start.16 = (bf16[704,1024]{1,0:T(8,128)(2,1)}, bf16[704,1024]{1,0:T(8,128)(2,1)}, u32[]{:S(2)}, u32[]{:S(2)}) collective-permute-start(bf16[704,1024]{1,0:T(8,128)(2,1)} %get-tuple-element.54.refs_4_.refs_6_), channel_id=1, source_target_pairs={{0,2},{1,3},{2,0},{3,1},{4,6},{5,7},{6,4},{7,5},{8,10},{9,11},{10,... | collective-permute-start | bytes 4325384 | tf_op jit(solution)/shard_map/ppermute | solution.py:250
  56.2 40.3 %collective-permute-start.13 = (bf16[80,2048]{1,0:T(8,128)(2,1)}, bf16[80,2048]{1,0:T(8,128)(2,1)S(1)}, u32[]{:S(2)}, u32[]{:S(2)}) collective-permute-start(bf16[80,2048]{1,0:T(8,128)(2,1)} %get-tuple-element.58), channel_id=1, source_target_pairs={{0,12},{4,0},{8,4},{12,8},{1,13},{5,1},{9,5},{13,9},{2,14},{6,2},{... | collective-permute-start | bytes 983048 | tf_op jit(solution)/shard_map/ppermute | solution.py:243
  60.3 36.2 %collective-permute-start.14 = (bf16[80,2048]{1,0:T(8,128)(2,1)}, bf16[80,2048]{1,0:T(8,128)(2,1)}, u32[]{:S(2)}, u32[]{:S(2)}) collective-permute-start(bf16[80,2048]{1,0:T(8,128)(2,1)} %get-tuple-element.60), channel_id=1, source_target_pairs={{0,8},{4,12},{8,0},{12,4},{1,9},{5,13},{9,1},{13,5},{2,10},{6,14},... | collective-permute-start | bytes 983048 | tf_op jit(solution)/shard_map/ppermute | solution.py:243
  60.3 36.2 %collective-permute-start.15 = (bf16[80,2048]{1,0:T(8,128)(2,1)}, bf16[80,2048]{1,0:T(8,128)(2,1)}, u32[]{:S(2)}, u32[]{:S(2)}) collective-permute-start(bf16[80,2048]{1,0:T(8,128)(2,1)} %get-tuple-element.62), channel_id=1, source_target_pairs={{0,4},{4,8},{8,12},{12,0},{1,5},{5,9},{9,13},{13,1},{2,6},{6,10},{... | collective-permute-start | bytes 983048 | tf_op jit(solution)/shard_map/ppermute | solution.py:243
  76.5 1.3 %collective-permute-start.12 = (f32[16,704]{1,0:T(8,128)S(1)}, f32[16,704]{1,0:T(8,128)S(1)}, u32[]{:S(2)}, u32[]{:S(2)}) collective-permute-start(f32[16,704]{1,0:T(8,128)S(1)} %shard_map.76), channel_id=1, source_target_pairs={{0,1},{1,0},{2,3},{3,2},{4,5},{5,4},{6,7},{7,6},{8,9},{9,8},{10,11... | collective-permute-start | bytes 135176 | tf_op jit(solution)/shard_map/ppermute | solution.py:246
  77.8 0.6 copy-start.5
  84.0 6.8 %collective-permute-start.2 = (bf16[704,1024]{1,0:T(8,128)(2,1)S(1)}, bf16[704,1024]{1,0:T(8,128)(2,1)S(1)}, u32[]{:S(2)}, u32[]{:S(2)}) collective-permute-start(bf16[704,1024]{1,0:T(8,128)(2,1)S(1)} %branch_1_fun.9.refs_4_), channel_id=1, source_target_pairs={{0,1},{1,0},{2,3},{3,2},{4,5},{5,4},{6,7},{7,6},{8,9},{9,8},{10,11... | collective-permute-start | bytes 4325384 | tf_op jit(solution)/shard_map/cond/branch_1_fun/ppermute | solution.py:246
  90.8 5.6 %collective-permute-start.3 = (f32[16,704]{1,0:T(8,128)S(1)}, f32[16,704]{1,0:T(8,128)}, u32[]{:S(2)}, u32[]{:S(2)}) collective-permute-start(f32[16,704]{1,0:T(8,128)S(1)} %get-tuple-element.33.refs_3_), channel_id=1, source_target_pairs={{0,2},{1,3},{2,0},{3,1},{4,6},{5,7},{6,4},{7,5},{8,10},{9,11},{10,... | collective-permute-start | bytes 135176 | tf_op jit(solution)/shard_map/cond/branch_1_fun/ppermute | solution.py:250

commit v7 on v6

--- a/solution.py
+++ b/solution.py
@@ -176,7 +176,7 @@
     n_low = len(lows)
 
     def kernel(counts_ref, id_ref, row_ref, *refs):
-        low_refs, up_refs = refs[:n_low], refs[n_low : n_low + ways][::-1]
+        low_refs, up_refs = refs[:n_low], refs[n_low : n_low + ways]
         sent_refs = refs[n_low + ways : -2]
         out_ref, low_ref = refs[-2:]
         step = pl.program_id(0)
@@ -223,7 +223,7 @@
         scratch_shapes=[pltpu.VMEM((rows, wide), jnp.bfloat16)],
         compiler_params=PARAMS,
         cost_estimate=CHEAP,
-    )(counts, ids, store_row, *lows, *ups[::-1], *[array for send in sends for array in send])
+    )(counts, ids, store_row, *lows, *ups, *[array for send in sends for array in send])
 
 
 def apart(live, function, *operands):
@@ -297,7 +297,7 @@
     low = low_parts(acts, far_downs, counts, ids, store_row, cap, per_owner, after=(last, *heads))
     far_ups = [ups[0]]
     for s in range(1, ways):
-        held, *_ = lax.optimization_barrier((ups[s], last, far_downs[s]))
+        held, *_ = lax.optimization_barrier((ups[s], last, *far_downs[1:]))
         far_ups.append(along_dp(held, s))
     chip_low = low + to_core(low)
     if tail:

time: 103 us -> 94.2 us (0.915)
  starting transfers between devices: 27.8 us -> 21.4 us
  waiting for transfers between devices: 10.6 us -> 8.82 us
    ppermute x9, starting transfers between devices: 22.9 us -> 15.9 us  [along_dp(): lax.ppermute(array, 'dp', [(i, (i + shift) % ways) for i in range(ways)])]
    ppermute x9, waiting for transfers between devices: 6.52 us -> 4.34 us  [along_dp(): lax.ppermute(array, 'dp', [(i, (i + shift) % ways) for i in range(ways)])]
  transfers between devices with their start and end apart: 17 -> 17, of which waited for: 6 -> 6; matrix products, arithmetic and copies ran while one was open for 0% -> 0% of each run, Pallas kernels for 44% -> 48%
where the time goes in v7:
time: 94.2 us; the launch traced here: 93.9 us
  Pallas kernels  62.7 us (67%)
  starting transfers between devices  21.4 us (23%)
  waiting for transfers between devices  8.82 us (9%)
    pallas_call x8, Pallas kernels, product(): pl.pallas_call(kernel, grid_spec=pltpu.PrefetchScalarGridSpec(num_scalar_...  47.6 us
    ppermute x9, starting transfers between devices, along_dp(): lax.ppermute(array, 'dp', [(i, (i + shift) % ways) for i in range(ways)])  15.9 us
    pallas_call x2, Pallas kernels, pick(): pl.pallas_call(kernel, in_specs=[SMEM] * (ways + 1) + [HBM] * n_stores +...  6.39 us
    pallas_call x1, Pallas kernels, finish(): pl.pallas_call(kernel, grid=(block // tile,), in_specs=specs, out_specs=h...  5.66 us
    ppermute x9, waiting for transfers between devices, along_dp(): lax.ppermute(array, 'dp', [(i, (i + shift) % ways) for i in range(ways)])  4.34 us
    ppermute x5, waiting for transfers between devices, to_core(): lax.ppermute(array, 'tensor', [(i, i ^ 1) for i in range(chips * CORES)])  4.11 us
    ppermute x3, starting transfers between devices, to_chip(): lax.ppermute(array, 'tensor', [(i, (i + CORES * shift) % size) for i in r...  4.05 us
    pallas_call x1, Pallas kernels, low_parts(): pl.pallas_call(kernel, in_specs=[SMEM] * 3 + [WHOLE] * (1 + ways) + [ANY]...  3.1 us
  transfers between devices with their start and end apart: 17, of which 6 were waited for; matrix products, arithmetic and copies ran while one was open for 0% of the time, Pallas kernels for 48%

profile of v7, /device:TPU:0, one launch (start us, length us, event | category | flops | bytes accessed | tf_op | source)
XLA Modules:
  0.0 93.9 jit_solution(11329775726607396005)
XLA Ops:
  0.0 0.1 pad_add_fusion.refs_0_
  0.1 6.7 %shard_map.73 = bf16[704,1024]{1,0:T(8,128)(2,1)S(1)} custom-call(s32[2]{0:T(128)S(1)} %pad_add_fusion.refs_0_, bf16[704,2048]{1,0:T(8,128)(2,1)} %acts_ref.1, bf16[2048,8192]{1,0:T(8,128)(2,1)} %refs_2_.3), custom_call_target="tpu_custom_call" | custom-call | flops 1000 | bytes 1000 | tf_op jit(solution)/shard_map/pallas_call | solution.py:64
  6.8 0.0 copy-start.1
  6.8 0.0 copy-start
  6.8 0.5 collective-permute-start.7
  7.4 2.8 %collective-permute-done.7.refs_3_ = bf16[704,1024]{1,0:T(8,128)(2,1)S(1)} collective-permute-done((bf16[704,1024]{1,0:T(8,128)(2,1)S(1)}, bf16[704,1024]{1,0:T(8,128)(2,1)S(1)}, u32[]{:S(2)}, u32[]{:S(2)}) %collective-permute-start.7) | collective-permute-done | bytes 1441824 | tf_op jit(solution)/shard_map/ppermute | solution.py:246
  10.2 5.6 %shard_map.74.refs_6_ = bf16[704,1024]{1,0:T(8,128)(2,1)S(1)} custom-call(s32[2]{0:T(128)S(1)} %pad_add_fusion.refs_0_, bf16[704,2048]{1,0:T(8,128)(2,1)S(1)} %copy-done.3, bf16[2048,8192]{1,0:T(8,128)(2,1)} %refs_2_.3, bf16[704,1024]{1,0:T(8,128)(2,1)S(1)} %collective-permute-done.7.refs_3_), custom_call_target="tpu_custom_call" | custom-call | flops 1000 | bytes 1000 | tf_op jit(solution)/shard_map/pallas_call | solution.py:64
  15.8 0.0 copy-start.2
  15.8 2.9 %collective-permute-start.11 = (bf16[704,1024]{1,0:T(8,128)(2,1)S(1)}, bf16[704,1024]{1,0:T(8,128)(2,1)S(1)}, u32[]{:S(2)}, u32[]{:S(2)}) collective-permute-start(bf16[704,1024]{1,0:T(8,128)(2,1)S(1)} %shard_map.74.refs_6_), channel_id=1, source_target_pairs={{0,2},{1,3},{2,0},{3,1},{4,6},{5,7},{6,4},{7,5},{8,10},{9,11},{10,... | collective-permute-start | bytes 4325384 | tf_op jit(solution)/shard_map/ppermute | solution.py:250
  18.7 3.6 %collective-permute-start.4 = (s32[1,16]{1,0:T(1,128)S(1)}, s32[1,16]{1,0:T(1,128)S(1)}, u32[]{:S(2)}, u32[]{:S(2)}) collective-permute-start(s32[1,16]{1,0:T(1,128)S(1)} %copy-done.1), channel_id=1, source_target_pairs={{0,12},{4,0},{8,4},{12,8},{1,13},{5,1},{9,5},{13,9},{2,14},{6,2},{... | collective-permute-start | bytes 200 | tf_op jit(solution)/shard_map/ppermute | solution.py:243
  22.3 0.0 collective-permute-start.5
  22.4 1.0 %collective-permute-start.6 = (s32[1,16]{1,0:T(1,128)S(1)}, s32[1,16]{1,0:T(1,128)S(1)}, u32[]{:S(2)}, u32[]{:S(2)}) collective-permute-start(s32[1,16]{1,0:T(1,128)S(1)} %copy-done.1), channel_id=1, source_target_pairs={{0,4},{4,8},{8,12},{12,0},{1,5},{5,9},{9,13},{13,1},{2,6},{6,10},{... | collective-permute-start | bytes 200 | tf_op jit(solution)/shard_map/ppermute | solution.py:243
  23.4 0.3 collective-permute-done.4.refs_1_
  23.6 3.1 %collective-permute-done.5.refs_2_ = s32[1,16]{1,0:T(1,128)S(1)} collective-permute-done((s32[1,16]{1,0:T(1,128)S(1)}, s32[1,16]{1,0:T(1,128)S(1)}, u32[]{:S(2)}, u32[]{:S(2)}) %collective-permute-start.5) | collective-permute-done | bytes 96 | tf_op jit(solution)/shard_map/ppermute | solution.py:243
  26.8 0.9 collective-permute-done.6.refs_3_
  27.7 3.2 %shard_map.75 = (bf16[80,2048]{1,0:T(8,128)(2,1)S(1)}, bf16[80,2048]{1,0:T(8,128)(2,1)}, bf16[80,2048]{1,0:T(8,128)(2,1)}, bf16[80,2048]{1,0:T(8,128)(2,1)}) custom-call(s32[1,16]{1,0:T(1,128)S(1)} %copy-done.1, s32[1,16]{1,0:T(1,128)S(1)} %collective-permute-done.4.refs_1_, s32[1,16]{1,0:T(1,128)S(1)} %collective-permute-done.5.refs_2_, ...), custom_call_target="tpu_custom_call" | custom-call | flops 1000 | bytes 1000 | tf_op jit(solution)/shard_map/pallas_call | solution.py:108
  30.9 0.1 collective-permute-start.8
  31.0 1.2 %collective-permute-start.9 = (bf16[80,2048]{1,0:T(8,128)(2,1)}, bf16[80,2048]{1,0:T(8,128)(2,1)}, u32[]{:S(2)}, u32[]{:S(2)}) collective-permute-start(bf16[80,2048]{1,0:T(8,128)(2,1)} %get-tuple-element.52), channel_id=1, source_target_pairs={{0,8},{4,12},{8,0},{12,4},{1,9},{5,13},{9,1},{13,5},{2,10},{6,14},... | collective-permute-start | bytes 983048 | tf_op jit(solution)/shard_map/ppermute | solution.py:243
  32.2 2.8 %collective-permute-start.10 = (bf16[80,2048]{1,0:T(8,128)(2,1)}, bf16[80,2048]{1,0:T(8,128)(2,1)}, u32[]{:S(2)}, u32[]{:S(2)}) collective-permute-start(bf16[80,2048]{1,0:T(8,128)(2,1)} %get-tuple-element.53), channel_id=1, source_target_pairs={{0,12},{4,0},{8,4},{12,8},{1,13},{5,1},{9,5},{13,9},{2,14},{6,2},{... | collective-permute-start | bytes 983048 | tf_op jit(solution)/shard_map/ppermute | solution.py:243
  35.1 18.2 %conditional.2 = (bf16[704,1024]{1,0:T(8,128)(2,1)}, bf16[704,1024]{1,0:T(8,128)(2,1)}) conditional(s32[]{:T(128)} %bitcast.2, () %tuple.26, (s32[2]{0:T(128)S(1)}, bf16[704,2048]{1,0:T(8,128)(2,1)S(1)}, bf16[2048,8192]{1,0:T(8,128)(2,1)}, bf16[80,2048]{1,0:T(8,128)(2,1)S(1)}) %tuple.37), branch_computations={%region_0.1_spmd, %region_1.2_spmd} | conditional | flops 3000 | bytes 11537432 | solution.py:231
  35.1 5.6 %branch_1_fun.6.refs_3_ = bf16[704,1024]{1,0:T(8,128)(2,1)S(1)} custom-call(s32[2]{0:T(128)S(1)} %get-tuple-element.23.refs_0_, bf16[704,2048]{1,0:T(8,128)(2,1)S(1)} %get-tuple-element.24.refs_1_, bf16[2048,8192]{1,0:T(8,128)(2,1)} %get-tuple-element.25.refs_2_, bf16[80,2048]{1,0:T(8,128)(2,1)S(1)} %get-tuple-element.26.refs_3_), custom_call_target="tpu_custom_call" | custom-call | flops 1000 | bytes 1000 | tf_op jit(solution)/shard_map/cond/branch_1_fun/pallas_call | solution.py:64
  40.7 0.1 collective-permute-start
  40.8 5.6 %branch_1_fun.7.refs_4_ = bf16[704,1024]{1,0:T(8,128)(2,1)S(1)} custom-call(s32[2]{0:T(128)S(1)} %get-tuple-element.23.refs_0_, bf16[704,2048]{1,0:T(8,128)(2,1)S(1)} %get-tuple-element.24.refs_1_, bf16[2048,8192]{1,0:T(8,128)(2,1)} %get-tuple-element.25.refs_2_, bf16[704,1024]{1,0:T(8,128)(2,1)S(1)} %branch_1_fun.6.refs_3_), custom_call_target="tpu_custom_call" | custom-call | flops 1000 | bytes 1000 | tf_op jit(solution)/shard_map/cond/branch_1_fun/pallas_call | solution.py:64
  46.3 0.0 collective-permute-done.refs_3_
  46.4 0.6 collective-permute-start.1
  46.9 6.3 %branch_1_fun.8 = bf16[704,1024]{1,0:T(8,128)(2,1)} custom-call(s32[2]{0:T(128)S(1)} %get-tuple-element.23.refs_0_, bf16[704,2048]{1,0:T(8,128)(2,1)S(1)} %get-tuple-element.24.refs_1_, bf16[2048,8192]{1,0:T(8,128)(2,1)} %get-tuple-element.25.refs_2_, bf16[704,1024]{1,0:T(8,128)(2,1)S(1)} %collective-permute-done.refs_3_, ...), custom_call_target="tpu_custom_call" | custom-call | flops 1000 | bytes 1000 | tf_op jit(solution)/shard_map/cond/branch_1_fun/pallas_call | solution.py:64
  53.3 0.6 collective-permute-start.16
  53.9 3.2 %shard_map.77 = (bf16[80,2048]{1,0:T(8,128)(2,1)S(1)}, bf16[80,2048]{1,0:T(8,128)(2,1)}, bf16[80,2048]{1,0:T(8,128)(2,1)}, bf16[80,2048]{1,0:T(8,128)(2,1)}) custom-call(s32[1,16]{1,0:T(1,128)S(1)} %copy-done.1, s32[1,16]{1,0:T(1,128)S(1)} %collective-permute-done.4.refs_1_, s32[1,16]{1,0:T(1,128)S(1)} %collective-permute-done.5.refs_2_, ...), custom_call_target="tpu_custom_call" | custom-call | flops 1000 | bytes 1000 | tf_op jit(solution)/shard_map/pallas_call | solution.py:108
  57.1 0.0 collective-permute-done.8.refs_1_
  57.1 0.0 collective-permute-done.10.refs_3_
  57.1 4.8 %collective-permute-start.13 = (bf16[80,2048]{1,0:T(8,128)(2,1)}, bf16[80,2048]{1,0:T(8,128)(2,1)S(1)}, u32[]{:S(2)}, u32[]{:S(2)}) collective-permute-start(bf16[80,2048]{1,0:T(8,128)(2,1)} %get-tuple-element.59), channel_id=1, source_target_pairs={{0,4},{4,8},{8,12},{12,0},{1,5},{5,9},{9,13},{13,1},{2,6},{6,10},{... | collective-permute-start | bytes 983048 | tf_op jit(solution)/shard_map/ppermute | solution.py:243
  62.0 1.1 %collective-permute-start.14 = (bf16[80,2048]{1,0:T(8,128)(2,1)}, bf16[80,2048]{1,0:T(8,128)(2,1)}, u32[]{:S(2)}, u32[]{:S(2)}) collective-permute-start(bf16[80,2048]{1,0:T(8,128)(2,1)} %get-tuple-element.61), channel_id=1, source_target_pairs={{0,8},{4,12},{8,0},{12,4},{1,9},{5,13},{9,1},{13,5},{2,10},{6,14},... | collective-permute-start | bytes 983048 | tf_op jit(solution)/shard_map/ppermute | solution.py:243
  63.0 1.3 %collective-permute-start.15 = (bf16[80,2048]{1,0:T(8,128)(2,1)}, bf16[80,2048]{1,0:T(8,128)(2,1)}, u32[]{:S(2)}, u32[]{:S(2)}) collective-permute-start(bf16[80,2048]{1,0:T(8,128)(2,1)} %get-tuple-element.63), channel_id=1, source_target_pairs={{0,12},{4,0},{8,4},{12,8},{1,13},{5,1},{9,5},{13,9},{2,14},{6,2},{... | collective-permute-start | bytes 983048 | tf_op jit(solution)/shard_map/ppermute | solution.py:243
  64.3 3.1 %shard_map.76 = f32[16,704]{1,0:T(8,128)S(1)} custom-call(s32[1,16]{1,0:T(1,128)S(1)} %copy-done.2, s32[1,16]{1,0:T(1,128)S(1)} %copy-done.1, s32[384]{0:T(512)S(1)} %copy-done, bf16[704,2048]{1,0:T(8,128)(2,1)S(1)} %copy-done.4, bf16[80,2048]{1,0:T(8,128)(2,1)S(1)} %copy-done.7, bf16[80,2048]{1,0:T(8,128)(2,1)} %collective-permute-done.8.refs_1_, ...), custom_call_target="tpu_custom_call" | custom-call | flops 22000001024 | bytes 1000 | tf_op jit(solution)/shard_map/pallas_call | solution.py:161
  67.4 1.3 %collective-permute-done.12 = f32[16,704]{1,0:T(8,128)S(1)} collective-permute-done((f32[16,704]{1,0:T(8,128)S(1)}, f32[16,704]{1,0:T(8,128)S(1)}, u32[]{:S(2)}, u32[]{:S(2)}) %collective-permute-start.12) | collective-permute-done | bytes 45088 | tf_op jit(solution)/shard_map/ppermute | solution.py:246
  68.7 0.6 copy-done.5
  69.3 18.9 %conditional.3 = (bf16[704,1024]{1,0:T(8,128)(2,1)}, bf16[704,1024]{1,0:T(8,128)(2,1)S(1)}, f32[16,704]{1,0:T(8,128)}) conditional(s32[]{:T(128)} %bitcast.2, () %tuple.28, (s32[2]{0:T(128)S(1)}, bf16[704,2048]{1,0:T(8,128)(2,1)S(1)}, bf16[2048,8192]{1,0:T(8,128)(2,1)}, f32[16,704]{1,0:T(8,128)S(1)}, bf16[704,1024]{1,0:T(8,128)(2,1)}) %tuple.38), branch_computations={%region_2.3_spmd, %region_3.4_spmd} | conditional | flops 3000 | bytes 5950496 | solution.py:231
  69.3 5.6 %branch_1_fun.9.refs_4_ = bf16[704,1024]{1,0:T(8,128)(2,1)S(1)} custom-call(s32[2]{0:T(128)S(1)} %get-tuple-element.28.refs_0_, bf16[704,2048]{1,0:T(8,128)(2,1)S(1)} %get-tuple-element.29.refs_1_, bf16[2048,8192]{1,0:T(8,128)(2,1)} %get-tuple-element.30.refs_2_, f32[16,704]{1,0:T(8,128)S(1)} %get-tuple-element.33.refs_3_), custom_call_target="tpu_custom_call" | custom-call | flops 1000 | bytes 1000 | tf_op jit(solution)/shard_map/cond/branch_1_fun/pallas_call | solution.py:64
  74.9 0.2 collective-permute-start.2
  75.1 6.6 %branch_1_fun.10.refs_4_ = bf16[704,1024]{1,0:T(8,128)(2,1)} custom-call(s32[2]{0:T(128)S(1)} %get-tuple-element.28.refs_0_, bf16[704,2048]{1,0:T(8,128)(2,1)S(1)} %get-tuple-element.29.refs_1_, bf16[2048,8192]{1,0:T(8,128)(2,1)} %get-tuple-element.30.refs_2_, bf16[704,1024]{1,0:T(8,128)(2,1)} %get-tuple-element.31.refs_3_, ...), custom_call_target="tpu_custom_call" | custom-call | flops 1000 | bytes 1000 | tf_op jit(solution)/shard_map/cond/branch_1_fun/pallas_call | solution.py:64
  81.7 0.0 collective-permute-done.2.refs_3_
  81.7 0.5 collective-permute-start.3
  82.3 5.6 %branch_1_fun.11 = bf16[704,1024]{1,0:T(8,128)(2,1)S(1)} custom-call(s32[2]{0:T(128)S(1)} %get-tuple-element.28.refs_0_, bf16[704,2048]{1,0:T(8,128)(2,1)S(1)} %get-tuple-element.29.refs_1_, bf16[2048,8192]{1,0:T(8,128)(2,1)} %get-tuple-element.30.refs_2_, bf16[704,1024]{1,0:T(8,128)(2,1)S(1)} %collective-permute-done.2.refs_3_, ...), custom_call_target="tpu_custom_call" | custom-call | flops 1000 | bytes 1000 | tf_op jit(solution)/shard_map/cond/branch_1_fun/pallas_call | solution.py:64
  87.9 0.4 collective-permute-done.3
  88.2 0.0 collective-permute-done.13.refs_3_
  88.2 0.0 collective-permute-done.14.refs_4_
  88.2 0.0 collective-permute-done.15.refs_5_
  88.2 5.7 %shard_map.78 = bf16[704,2048]{1,0:T(8,128)(2,1)} custom-call(s32[1,16]{1,0:T(1,128)S(1)} %copy-done.2, s32[1,16]{1,0:T(1,128)S(1)} %copy-done.1, s32[384]{0:T(512)S(1)} %copy-done, f32[16,704]{1,0:T(8,128)} %copy-done.5, f32[16,704]{1,0:T(8,128)} %get-tuple-element.56.refs_1_, bf16[80,2048]{1,0:T(8,128)(2,1)S(1)} %get-tuple-element.57.refs_2_, ...), custom_call_target="tpu_custom_call" | custom-call | flops 1000 | bytes 1000 | tf_op jit(solution)/shard_map/pallas_call | solution.py:217
  (18 shorter events, 0.0 us)
Async XLA Ops:
  0.1 10.1 %copy-start.3 = (bf16[704,2048]{1,0:T(8,128)(2,1)S(1)}, bf16[704,2048]{1,0:T(8,128)(2,1)}, u32[]{:S(2)}) copy-start(bf16[704,2048]{1,0:T(8,128)(2,1)} %acts_ref.1) | copy-start | bytes 8650756
  6.8 11.9 %copy-start.1 = (s32[1,16]{1,0:T(1,128)S(1)}, s32[1,16]{1,0:T(1,128)}, u32[]{:S(2)}) copy-start(s32[1,16]{1,0:T(1,128)} %id_ref.3) | copy-start | bytes 196
  6.8 20.9 %copy-start = (s32[384]{0:T(512)S(1)}, s32[384]{0:T(512)}, u32[]{:S(2)}) copy-start(s32[384]{0:T(512)} %row_ref.3) | copy-start | bytes 4612
  6.8 3.4 %collective-permute-start.7 = (bf16[704,1024]{1,0:T(8,128)(2,1)S(1)}, bf16[704,1024]{1,0:T(8,128)(2,1)S(1)}, u32[]{:S(2)}, u32[]{:S(2)}) collective-permute-start(bf16[704,1024]{1,0:T(8,128)(2,1)S(1)} %shard_map.73), channel_id=1, source_target_pairs={{0,1},{1,0},{2,3},{3,2},{4,5},{5,4},{6,7},{7,6},{8,9},{9,8},{10,11... | collective-permute-start | bytes 4325384 | tf_op jit(solution)/shard_map/ppermute | solution.py:246
  15.8 19.2 %copy-start.2 = (s32[1,16]{1,0:T(1,128)S(1)}, s32[1,16]{1,0:T(1,128)}, u32[]{:S(2)}) copy-start(s32[1,16]{1,0:T(1,128)} %counts_ref.3) | copy-start | bytes 196
  15.8 48.5 %collective-permute-start.11 = (bf16[704,1024]{1,0:T(8,128)(2,1)S(1)}, bf16[704,1024]{1,0:T(8,128)(2,1)S(1)}, u32[]{:S(2)}, u32[]{:S(2)}) collective-permute-start(bf16[704,1024]{1,0:T(8,128)(2,1)S(1)} %shard_map.74.refs_6_), channel_id=1, source_target_pairs={{0,2},{1,3},{2,0},{3,1},{4,6},{5,7},{6,4},{7,5},{8,10},{9,11},{10,... | collective-permute-start | bytes 4325384 | tf_op jit(solution)/shard_map/ppermute | solution.py:250
  18.7 4.9 %collective-permute-start.4 = (s32[1,16]{1,0:T(1,128)S(1)}, s32[1,16]{1,0:T(1,128)S(1)}, u32[]{:S(2)}, u32[]{:S(2)}) collective-permute-start(s32[1,16]{1,0:T(1,128)S(1)} %copy-done.1), channel_id=1, source_target_pairs={{0,12},{4,0},{8,4},{12,8},{1,13},{5,1},{9,5},{13,9},{2,14},{6,2},{... | collective-permute-start | bytes 200 | tf_op jit(solution)/shard_map/ppermute | solution.py:243
  22.3 4.4 %collective-permute-start.5 = (s32[1,16]{1,0:T(1,128)S(1)}, s32[1,16]{1,0:T(1,128)S(1)}, u32[]{:S(2)}, u32[]{:S(2)}) collective-permute-start(s32[1,16]{1,0:T(1,128)S(1)} %copy-done.1), channel_id=1, source_target_pairs={{0,8},{4,12},{8,0},{12,4},{1,9},{5,13},{9,1},{13,5},{2,10},{6,14},... | collective-permute-start | bytes 200 | tf_op jit(solution)/shard_map/ppermute | solution.py:243
  22.4 5.3 %collective-permute-start.6 = (s32[1,16]{1,0:T(1,128)S(1)}, s32[1,16]{1,0:T(1,128)S(1)}, u32[]{:S(2)}, u32[]{:S(2)}) collective-permute-start(s32[1,16]{1,0:T(1,128)S(1)} %copy-done.1), channel_id=1, source_target_pairs={{0,4},{4,8},{8,12},{12,0},{1,5},{5,9},{9,13},{13,1},{2,6},{6,10},{... | collective-permute-start | bytes 200 | tf_op jit(solution)/shard_map/ppermute | solution.py:243
  30.9 4.2 %copy-start.6 = (bf16[80,2048]{1,0:T(8,128)(2,1)}, bf16[80,2048]{1,0:T(8,128)(2,1)S(1)}, u32[]{:S(2)}) copy-start(bf16[80,2048]{1,0:T(8,128)(2,1)S(1)} %get-tuple-element.50.refs_0_) | copy-start | bytes 983044
  30.9 26.2 %collective-permute-start.8 = (bf16[80,2048]{1,0:T(8,128)(2,1)}, bf16[80,2048]{1,0:T(8,128)(2,1)}, u32[]{:S(2)}, u32[]{:S(2)}) collective-permute-start(bf16[80,2048]{1,0:T(8,128)(2,1)} %get-tuple-element.51), channel_id=1, source_target_pairs={{0,4},{4,8},{8,12},{12,0},{1,5},{5,9},{9,13},{13,1},{2,6},{6,10},{... | collective-permute-start | bytes 983048 | tf_op jit(solution)/shard_map/ppermute | solution.py:243
  31.0 26.1 %collective-permute-start.9 = (bf16[80,2048]{1,0:T(8,128)(2,1)}, bf16[80,2048]{1,0:T(8,128)(2,1)}, u32[]{:S(2)}, u32[]{:S(2)}) collective-permute-start(bf16[80,2048]{1,0:T(8,128)(2,1)} %get-tuple-element.52), channel_id=1, source_target_pairs={{0,8},{4,12},{8,0},{12,4},{1,9},{5,13},{9,1},{13,5},{2,10},{6,14},... | collective-permute-start | bytes 983048 | tf_op jit(solution)/shard_map/ppermute | solution.py:243
  32.2 24.9 %collective-permute-start.10 = (bf16[80,2048]{1,0:T(8,128)(2,1)}, bf16[80,2048]{1,0:T(8,128)(2,1)}, u32[]{:S(2)}, u32[]{:S(2)}) collective-permute-start(bf16[80,2048]{1,0:T(8,128)(2,1)} %get-tuple-element.53), channel_id=1, source_target_pairs={{0,12},{4,0},{8,4},{12,8},{1,13},{5,1},{9,5},{13,9},{2,14},{6,2},{... | collective-permute-start | bytes 983048 | tf_op jit(solution)/shard_map/ppermute | solution.py:243
  40.7 5.7 %collective-permute-start = (bf16[704,1024]{1,0:T(8,128)(2,1)S(1)}, bf16[704,1024]{1,0:T(8,128)(2,1)S(1)}, u32[]{:S(2)}, u32[]{:S(2)}) collective-permute-start(bf16[704,1024]{1,0:T(8,128)(2,1)S(1)} %branch_1_fun.6.refs_3_), channel_id=1, source_target_pairs={{0,1},{1,0},{2,3},{3,2},{4,5},{5,4},{6,7},{7,6},{8,9},{9,8},{10,11... | collective-permute-start | bytes 4325384 | tf_op jit(solution)/shard_map/cond/branch_1_fun/ppermute | solution.py:246
  46.4 6.9 %collective-permute-start.1 = (bf16[704,1024]{1,0:T(8,128)(2,1)S(1)}, bf16[704,1024]{1,0:T(8,128)(2,1)}, u32[]{:S(2)}, u32[]{:S(2)}) collective-permute-start(bf16[704,1024]{1,0:T(8,128)(2,1)S(1)} %branch_1_fun.7.refs_4_), channel_id=1, source_target_pairs={{0,1},{1,0},{2,3},{3,2},{4,5},{5,4},{6,7},{7,6},{8,9},{9,8},{10,11... | collective-permute-start | bytes 4325384 | tf_op jit(solution)/shard_map/cond/branch_1_fun/ppermute | solution.py:246
  53.3 11.1 %copy-start.4 = (bf16[704,2048]{1,0:T(8,128)(2,1)S(1)}, bf16[704,2048]{1,0:T(8,128)(2,1)}, u32[]{:S(2)}) copy-start(bf16[704,2048]{1,0:T(8,128)(2,1)} %acts_ref.1) | copy-start | bytes 8650756
  53.3 11.1 %copy-start.7 = (bf16[80,2048]{1,0:T(8,128)(2,1)S(1)}, bf16[80,2048]{1,0:T(8,128)(2,1)}, u32[]{:S(2)}) copy-start(bf16[80,2048]{1,0:T(8,128)(2,1)} %copy-done.6) | copy-start | bytes 983044
  53.3 35.0 %collective-permute-start.16 = (bf16[704,1024]{1,0:T(8,128)(2,1)}, bf16[704,1024]{1,0:T(8,128)(2,1)}, u32[]{:S(2)}, u32[]{:S(2)}) collective-permute-start(bf16[704,1024]{1,0:T(8,128)(2,1)} %get-tuple-element.54.refs_4_.refs_6_), channel_id=1, source_target_pairs={{0,2},{1,3},{2,0},{3,1},{4,6},{5,7},{6,4},{7,5},{8,10},{9,11},{10,... | collective-permute-start | bytes 4325384 | tf_op jit(solution)/shard_map/ppermute | solution.py:250
  57.1 31.1 %collective-permute-start.13 = (bf16[80,2048]{1,0:T(8,128)(2,1)}, bf16[80,2048]{1,0:T(8,128)(2,1)S(1)}, u32[]{:S(2)}, u32[]{:S(2)}) collective-permute-start(bf16[80,2048]{1,0:T(8,128)(2,1)} %get-tuple-element.59), channel_id=1, source_target_pairs={{0,4},{4,8},{8,12},{12,0},{1,5},{5,9},{9,13},{13,1},{2,6},{6,10},{... | collective-permute-start | bytes 983048 | tf_op jit(solution)/shard_map/ppermute | solution.py:243
  62.0 26.3 %collective-permute-start.14 = (bf16[80,2048]{1,0:T(8,128)(2,1)}, bf16[80,2048]{1,0:T(8,128)(2,1)}, u32[]{:S(2)}, u32[]{:S(2)}) collective-permute-start(bf16[80,2048]{1,0:T(8,128)(2,1)} %get-tuple-element.61), channel_id=1, source_target_pairs={{0,8},{4,12},{8,0},{12,4},{1,9},{5,13},{9,1},{13,5},{2,10},{6,14},... | collective-permute-start | bytes 983048 | tf_op jit(solution)/shard_map/ppermute | solution.py:243
  63.0 25.2 %collective-permute-start.15 = (bf16[80,2048]{1,0:T(8,128)(2,1)}, bf16[80,2048]{1,0:T(8,128)(2,1)}, u32[]{:S(2)}, u32[]{:S(2)}) collective-permute-start(bf16[80,2048]{1,0:T(8,128)(2,1)} %get-tuple-element.63), channel_id=1, source_target_pairs={{0,12},{4,0},{8,4},{12,8},{1,13},{5,1},{9,5},{13,9},{2,14},{6,2},{... | collective-permute-start | bytes 983048 | tf_op jit(solution)/shard_map/ppermute | solution.py:243
  67.4 1.3 %collective-permute-start.12 = (f32[16,704]{1,0:T(8,128)S(1)}, f32[16,704]{1,0:T(8,128)S(1)}, u32[]{:S(2)}, u32[]{:S(2)}) collective-permute-start(f32[16,704]{1,0:T(8,128)S(1)} %shard_map.76), channel_id=1, source_target_pairs={{0,1},{1,0},{2,3},{3,2},{4,5},{5,4},{6,7},{7,6},{8,9},{9,8},{10,11... | collective-permute-start | bytes 135176 | tf_op jit(solution)/shard_map/ppermute | solution.py:246
  68.7 0.6 copy-start.5
  74.9 6.8 %collective-permute-start.2 = (bf16[704,1024]{1,0:T(8,128)(2,1)S(1)}, bf16[704,1024]{1,0:T(8,128)(2,1)S(1)}, u32[]{:S(2)}, u32[]{:S(2)}) collective-permute-start(bf16[704,1024]{1,0:T(8,128)(2,1)S(1)} %branch_1_fun.9.refs_4_), channel_id=1, source_target_pairs={{0,1},{1,0},{2,3},{3,2},{4,5},{5,4},{6,7},{7,6},{8,9},{9,8},{10,11... | collective-permute-start | bytes 4325384 | tf_op jit(solution)/shard_map/cond/branch_1_fun/ppermute | solution.py:246
  81.7 6.5 %collective-permute-start.3 = (f32[16,704]{1,0:T(8,128)S(1)}, f32[16,704]{1,0:T(8,128)}, u32[]{:S(2)}, u32[]{:S(2)}) collective-permute-start(f32[16,704]{1,0:T(8,128)S(1)} %get-tuple-element.33.refs_3_), channel_id=1, source_target_pairs={{0,2},{1,3},{2,0},{3,1},{4,6},{5,7},{6,4},{7,5},{8,10},{9,11},{10,... | collective-permute-start | bytes 135176 | tf_op jit(solution)/shard_map/cond/branch_1_fun/ppermute | solution.py:250
